TPU v7x, 512 devices: a whole 4x4x16 slice. The times are simulated.
512 devices in a mesh: mode: 32 (over y, z_hi, x), rows: 16 (over z_lo, core).
Axes of the slice: x: 4, y: 4, z: 16 (z_hi: 2, z_lo: 8; z = z_hi * 8 + z_lo), core: 2. Of those that a mesh axis runs over, the one named last changes fastest.
Arguments:
- tangents: float32 [128, 3, 128, 1024], P('mode', None, 'rows'), may hold values from -6 to 6
- checkpoints: float32 [8, 3, 128, 1024], P(None, None, 'rows', 'mode'), may hold values from 0 to 0.5
- owner_order: int32 [8], replicated, may hold values from 0 to 7, each once
- land_mask: int32 [128, 1024], P('rows'), may hold values 0 or 1
- coefficients: float32 [128, 128], replicated, may hold values from -0.9 to 0.9
Outputs:
- vectors: float32 [128, 3, 128, 1024], P(None, None, 'rows', 'mode')
Inputs may be any that keep to these rules, and one draw needn't show every extreme that they name: `owner_order`: every checkpoint slot is named by exactly one step.
All inputs are finite; a program needn't handle non-finite values. No bound on the sum of `land_mask` on one device may be relied on, other than what follows from the above.
Results may differ from a plain program's by a relative error of at most 0.0002.
Values sent between devices are 32-bit elements; how exact they have to be, the bound alone decides.
No kernel may reach another device: no remote copies, remote signals or barrier semaphores. Data moves between devices by JAX's collectives and lax.ppermute only.
A program may use at most 64 MiB of HBM per device.

v0:
```python
import jax
import jax.numpy as jnp
from jax import lax
from jax.sharding import PartitionSpec as P

mean_depth = 1.0
gravity = 1.0
coriolis = 0.5
time_step = 0.5


def padded(cells, sides, width):
    for axis, dim in sides:
        count = lax.axis_size(axis)
        ends = count - 1
        head = lax.slice_in_dim(cells, 0, width, axis=dim)
        tail = lax.slice_in_dim(cells, cells.shape[dim] - width, cells.shape[dim], axis=dim)
        cells = jnp.concatenate(
            [
                lax.ppermute(tail, axis, [(i, (i + 1) % count) for i in range(ends)]),
                cells,
                lax.ppermute(head, axis, [((i + 1) % count, i) for i in range(ends)]),
            ],
            axis=dim,
        )
    return cells


def deriv_x(values):
    return 0.5 * (jnp.roll(values, -1, -1) - jnp.roll(values, 1, -1))


def deriv_y(values):
    return 0.5 * (values[..., 2:, :] - values[..., :-2, :])


def interior(values):
    return values[..., 1:-1, :]


def tendency(base_flow, current):
    depth_total = mean_depth + base_flow[0]
    flow_u = base_flow[1]
    flow_v = base_flow[2]
    height = current[:, 0]
    zonal = current[:, 1]
    meridional = current[:, 2]
    flux_x = depth_total * zonal + height * flow_u
    flux_y = depth_total * meridional + height * flow_v
    height_rate = -(interior(deriv_x(flux_x)) + deriv_y(flux_y))
    zonal_mid = interior(zonal)
    merid_mid = interior(meridional)
    flow_umid = interior(flow_u)
    flow_vmid = interior(flow_v)
    zonal_rate = (
        -(
            flow_umid * interior(deriv_x(zonal))
            + zonal_mid * interior(deriv_x(flow_u))
            + flow_vmid * deriv_y(zonal)
            + merid_mid * deriv_y(flow_u)
        )
        + coriolis * merid_mid
        - gravity * interior(deriv_x(height))
    )
    merid_rate = (
        -(
            flow_umid * interior(deriv_x(meridional))
            + zonal_mid * interior(deriv_x(flow_v))
            + flow_vmid * deriv_y(meridional)
            + merid_mid * deriv_y(flow_v)
        )
        - coriolis * zonal_mid
        - gravity * deriv_y(height)
    )
    return jnp.stack([height_rate, zonal_rate, merid_rate], 1)


def on_device(tangents, checkpoints, owner_order, land_mask, coefficients):
    wet_mask = land_mask.astype(jnp.float32)
    current = wet_mask * tangents
    depth = 1
    flows_wide, wet_stack = (
        padded(checkpoints, (("rows", 2),), depth),
        padded(wet_mask[None, None], (("rows", 2),), depth),
    )

    def fetch_flow(step_index):
        held_tile = lax.dynamic_index_in_dim(flows_wide, owner_order[step_index], 0, keepdims=False)
        return lax.all_gather(held_tile, "mode", axis=2, tiled=True)

    total_steps = owner_order.shape[0]

    def advance(step_index, current):
        base_wide = fetch_flow(step_index)
        widened = padded(current, (("rows", 2),), 1)
        slope_one = tendency(base_wide, widened)
        middle = wet_mask * (current + time_step * slope_one)
        middle_wide = padded(middle, (("rows", 2),), 1)
        slope_two = tendency(base_wide, middle_wide)
        return wet_mask * (current + 0.5 * time_step * (slope_one + slope_two))

    final = lax.fori_loop(0, total_steps, advance, current)
    mixing = jnp.eye(coefficients.shape[0], dtype=jnp.float32) + jnp.triu(coefficients)
    cell_block = lax.all_to_all(final, "mode", split_axis=3, concat_axis=0, tiled=True)
    flattened = cell_block.reshape(cell_block.shape[0], -1)
    mixed = jnp.dot(
        mixing.T, flattened, precision=lax.Precision.HIGHEST, preferred_element_type=jnp.float32
    )
    return mixed.reshape(cell_block.shape)


def solution(mesh):
    placed = (
        P("mode", None, "rows", None),
        P(None, None, "rows", "mode"),
        P(),
        P("rows", None),
        P(),
    )
    return jax.shard_map(
        on_device,
        mesh=mesh,
        in_specs=placed,
        out_specs=P(None, None, "rows", "mode"),
        check_vma=False,
    )
```

profile of v0, /device:TPU:1, one launch (start us, length us, event | category | flops | bytes accessed | tf_op | source)
XLA Modules:
  0.0 1685.6 jit_solution(5932026285515117026)
XLA Ops:
  0.9 4.9 collective-permute-start.4
  5.9 5.1 collective-permute-start.5
  14.1 1616.7 %while.13 = (s32[]{:T(128)}, f32[4,3,8,1024]{3,2,1,0:T(8,128)S(1)}, f32[8,1024]{1,0:T(8,128)}, s32[8]{0:T(128)}, f32[8,3,10,32]{3,0,2,1:T(8,128)}, /*index=5*/s32[]{:T(128)}, s32[]{:T(128)}, s32[]{:T(128)}) while((s32[]{:T(128)}, f32[4,3,8,1024]{3,2,1,0:T(8,128)S(1)}, f32[8,1024]{1,0:T(8,128)}, s32[8]{0:T(128)}, f32[8,3,10,32]{3,0,2,1:T(8,128)}, ...), condition=%wide.region_1.2_spmd, body=%wide.region_0.1_spmd.sunk | while | flops 5195781 | bytes 25504440 | solution.py:102
  16.7 3.6 collective-permute-start.1
  24.6 201.6 %all-gather.2 = f32[1,3,10,1024]{2,0,1,3:T(1,128)S(1)} all-gather(f32[1,3,10,32]{2,0,1,3:T(1,128)S(1)} %copy.138), channel_id=2, replica_groups=mesh['mode'=32,'rows'=16] {'mode'}, dimensions={3}, use_global_device_ids=true | all-gather | bytes 126720 | tf_op jit(solution)/shard_map/while/body/eval_jaxpr/all_gather | solution.py:89
  228.5 3.1 copy.139
  240.5 4.3 collective-permute-start.2
  250.5 2.1 collective-permute-start
  252.6 4.1 collective-permute-start.1
  260.8 150.6 %all-gather.2 = f32[1,3,10,1024]{2,0,1,3:T(1,128)S(1)} all-gather(f32[1,3,10,32]{2,0,1,3:T(1,128)S(1)} %copy.138), channel_id=2, replica_groups=mesh['mode'=32,'rows'=16] {'mode'}, dimensions={3}, use_global_device_ids=true | all-gather | bytes 126720 | tf_op jit(solution)/shard_map/while/body/eval_jaxpr/all_gather | solution.py:89
  413.8 3.1 copy.139
  425.7 21.6 %collective-permute-start.2 = (f32[4,3,1,1024]{3,2,0,1:T(1,128)S(1)}, f32[4,3,1,1024]{3,2,0,1:T(1,128)S(1)}, u32[]{:S(2)}, u32[]{:S(2)}) collective-permute-start(f32[4,3,1,1024]{3,2,0,1:T(1,128)S(1)} %get-tuple-element.329), channel_id=1, source_target_pairs={{1,0},{2,1},{3,2},{4,3},{5,4},{6,5},{7,6},{8,7},{9,8},{10,9},{11,1... | collective-permute-start | bytes 147464 | tf_op jit(solution)/shard_map/while/body/eval_jaxpr/ppermute | solution.py:22
  453.1 2.1 collective-permute-start
  455.1 4.1 collective-permute-start.1
  463.4 144.8 %all-gather.2 = f32[1,3,10,1024]{2,0,1,3:T(1,128)S(1)} all-gather(f32[1,3,10,32]{2,0,1,3:T(1,128)S(1)} %copy.138), channel_id=2, replica_groups=mesh['mode'=32,'rows'=16] {'mode'}, dimensions={3}, use_global_device_ids=true | all-gather | bytes 126720 | tf_op jit(solution)/shard_map/while/body/eval_jaxpr/all_gather | solution.py:89
  610.5 3.1 copy.139
  622.5 12.8 collective-permute-start.2
  635.3 7.8 collective-permute-start.3
  648.7 4.2 collective-permute-start.1
  657.2 149.6 %all-gather.2 = f32[1,3,10,1024]{2,0,1,3:T(1,128)S(1)} all-gather(f32[1,3,10,32]{2,0,1,3:T(1,128)S(1)} %copy.138), channel_id=2, replica_groups=mesh['mode'=32,'rows'=16] {'mode'}, dimensions={3}, use_global_device_ids=true | all-gather | bytes 126720 | tf_op jit(solution)/shard_map/while/body/eval_jaxpr/all_gather | solution.py:89
  809.1 3.1 copy.139
  821.1 9.6 collective-permute-start.2
  830.7 6.7 collective-permute-start.3
  843.0 4.2 collective-permute-start.1
  851.5 146.7 %all-gather.2 = f32[1,3,10,1024]{2,0,1,3:T(1,128)S(1)} all-gather(f32[1,3,10,32]{2,0,1,3:T(1,128)S(1)} %copy.138), channel_id=2, replica_groups=mesh['mode'=32,'rows'=16] {'mode'}, dimensions={3}, use_global_device_ids=true | all-gather | bytes 126720 | tf_op jit(solution)/shard_map/while/body/eval_jaxpr/all_gather | solution.py:89
  1000.5 3.1 copy.139
  1012.5 12.5 collective-permute-start.2
  1025.0 15.0 collective-permute-start.3
  1045.6 4.2 collective-permute-start.1
  1054.1 147.2 %all-gather.2 = f32[1,3,10,1024]{2,0,1,3:T(1,128)S(1)} all-gather(f32[1,3,10,32]{2,0,1,3:T(1,128)S(1)} %copy.138), channel_id=2, replica_groups=mesh['mode'=32,'rows'=16] {'mode'}, dimensions={3}, use_global_device_ids=true | all-gather | bytes 126720 | tf_op jit(solution)/shard_map/while/body/eval_jaxpr/all_gather | solution.py:89
  1203.6 3.1 copy.139
  1215.5 11.4 collective-permute-start.2
  1227.0 2.0 collective-permute-start.3
  1234.7 4.2 collective-permute-start.1
  1243.1 145.4 %all-gather.2 = f32[1,3,10,1024]{2,0,1,3:T(1,128)S(1)} all-gather(f32[1,3,10,32]{2,0,1,3:T(1,128)S(1)} %copy.138), channel_id=2, replica_groups=mesh['mode'=32,'rows'=16] {'mode'}, dimensions={3}, use_global_device_ids=true | all-gather | bytes 126720 | tf_op jit(solution)/shard_map/while/body/eval_jaxpr/all_gather | solution.py:89
  1390.9 3.1 copy.139
  1402.8 14.8 collective-permute-start.2
  1417.7 16.1 collective-permute-start.3
  1439.4 4.2 collective-permute-start.1
  1447.9 149.4 %all-gather.2 = f32[1,3,10,1024]{2,0,1,3:T(1,128)S(1)} all-gather(f32[1,3,10,32]{2,0,1,3:T(1,128)S(1)} %copy.138), channel_id=2, replica_groups=mesh['mode'=32,'rows'=16] {'mode'}, dimensions={3}, use_global_device_ids=true | all-gather | bytes 126720 | tf_op jit(solution)/shard_map/while/body/eval_jaxpr/all_gather | solution.py:89
  1599.6 3.1 copy.139
  1611.5 14.3 collective-permute-start.2
  1630.8 4.6 copy.94
  1635.4 9.3 reshape.31
  1644.7 4.1 all-to-all-start
  1648.8 17.8 %all-to-all-done = f32[32,1,3072]{2,1,0:T(1,128)S(1)} async-done(((f32[32,1,3072]{2,1,0:T(1,128)}), f32[32,1,3072]{2,1,0:T(1,128)S(1)}, u32[]{:S(2)}, u32[]{:S(2)}) %all-to-all-start) | async-done | bytes 393248 | tf_op jit(solution)/shard_map/all_to_all | solution.py:104
  1668.7 9.2 reshape.32
  1677.9 5.6 copy.95
  (554 shorter events, 161.1 us)
Async XLA Ops:
  0.9 12.5 collective-permute-start.4
  5.9 7.6 collective-permute-start.5
  14.8 222.8 %collective-permute-start = (f32[4,3,1,1024]{3,2,0,1:T(1,128)}, f32[4,3,1,1024]{3,2,0,1:T(1,128)}, u32[]{:S(2)}, u32[]{:S(2)}) collective-permute-start(f32[4,3,1,1024]{3,2,0,1:T(1,128)} %get-tuple-element.286), channel_id=1, source_target_pairs={{1,0},{2,1},{3,2},{4,3},{5,4},{6,5},{7,6},{8,7},{9,8},{10,9},{11,1... | collective-permute-start | bytes 147464 | tf_op jit(solution)/shard_map/while/body/eval_jaxpr/ppermute | solution.py:22
  16.7 220.8 %collective-permute-start.1 = (f32[4,3,1,1024]{3,2,0,1:T(1,128)}, f32[4,3,1,1024]{3,2,0,1:T(1,128)}, u32[]{:S(2)}, u32[]{:S(2)}) collective-permute-start(f32[4,3,1,1024]{3,2,0,1:T(1,128)} %get-tuple-element.287), channel_id=1, source_target_pairs={{0,1},{1,2},{2,3},{3,4},{4,5},{5,6},{6,7},{7,8},{8,9},{9,10},{10,1... | collective-permute-start | bytes 147464 | tf_op jit(solution)/shard_map/while/body/eval_jaxpr/ppermute | solution.py:20
  234.4 2.4 copy-start.1
  234.4 2.4 copy-start.2
  240.5 6.3 collective-permute-start.2
  244.8 3.1 collective-permute-start.3
  250.5 172.4 %collective-permute-start = (f32[4,3,1,1024]{3,2,0,1:T(1,128)}, f32[4,3,1,1024]{3,2,0,1:T(1,128)}, u32[]{:S(2)}, u32[]{:S(2)}) collective-permute-start(f32[4,3,1,1024]{3,2,0,1:T(1,128)} %get-tuple-element.286), channel_id=1, source_target_pairs={{1,0},{2,1},{3,2},{4,3},{5,4},{6,5},{7,6},{8,7},{9,8},{10,9},{11,1... | collective-permute-start | bytes 147464 | tf_op jit(solution)/shard_map/while/body/eval_jaxpr/ppermute | solution.py:22
  252.6 170.3 %collective-permute-start.1 = (f32[4,3,1,1024]{3,2,0,1:T(1,128)}, f32[4,3,1,1024]{3,2,0,1:T(1,128)}, u32[]{:S(2)}, u32[]{:S(2)}) collective-permute-start(f32[4,3,1,1024]{3,2,0,1:T(1,128)} %get-tuple-element.287), channel_id=1, source_target_pairs={{0,1},{1,2},{2,3},{3,4},{4,5},{5,6},{6,7},{7,8},{8,9},{9,10},{10,1... | collective-permute-start | bytes 147464 | tf_op jit(solution)/shard_map/while/body/eval_jaxpr/ppermute | solution.py:20
  419.7 2.4 copy-start.1
  419.7 2.4 copy-start.2
  425.7 23.6 %collective-permute-start.2 = (f32[4,3,1,1024]{3,2,0,1:T(1,128)S(1)}, f32[4,3,1,1024]{3,2,0,1:T(1,128)S(1)}, u32[]{:S(2)}, u32[]{:S(2)}) collective-permute-start(f32[4,3,1,1024]{3,2,0,1:T(1,128)S(1)} %get-tuple-element.329), channel_id=1, source_target_pairs={{1,0},{2,1},{3,2},{4,3},{5,4},{6,5},{7,6},{8,7},{9,8},{10,9},{11,1... | collective-permute-start | bytes 147464 | tf_op jit(solution)/shard_map/while/body/eval_jaxpr/ppermute | solution.py:22
  447.4 3.1 collective-permute-start.3
  453.1 166.5 %collective-permute-start = (f32[4,3,1,1024]{3,2,0,1:T(1,128)}, f32[4,3,1,1024]{3,2,0,1:T(1,128)}, u32[]{:S(2)}, u32[]{:S(2)}) collective-permute-start(f32[4,3,1,1024]{3,2,0,1:T(1,128)} %get-tuple-element.286), channel_id=1, source_target_pairs={{1,0},{2,1},{3,2},{4,3},{5,4},{6,5},{7,6},{8,7},{9,8},{10,9},{11,1... | collective-permute-start | bytes 147464 | tf_op jit(solution)/shard_map/while/body/eval_jaxpr/ppermute | solution.py:22
  455.1 164.5 %collective-permute-start.1 = (f32[4,3,1,1024]{3,2,0,1:T(1,128)}, f32[4,3,1,1024]{3,2,0,1:T(1,128)}, u32[]{:S(2)}, u32[]{:S(2)}) collective-permute-start(f32[4,3,1,1024]{3,2,0,1:T(1,128)} %get-tuple-element.287), channel_id=1, source_target_pairs={{0,1},{1,2},{2,3},{3,4},{4,5},{5,6},{6,7},{7,8},{8,9},{9,10},{10,1... | collective-permute-start | bytes 147464 | tf_op jit(solution)/shard_map/while/body/eval_jaxpr/ppermute | solution.py:20
  616.4 2.4 copy-start.1
  616.4 2.4 copy-start.2
  622.5 20.6 %collective-permute-start.2 = (f32[4,3,1,1024]{3,2,0,1:T(1,128)S(1)}, f32[4,3,1,1024]{3,2,0,1:T(1,128)S(1)}, u32[]{:S(2)}, u32[]{:S(2)}) collective-permute-start(f32[4,3,1,1024]{3,2,0,1:T(1,128)S(1)} %get-tuple-element.329), channel_id=1, source_target_pairs={{1,0},{2,1},{3,2},{4,3},{5,4},{6,5},{7,6},{8,7},{9,8},{10,9},{11,1... | collective-permute-start | bytes 147464 | tf_op jit(solution)/shard_map/while/body/eval_jaxpr/ppermute | solution.py:22
  635.3 9.0 collective-permute-start.3
  646.8 171.4 %collective-permute-start = (f32[4,3,1,1024]{3,2,0,1:T(1,128)}, f32[4,3,1,1024]{3,2,0,1:T(1,128)}, u32[]{:S(2)}, u32[]{:S(2)}) collective-permute-start(f32[4,3,1,1024]{3,2,0,1:T(1,128)} %get-tuple-element.286), channel_id=1, source_target_pairs={{1,0},{2,1},{3,2},{4,3},{5,4},{6,5},{7,6},{8,7},{9,8},{10,9},{11,1... | collective-permute-start | bytes 147464 | tf_op jit(solution)/shard_map/while/body/eval_jaxpr/ppermute | solution.py:22
  648.7 169.5 %collective-permute-start.1 = (f32[4,3,1,1024]{3,2,0,1:T(1,128)}, f32[4,3,1,1024]{3,2,0,1:T(1,128)}, u32[]{:S(2)}, u32[]{:S(2)}) collective-permute-start(f32[4,3,1,1024]{3,2,0,1:T(1,128)} %get-tuple-element.287), channel_id=1, source_target_pairs={{0,1},{1,2},{2,3},{3,4},{4,5},{5,6},{6,7},{7,8},{8,9},{9,10},{10,1... | collective-permute-start | bytes 147464 | tf_op jit(solution)/shard_map/while/body/eval_jaxpr/ppermute | solution.py:20
  815.0 2.4 copy-start.1
  815.0 2.4 copy-start.2
  821.1 16.3 collective-permute-start.2
  830.7 7.8 collective-permute-start.3
  841.1 168.5 %collective-permute-start = (f32[4,3,1,1024]{3,2,0,1:T(1,128)}, f32[4,3,1,1024]{3,2,0,1:T(1,128)}, u32[]{:S(2)}, u32[]{:S(2)}) collective-permute-start(f32[4,3,1,1024]{3,2,0,1:T(1,128)} %get-tuple-element.286), channel_id=1, source_target_pairs={{1,0},{2,1},{3,2},{4,3},{5,4},{6,5},{7,6},{8,7},{9,8},{10,9},{11,1... | collective-permute-start | bytes 147464 | tf_op jit(solution)/shard_map/while/body/eval_jaxpr/ppermute | solution.py:22
  843.0 166.6 %collective-permute-start.1 = (f32[4,3,1,1024]{3,2,0,1:T(1,128)}, f32[4,3,1,1024]{3,2,0,1:T(1,128)}, u32[]{:S(2)}, u32[]{:S(2)}) collective-permute-start(f32[4,3,1,1024]{3,2,0,1:T(1,128)} %get-tuple-element.287), channel_id=1, source_target_pairs={{0,1},{1,2},{2,3},{3,4},{4,5},{5,6},{6,7},{7,8},{8,9},{9,10},{10,1... | collective-permute-start | bytes 147464 | tf_op jit(solution)/shard_map/while/body/eval_jaxpr/ppermute | solution.py:20
  1006.4 2.4 copy-start.1
  1006.4 2.4 copy-start.2
  1012.5 27.5 %collective-permute-start.2 = (f32[4,3,1,1024]{3,2,0,1:T(1,128)S(1)}, f32[4,3,1,1024]{3,2,0,1:T(1,128)S(1)}, u32[]{:S(2)}, u32[]{:S(2)}) collective-permute-start(f32[4,3,1,1024]{3,2,0,1:T(1,128)S(1)} %get-tuple-element.329), channel_id=1, source_target_pairs={{1,0},{2,1},{3,2},{4,3},{5,4},{6,5},{7,6},{8,7},{9,8},{10,9},{11,1... | collective-permute-start | bytes 147464 | tf_op jit(solution)/shard_map/while/body/eval_jaxpr/ppermute | solution.py:22
  1025.0 16.2 collective-permute-start.3
  1043.7 169.0 %collective-permute-start = (f32[4,3,1,1024]{3,2,0,1:T(1,128)}, f32[4,3,1,1024]{3,2,0,1:T(1,128)}, u32[]{:S(2)}, u32[]{:S(2)}) collective-permute-start(f32[4,3,1,1024]{3,2,0,1:T(1,128)} %get-tuple-element.286), channel_id=1, source_target_pairs={{1,0},{2,1},{3,2},{4,3},{5,4},{6,5},{7,6},{8,7},{9,8},{10,9},{11,1... | collective-permute-start | bytes 147464 | tf_op jit(solution)/shard_map/while/body/eval_jaxpr/ppermute | solution.py:22
  1045.6 167.0 %collective-permute-start.1 = (f32[4,3,1,1024]{3,2,0,1:T(1,128)}, f32[4,3,1,1024]{3,2,0,1:T(1,128)}, u32[]{:S(2)}, u32[]{:S(2)}) collective-permute-start(f32[4,3,1,1024]{3,2,0,1:T(1,128)} %get-tuple-element.287), channel_id=1, source_target_pairs={{0,1},{1,2},{2,3},{3,4},{4,5},{5,6},{6,7},{7,8},{8,9},{9,10},{10,1... | collective-permute-start | bytes 147464 | tf_op jit(solution)/shard_map/while/body/eval_jaxpr/ppermute | solution.py:20
  1209.5 2.4 copy-start.2
  1215.5 13.5 collective-permute-start.2
  1227.0 3.2 collective-permute-start.3
  1232.7 167.2 %collective-permute-start = (f32[4,3,1,1024]{3,2,0,1:T(1,128)}, f32[4,3,1,1024]{3,2,0,1:T(1,128)}, u32[]{:S(2)}, u32[]{:S(2)}) collective-permute-start(f32[4,3,1,1024]{3,2,0,1:T(1,128)} %get-tuple-element.286), channel_id=1, source_target_pairs={{1,0},{2,1},{3,2},{4,3},{5,4},{6,5},{7,6},{8,7},{9,8},{10,9},{11,1... | collective-permute-start | bytes 147464 | tf_op jit(solution)/shard_map/while/body/eval_jaxpr/ppermute | solution.py:22
  1234.7 165.2 %collective-permute-start.1 = (f32[4,3,1,1024]{3,2,0,1:T(1,128)}, f32[4,3,1,1024]{3,2,0,1:T(1,128)}, u32[]{:S(2)}, u32[]{:S(2)}) collective-permute-start(f32[4,3,1,1024]{3,2,0,1:T(1,128)} %get-tuple-element.287), channel_id=1, source_target_pairs={{0,1},{1,2},{2,3},{3,4},{4,5},{5,6},{6,7},{7,8},{8,9},{9,10},{10,1... | collective-permute-start | bytes 147464 | tf_op jit(solution)/shard_map/while/body/eval_jaxpr/ppermute | solution.py:20
  1396.7 2.4 copy-start.2
  1402.8 31.0 %collective-permute-start.2 = (f32[4,3,1,1024]{3,2,0,1:T(1,128)S(1)}, f32[4,3,1,1024]{3,2,0,1:T(1,128)S(1)}, u32[]{:S(2)}, u32[]{:S(2)}) collective-permute-start(f32[4,3,1,1024]{3,2,0,1:T(1,128)S(1)} %get-tuple-element.329), channel_id=1, source_target_pairs={{1,0},{2,1},{3,2},{4,3},{5,4},{6,5},{7,6},{8,7},{9,8},{10,9},{11,1... | collective-permute-start | bytes 147464 | tf_op jit(solution)/shard_map/while/body/eval_jaxpr/ppermute | solution.py:22
  1417.7 17.3 %collective-permute-start.3 = (f32[4,3,1,1024]{3,2,0,1:T(1,128)S(1)}, f32[4,3,1,1024]{3,2,0,1:T(1,128)S(1)}, u32[]{:S(2)}, u32[]{:S(2)}) collective-permute-start(f32[4,3,1,1024]{3,2,0,1:T(1,128)S(1)} %get-tuple-element.330), channel_id=1, source_target_pairs={{0,1},{1,2},{2,3},{3,4},{4,5},{5,6},{6,7},{7,8},{8,9},{9,10},{10,1... | collective-permute-start | bytes 147464 | tf_op jit(solution)/shard_map/while/body/eval_jaxpr/ppermute | solution.py:20
  1437.5 171.1 %collective-permute-start = (f32[4,3,1,1024]{3,2,0,1:T(1,128)}, f32[4,3,1,1024]{3,2,0,1:T(1,128)}, u32[]{:S(2)}, u32[]{:S(2)}) collective-permute-start(f32[4,3,1,1024]{3,2,0,1:T(1,128)} %get-tuple-element.286), channel_id=1, source_target_pairs={{1,0},{2,1},{3,2},{4,3},{5,4},{6,5},{7,6},{8,7},{9,8},{10,9},{11,1... | collective-permute-start | bytes 147464 | tf_op jit(solution)/shard_map/while/body/eval_jaxpr/ppermute | solution.py:22
  1439.4 169.2 %collective-permute-start.1 = (f32[4,3,1,1024]{3,2,0,1:T(1,128)}, f32[4,3,1,1024]{3,2,0,1:T(1,128)}, u32[]{:S(2)}, u32[]{:S(2)}) collective-permute-start(f32[4,3,1,1024]{3,2,0,1:T(1,128)} %get-tuple-element.287), channel_id=1, source_target_pairs={{0,1},{1,2},{2,3},{3,4},{4,5},{5,6},{6,7},{7,8},{8,9},{9,10},{10,1... | collective-permute-start | bytes 147464 | tf_op jit(solution)/shard_map/while/body/eval_jaxpr/ppermute | solution.py:20
  1605.4 2.4 copy-start.2
  1611.5 16.2 collective-permute-start.2
  1625.8 3.1 collective-permute-start.3
  1644.7 21.9 %all-to-all-start = ((f32[32,1,3072]{2,1,0:T(1,128)}), f32[32,1,3072]{2,1,0:T(1,128)S(1)}, u32[]{:S(2)}, u32[]{:S(2)}) async-start(f32[32,1,3072]{2,1,0:T(1,128)} %reshape.31), calls=%async_computation | async-start | bytes 786432 | tf_op jit(solution)/shard_map/all_to_all | solution.py:104
  (21 other events, 30.7 us)
where the time goes:
time: 1700 us; the launch traced here: 1690 us
  blocking collectives  1240 us (73%)
  starting transfers between devices  217 us (13%)
  local copies, waits for them, and re-layouts  139 us (8%)
  other arithmetic  47.6 us (3%)
  waiting for transfers between devices  27.2 us (2%)
  loops' own time  17.7 us (1%)
    all_gather x8, blocking collectives, fetch_flow(): return lax.all_gather(held_tile, 'mode', axis=2, tiled=True)  1240 us
    ppermute x17, starting transfers between devices, padded(): lax.ppermute(head, axis, [((i + 1) % count, i) for i in range(ends)])  122 us
    ppermute x17, starting transfers between devices, padded(): lax.ppermute(tail, axis, [(i, (i + 1) % count) for i in range(ends)])  91.2 us
    slice x208, local copies, waits for them, and re-layouts, deriv_x(): return 0.5 * (jnp.roll(values, -1, -1) - jnp.roll(values, 1, -1))  49.1 us
  transfers between devices with their start and end apart: 35, of which 9 were waited for; matrix products, arithmetic and copies ran while one was open for 7% of the time, Pallas kernels for 0%

commit v1 on v0

v1 whole, which is shorter than its diff:
```python
import jax
import jax.numpy as jnp
from jax import lax
from jax.experimental import pallas as pl
from jax.experimental.pallas import tpu as pltpu
from jax.sharding import PartitionSpec as P

SIZES = (4, 2, 4, 8, 2)
AXES = ("y", "zh", "x", "zl", "c")
STEPS = 8
LANES = 128
HALO = 16
STRIP = 16
TALL = STRIP + 2 * HALO
PEERS = 16
COEFS = 15
f32 = jnp.float32


def edges(left, right, left_turned, right_turned, lane):
    zero = jnp.zeros_like(left)
    out = jnp.where((lane >= 64) & (lane < 80), right_turned, zero)
    out = jnp.where((lane >= 48) & (lane < 64), left_turned, out)
    out = jnp.where(lane < 16, right, out)
    return jnp.where(lane >= 112, left, out)


def from_right(cells, lane):
    a, b, c = (pltpu.roll(x, LANES - 1, 1) for x in cells)
    last, mid = lane == LANES - 1, lane == 63
    return jnp.where(last, c, a), jnp.where(mid, c, b), jnp.where(last, a, jnp.where(mid, b, c))


def from_left(cells, lane):
    a, b, c = (pltpu.roll(x, 1, 1) for x in cells)
    first, mid = lane == 0, lane == 64
    return jnp.where(first, c, a), jnp.where(mid, c, b), jnp.where(first, a, jnp.where(mid, b, c))


def pack_kernel(block_ref, order_ref, tan_ref, base_ref, mask_ref, send_ref, flow_ref, wet_ref):
    lane = lax.broadcasted_iota(jnp.int32, (8, LANES), 1)
    wet = [mask_ref[:, k * LANES : (k + 1) * LANES].astype(f32) for k in range(8)]
    for core in range(2):
        for f in range(3):
            one = [tan_ref[2 * core, f, :, k * LANES : (k + 1) * LANES] * wet[k] for k in range(8)]
            two = [
                pltpu.roll(tan_ref[2 * core + 1, f, :, k * LANES : (k + 1) * LANES] * wet[k], 64, 1) for k in range(8)
            ]
            for s in range(8):
                left, right = (s + 7) % 8, (s + 1) % 8
                halo = edges(one[left], one[right], two[left], two[right], lane)
                for v, part in enumerate((one[s], two[s], halo)):
                    send_ref[2 * s + core, v * 24 + f * 8 : v * 24 + f * 8 + 8, :] = part
    s = block_ref[0]

    def column(k):
        return mask_ref[:, pl.ds(pl.multiple_of(k * LANES, LANES), LANES)].astype(f32)

    here, left, right = column(s), column(lax.rem(s + 7, 8)), column(lax.rem(s + 1, 8))
    wet_ref[0:8, :] = here
    wet_ref[8:16, :] = pltpu.roll(here, 64, 1)
    wet_ref[16:24, :] = edges(left, right, pltpu.roll(left, 64, 1), pltpu.roll(right, 64, 1), lane)
    for high in range(2):
        for f in range(3):
            flow = jnp.concatenate([base_ref[order_ref[high * 4 + low], f] for low in range(4)], axis=1)
            for k in range(4):
                flow_ref[k, (high * 3 + f) * 8 : (high * 3 + f) * 8 + 8, :] = flow


def march_kernel(
    core_ref, prev_ref, own_ref, next_ref, sp_ref, so_ref, sn_ref, tp_ref, to_ref, tn_ref,
    out_ref, state, middle, base, wet, coef,
):
    lane = lax.broadcasted_iota(jnp.int32, (8, LANES), 1)
    for z, ref in enumerate((prev_ref, own_ref, next_ref)):
        for c in range(2):
            for f in range(3):
                for r in range(8):
                    for v in range(3):
                        state[f, z * 16 + c * 8 + r, v] = ref[pl.ds(c * 72 + v * 24 + f * 8 + r, 8, stride=144), :]
    core = core_ref[0]
    for turn, refs in enumerate(((sp_ref, so_ref, sn_ref), (tp_ref, to_ref, tn_ref))):
        place = core if turn == 0 else 1 - core
        for z, ref in enumerate(refs):
            top = pl.multiple_of(place * 8 + z * 16, 8)
            for v in range(3):
                wet[v, pl.ds(top, 8), :] = ref[288 + v * 8 : 288 + v * 8 + 8, :] * 0.25
            for high in range(2):
                for f in range(3):
                    at = (high * 3 + f) * 8
                    quads = [ref[x * 48 + at : x * 48 + at + 8, :] for x in range(4)]
                    lefts = ref[192 + at : 192 + at + 8, :]
                    rights = ref[240 + at : 240 + at + 8, :]
                    for low in range(4):
                        out = pltpu.roll(quads[0], (128 - 32 * low) % 128, 1) if low else quads[0]
                        for x in range(1, 4):
                            turned = pltpu.roll(quads[x], 32 * (x - low) % 128, 1) if x != low else quads[x]
                            out = jnp.where(lane >= 32 * x, turned, out)
                        left = pltpu.roll(lefts, (96 - 32 * low) % 128, 1)
                        left_turned = pltpu.roll(lefts, (160 - 32 * low) % 128, 1)
                        right = pltpu.roll(rights, (128 - 32 * low) % 128, 1)
                        right_turned = pltpu.roll(rights, (192 - 32 * low) % 128, 1)
                        halo = edges(left, right, left_turned, right_turned, lane)
                        rows = pl.ds(top + 8, 8)
                        base[high * 4 + low, f, 0, rows, :] = out
                        base[high * 4 + low, f, 1, rows, :] = pltpu.roll(out, 64, 1)
                        base[high * 4 + low, f, 2, rows, :] = halo

    def prepare(step, tile):
        top = tile * 8
        w = [wet[v, top : top + 8, :] for v in range(3)]

        def rows(f, shift):
            return [base[step, f, v, top + 8 + shift : top + 16 + shift, :] for v in range(3)]

        depth = [x + 1.0 for x in rows(0, 0)]
        b, c = rows(1, 0), rows(2, 0)
        hp, hm = from_right(depth, lane), from_left(depth, lane)
        bp, bm = from_right(b, lane), from_left(b, lane)
        cp, cm = from_right(c, lane), from_left(c, lane)
        hn, hs = rows(0, 1), rows(0, -1)
        bn, bs = rows(1, 1), rows(1, -1)
        cn, cs = rows(2, 1), rows(2, -1)
        for v in range(3):
            q = w[v]
            parts = (
                -q * hp[v], q * hm[v], -q * bp[v], q * bm[v],
                -q * (hn[v] + 1.0), q * (hs[v] + 1.0), -q * cn[v], q * cs[v],
                -q * b[v], -q * c[v],
                -q * (bp[v] - bm[v]), q * (1.0 - (bn[v] - bs[v])), -q * (1.0 + (cp[v] - cm[v])), -q * (cn[v] - cs[v]),
                q,
            )
            for k, part in enumerate(parts):
                coef[k, v, top : top + 8, :] = part

    def rates(ref, r):
        h, u, m = ([ref[f, r, v] for v in range(3)] for f in range(3))
        hn, un, mn = ([ref[f, r + 1, v] for v in range(3)] for f in range(3))
        hs, us, ms = ([ref[f, r - 1, v] for v in range(3)] for f in range(3))
        hp, hm = from_right(h, lane), from_left(h, lane)
        up, um = from_right(u, lane), from_left(u, lane)
        mp, mm = from_right(m, lane), from_left(m, lane)
        fields = ([], [], [])
        for v in range(3):
            k = [coef[i, v, pl.ds(r, 1), :] for i in range(COEFS)]
            fields[0].append(
                ((k[0] * up[v] + k[1] * um[v]) + (k[2] * hp[v] + k[3] * hm[v]))
                + ((k[4] * mn[v] + k[5] * ms[v]) + (k[6] * hn[v] + k[7] * hs[v]))
            )
            fields[1].append(
                (k[8] * (up[v] - um[v]) + k[9] * (un[v] - us[v]))
                + ((k[10] * u[v] + k[11] * m[v]) - k[14] * (hp[v] - hm[v]))
            )
            fields[2].append(
                (k[8] * (mp[v] - mm[v]) + k[9] * (mn[v] - ms[v]))
                + ((k[12] * u[v] + k[13] * m[v]) - k[14] * (hn[v] - hs[v]))
            )
        return fields

    for step in range(STEPS):
        low, high = 2 * step + 1, TALL - 2 * step - 1
        for tile in range(low // 8, (high + 7) // 8):
            prepare(step, tile)

        def first(i, _, low=low):
            for r in (low + 2 * i, low + 2 * i + 1):
                change = rates(state, r)
                for f in range(3):
                    for v in range(3):
                        middle[f, r, v] = state[f, r, v] + change[f][v]
            return _

        lax.fori_loop(0, (high - low) // 2, first, 0)

        def second(i, _, low=low + 1):
            for r in (low + 2 * i, low + 2 * i + 1):
                change = rates(middle, r)
                for f in range(3):
                    for v in range(3):
                        state[f, r, v] = 0.5 * ((state[f, r, v] + middle[f, r, v]) + change[f][v])
            return _

        lax.fori_loop(0, (high - low - 2) // 2, second, 0)

    for c in range(2):
        for f in range(3):
            for high in range(2):
                for v in range(2):
                    lines = [state[f, HALO + c * 8 + high * 4 + low, v] for low in range(4)]
                    for x in range(4):
                        at = (x + 2 * v) % 4
                        out = pltpu.roll(lines[0], (128 - 32 * at) % 128, 1) if at else lines[0]
                        for low in range(1, 4):
                            turned = pltpu.roll(lines[low], 32 * (low - at) % 128, 1) if low != at else lines[low]
                            out = jnp.where(lane >= 32 * low, turned, out)
                        row = ((f * 2 + high) * 2 + v) * 8
                        out_ref[x * 2 + c, row : row + 8, :] = out


def mix_kernel(coef_ref, cells_ref, out_ref, mixing):
    row = lax.broadcasted_iota(jnp.int32, (128, 128), 0)
    col = lax.broadcasted_iota(jnp.int32, (128, 128), 1)
    mixing[...] = jnp.where(row <= col, coef_ref[...], 0.0) + jnp.where(row == col, 1.0, 0.0)
    matrix = jnp.concatenate([mixing[pl.ds(t, 8, stride=16), :] for t in range(16)], axis=0)
    for k in range(6):
        cells = jnp.concatenate([cells_ref[p * 96 + k * 16 : p * 96 + k * 16 + 16, :] for p in range(8)], axis=0)
        out_ref[k * 128 : (k + 1) * 128, :] = lax.dot_general(
            cells, matrix, (((0,), (0,)), ((), ())), precision=lax.Precision.HIGHEST, preferred_element_type=f32
        )


VMEM = pl.BlockSpec(memory_space=pltpu.VMEM)
SMEM = pl.BlockSpec(memory_space=pltpu.SMEM)


def on_device(tangents, checkpoints, owner_order, land_mask, coefficients):
    block = lax.axis_index("y") * 2 + lax.axis_index("zh")
    core = lax.axis_index("c")
    send, flow, wet = pl.pallas_call(
        pack_kernel,
        out_shape=(
            jax.ShapeDtypeStruct((PEERS, 72, LANES), f32),
            jax.ShapeDtypeStruct((4, 48, LANES), f32),
            jax.ShapeDtypeStruct((24, LANES), f32),
        ),
        in_specs=[SMEM, SMEM, VMEM, VMEM, VMEM],
        out_specs=(VMEM, VMEM, VMEM),
        compiler_params=pltpu.CompilerParams(vmem_limit_bytes=16 * 2**20),
    )(block.reshape(1).astype(jnp.int32), owner_order, tangents, checkpoints, land_mask)

    up = [(i, i + 1) for i in range(7)]
    down = [(i + 1, i) for i in range(7)]
    flows = lax.all_to_all(flow, "x", 0, 0, tiled=True)
    left = lax.ppermute(flows[3], ("y", "zh"), [(i, (i + 1) % 8) for i in range(8)])
    right = lax.ppermute(flows[0], ("y", "zh"), [((i + 1) % 8, i) for i in range(8)])
    strip = jnp.concatenate([flows.reshape(192, LANES), left, right, wet], axis=0)
    strips = [lax.ppermute(strip, "zl", up), strip, lax.ppermute(strip, "zl", down)]
    others = [lax.ppermute(x, "c", [(0, 1), (1, 0)]) for x in strips]

    own = lax.all_to_all(send, ("y", "zh", "c"), 0, 0, tiled=True)
    parts = [lax.ppermute(own, "zl", up), own, lax.ppermute(own, "zl", down)]
    parts = [x.reshape(PEERS * 72, LANES) for x in parts]
    out = pl.pallas_call(
        march_kernel,
        out_shape=jax.ShapeDtypeStruct((8, 96, LANES), f32),
        in_specs=[SMEM] + [VMEM] * 9,
        out_specs=VMEM,
        scratch_shapes=[
            pltpu.VMEM((3, TALL, 3, 8, LANES), f32),
            pltpu.VMEM((3, TALL, 3, 8, LANES), f32),
            pltpu.VMEM((STEPS, 3, 3, TALL + 16, LANES), f32),
            pltpu.VMEM((3, TALL, LANES), f32),
            pltpu.VMEM((COEFS, 3, TALL, LANES), f32),
        ],
        compiler_params=pltpu.CompilerParams(vmem_limit_bytes=32 * 2**20),
    )(core.reshape(1).astype(jnp.int32), *parts, *strips, *others)
    cells = lax.all_to_all(out, ("x", "c"), 0, 0, tiled=True)
    mixed = pl.pallas_call(
        mix_kernel,
        out_shape=jax.ShapeDtypeStruct((768, 128), f32),
        in_specs=[VMEM, VMEM],
        out_specs=VMEM,
        scratch_shapes=[pltpu.VMEM((128, 128), f32)],
        compiler_params=pltpu.CompilerParams(vmem_limit_bytes=16 * 2**20),
    )(coefficients, cells.reshape(768, LANES))
    return mixed.reshape(3, 8, 32, 128).transpose(3, 0, 1, 2)


def solution(mesh):
    fine = jax.sharding.Mesh(mesh.devices.reshape(SIZES), AXES)
    mode, rows = ("y", "zh", "x"), ("zl", "c")
    placed = (
        P(mode, None, rows, None),
        P(None, None, rows, mode),
        P(),
        P(rows, None),
        P(),
    )
    return jax.shard_map(
        on_device, mesh=fine, in_specs=placed, out_specs=P(None, None, rows, mode), check_vma=False
    )
```

time: 1700 us -> 160 us (0.09)
  blocking collectives: 1240 us -> 57.2 us
  starting transfers between devices: 217 us -> 52.8 us
  local copies, waits for them, and re-layouts: 139 us -> 3.31 us
  other arithmetic: 47.6 us -> 0.01 us
  Pallas kernels: 0 us -> 44.2 us
  waiting for transfers between devices: 27.2 us -> 1.93 us
  loops' own time: 17.7 us -> 0 us
    all_gather x8 -> x0, blocking collectives: 1240 us -> none  [fetch_flow(): return lax.all_gather(held_tile, 'mode', axis=2, tiled=True)]
    ppermute x34 -> x9, starting transfers between devices: 213 us -> 48.8 us  [the longest x2 18.5 us: on_device(): parts = [lax.ppermute(own, 'zl', up), own, lax.ppermute(own, 'zl', down)]]
    all_to_all x0 -> x2, blocking collectives: none -> 57.2 us  [the longest x1 44.1 us: on_device(): own = lax.all_to_all(send, ('y', 'zh', 'c'), 0, 0, tiled=True)]
    slice x225 -> x0, local copies, waits for them, and re-layouts: 55.3 us -> none  [the longest x208 49.1 us: deriv_x(): return 0.5 * (jnp.roll(values, -1, -1) - jnp.roll(values, 1, -1))]
    pallas_call x0 -> x3, Pallas kernels: none -> 44.2 us  [the longest x1 41.6 us: on_device(): pl.pallas_call(march_kernel, out_shape=jax.ShapeDtypeStruct((8, 96, LANES...]
    all_gather x8 -> x0, local copies, waits for them, and re-layouts: 24.7 us -> none  [fetch_flow(): return lax.all_gather(held_tile, 'mode', axis=2, tiled=True)]
    dynamic_slice x24 -> x0, local copies, waits for them, and re-layouts: 18.2 us -> none  [the longest x8 9.95 us: fetch_flow(): owner_order[step_index]]
    all_to_all x1, waiting for transfers between devices: 17.8 us -> 0.01 us  [on_device(): flows = lax.all_to_all(flow, 'x', 0, 0, tiled=True)]
  transfers between devices with their start and end apart: 35 -> 10, of which waited for: 9 -> 2; matrix products, arithmetic and copies ran while one was open for 7% -> 0% of each run, Pallas kernels for 0% -> 0%
where the time goes in v1:
time: 160 us
  blocking collectives  57.2 us (36%)
  starting transfers between devices  52.8 us (33%)
  Pallas kernels  44.2 us (28%)
  local copies, waits for them, and re-layouts  3.31 us (2%)
  waiting for transfers between devices  1.93 us (1%)
    all_to_all x1, blocking collectives, on_device(): own = lax.all_to_all(send, ('y', 'zh', 'c'), 0, 0, tiled=True)  44.1 us
    pallas_call x1, Pallas kernels, on_device(): pl.pallas_call(march_kernel, out_shape=jax.ShapeDtypeStruct((8, 96, LANES...  41.6 us
    ppermute x2, starting transfers between devices, on_device(): parts = [lax.ppermute(own, 'zl', up), own, lax.ppermute(own, 'zl', down)]  18.5 us
    ppermute x1, starting transfers between devices, on_device(): lax.ppermute(flows[0], ('y', 'zh'), [((i + 1) % 8, i) for i in range(8)])  13.9 us
    all_to_all x1, blocking collectives, on_device(): cells = lax.all_to_all(out, ('x', 'c'), 0, 0, tiled=True)  13.2 us
    ppermute x3, starting transfers between devices, on_device(): others = [lax.ppermute(x, 'c', [(0, 1), (1, 0)]) for x in strips]  8.91 us
    all_to_all x1, starting transfers between devices, on_device(): flows = lax.all_to_all(flow, 'x', 0, 0, tiled=True)  4.01 us
    ppermute x1, starting transfers between devices, on_device(): lax.ppermute(strip, 'zl', up)  4 us
  transfers between devices with their start and end apart: 10, of which 2 were waited for; matrix products, arithmetic and copies ran while one was open for 0% of the time, Pallas kernels for 0%

profile of v1, /device:TPU:1, one launch (start us, length us, event | category | flops | bytes accessed | tf_op | source)
XLA Modules:
  0.0 159.6 jit_solution(10798732872370382235)
XLA Ops:
  0.0 0.0 copy-start.4
  0.0 0.7 copy-done.4
  0.7 0.0 copy-start
  0.7 1.0 copy-done
  1.7 0.0 copy-start.1
  1.7 0.9 copy-done.1
  2.5 0.0 copy-start.3
  2.5 0.8 copy-done.3
  3.3 1.3 shard_map.55
  4.6 44.1 %all_to_all.15 = f32[16,72,128]{2,1,0:T(8,128)S(1)} all-to-all(f32[16,72,128]{2,1,0:T(8,128)S(1)} %get-tuple-element.8), channel_id=1, replica_groups=mesh['y'=4,'zh'=2,'x'=4,'zl'=8,'c'=2] {'y','zh','c'}, dimensions={0} | all-to-all | bytes 1179648 | tf_op jit(solution)/shard_map/all_to_all | solution.py:240
  48.7 4.0 %all-to-all-start.1 = ((f32[4,48,128]{2,1,0:T(8,128)}), f32[4,48,128]{2,1,0:T(8,128)S(1)}, u32[]{:S(2)}, u32[]{:S(2)}) async-start(f32[4,48,128]{2,1,0:T(8,128)} %get-tuple-element.9), calls=%async_computation.1 | async-start | bytes 196608 | tf_op jit(solution)/shard_map/all_to_all | solution.py:233
  52.7 1.3 collective-permute-start.1
  54.0 17.2 %collective-permute-start = (f32[16,72,128]{2,1,0:T(8,128)S(1)}, f32[16,72,128]{2,1,0:T(8,128)S(1)}, u32[]{:S(2)}, u32[]{:S(2)}) collective-permute-start(f32[16,72,128]{2,1,0:T(8,128)S(1)} %all_to_all.15), channel_id=1, source_target_pairs={{0,2},{2,4},{4,6},{6,8},{8,10},{10,12},{12,14},{1,3},{3,5},{5,7},{... | collective-permute-start | bytes 1769480 | tf_op jit(solution)/shard_map/ppermute | solution.py:241
  71.2 0.0 all-to-all-done.1
  71.2 2.2 %collective-permute-start.2 = (f32[48,128]{1,0:T(8,128)S(1)}, f32[48,128]{1,0:T(8,128)S(1)}, u32[]{:S(2)}, u32[]{:S(2)}) collective-permute-start(f32[48,128]{1,0:T(8,128)S(1)} %get-tuple-element.11), channel_id=1, source_target_pairs={{0,64},{64,128},{128,192},{192,256},{256,320},{320,384},{384,448},... | collective-permute-start | bytes 73736 | tf_op jit(solution)/shard_map/ppermute | solution.py:234
  73.5 13.9 %collective-permute-start.3 = (f32[48,128]{1,0:T(8,128)S(1)}, f32[48,128]{1,0:T(8,128)S(1)}, u32[]{:S(2)}, u32[]{:S(2)}) collective-permute-start(f32[48,128]{1,0:T(8,128)S(1)} %get-tuple-element.12), channel_id=1, source_target_pairs={{64,0},{128,64},{192,128},{256,192},{320,256},{384,320},{448,384},... | collective-permute-start | bytes 73736 | tf_op jit(solution)/shard_map/ppermute | solution.py:235
  87.3 0.0 collective-permute-done.2
  87.3 0.9 collective-permute-done.3
  88.3 1.3 collective-permute-start.5
  89.6 4.0 %collective-permute-start.4 = (f32[312,128]{1,0:T(8,128)S(1)}, f32[312,128]{1,0:T(8,128)S(1)}, u32[]{:S(2)}, u32[]{:S(2)}) collective-permute-start(f32[312,128]{1,0:T(8,128)S(1)} %pad_maximum_fusion.so_ref), channel_id=1, source_target_pairs={{0,2},{2,4},{4,6},{6,8},{8,10},{10,12},{12,14},{1,3},{3,5},{5,7},{... | collective-permute-start | bytes 479240 | tf_op jit(solution)/shard_map/ppermute | solution.py:237
  93.6 4.6 %collective-permute-start.7 = (f32[312,128]{1,0:T(8,128)S(1)}, f32[312,128]{1,0:T(8,128)S(1)}, u32[]{:S(2)}, u32[]{:S(2)}) collective-permute-start(f32[312,128]{1,0:T(8,128)S(1)} %pad_maximum_fusion.so_ref), channel_id=1, source_target_pairs={{0,1},{1,0},{2,3},{3,2},{4,5},{5,4},{6,7},{7,6},{8,9},{9,8},{10,11... | collective-permute-start | bytes 479240 | tf_op jit(solution)/shard_map/ppermute | solution.py:238
  98.2 0.0 collective-permute-done.5.sn_ref
  98.2 1.9 %collective-permute-start.8 = (f32[312,128]{1,0:T(8,128)S(1)}, f32[312,128]{1,0:T(8,128)S(1)}, u32[]{:S(2)}, u32[]{:S(2)}) collective-permute-start(f32[312,128]{1,0:T(8,128)S(1)} %collective-permute-done.5.sn_ref), channel_id=1, source_target_pairs={{0,1},{1,0},{2,3},{3,2},{4,5},{5,4},{6,7},{7,6},{8,9},{9,8},{10,11... | collective-permute-start | bytes 479240 | tf_op jit(solution)/shard_map/ppermute | solution.py:238
  100.1 0.0 collective-permute-done.4.sp_ref
  100.1 2.4 %collective-permute-start.6 = (f32[312,128]{1,0:T(8,128)S(1)}, f32[312,128]{1,0:T(8,128)S(1)}, u32[]{:S(2)}, u32[]{:S(2)}) collective-permute-start(f32[312,128]{1,0:T(8,128)S(1)} %collective-permute-done.4.sp_ref), channel_id=1, source_target_pairs={{0,1},{1,0},{2,3},{3,2},{4,5},{5,4},{6,7},{7,6},{8,9},{9,8},{10,11... | collective-permute-start | bytes 479240 | tf_op jit(solution)/shard_map/ppermute | solution.py:238
  102.6 0.0 collective-permute-done.7.to_ref
  102.6 0.0 collective-permute-done.8.tn_ref
  102.6 1.0 collective-permute-done.6.tp_ref
  103.6 0.0 collective-permute-done.1
  103.6 0.0 collective-permute-done
  103.6 41.6 %shard_map.56 = f32[8,96,128]{2,1,0:T(8,128)S(1)} custom-call(s32[1]{0:T(128)} %bitcast.core_ref, f32[1152,128]{1,0:T(8,128)S(1)} %bitcast.17, f32[1152,128]{1,0:T(8,128)S(1)} %bitcast.14, f32[1152,128]{1,0:T(8,128)S(1)} %bitcast.16, f32[312,128]{1,0:T(8,128)S(1)} %collective-permute-done.4.sp_ref, f32[312,128]{1,0:T(8,128)S(1)} %pad_maximum_fusion.so_ref, ...), custom_call_target="tpu_custom_call" | custom-call | tf_op jit(solution)/shard_map/pallas_call | solution.py:243
  145.2 0.0 copy-start.2
  145.2 13.2 %all_to_all.16 = f32[8,96,128]{2,1,0:T(8,128)S(1)} all-to-all(f32[8,96,128]{2,1,0:T(8,128)S(1)} %shard_map.56), channel_id=1, replica_groups=mesh['y'=4,'zh'=2,'x'=4,'zl'=8,'c'=2] {'x','c'}, dimensions={0} | all-to-all | bytes 786432 | tf_op jit(solution)/shard_map/all_to_all | solution.py:257
  158.4 0.0 copy-done.2
  158.4 1.3 shard_map.57
  (2 shorter events, 0.0 us)
Async XLA Ops:
  0.0 0.7 copy-start.4
  0.7 1.0 copy-start
  1.7 0.9 copy-start.1
  2.5 0.8 copy-start.3
  48.7 22.5 %all-to-all-start.1 = ((f32[4,48,128]{2,1,0:T(8,128)}), f32[4,48,128]{2,1,0:T(8,128)S(1)}, u32[]{:S(2)}, u32[]{:S(2)}) async-start(f32[4,48,128]{2,1,0:T(8,128)} %get-tuple-element.9), calls=%async_computation.1 | async-start | bytes 196608 | tf_op jit(solution)/shard_map/all_to_all | solution.py:233
  52.7 50.9 %collective-permute-start.1 = (f32[16,72,128]{2,1,0:T(8,128)S(1)}, f32[16,72,128]{2,1,0:T(8,128)S(1)}, u32[]{:S(2)}, u32[]{:S(2)}) collective-permute-start(f32[16,72,128]{2,1,0:T(8,128)S(1)} %all_to_all.15), channel_id=1, source_target_pairs={{2,0},{4,2},{6,4},{8,6},{10,8},{12,10},{14,12},{3,1},{5,3},{7,5},{... | collective-permute-start | bytes 1769480 | tf_op jit(solution)/shard_map/ppermute | solution.py:241
  54.0 49.6 %collective-permute-start = (f32[16,72,128]{2,1,0:T(8,128)S(1)}, f32[16,72,128]{2,1,0:T(8,128)S(1)}, u32[]{:S(2)}, u32[]{:S(2)}) collective-permute-start(f32[16,72,128]{2,1,0:T(8,128)S(1)} %all_to_all.15), channel_id=1, source_target_pairs={{0,2},{2,4},{4,6},{6,8},{8,10},{10,12},{12,14},{1,3},{3,5},{5,7},{... | collective-permute-start | bytes 1769480 | tf_op jit(solution)/shard_map/ppermute | solution.py:241
  71.2 16.1 %collective-permute-start.2 = (f32[48,128]{1,0:T(8,128)S(1)}, f32[48,128]{1,0:T(8,128)S(1)}, u32[]{:S(2)}, u32[]{:S(2)}) collective-permute-start(f32[48,128]{1,0:T(8,128)S(1)} %get-tuple-element.11), channel_id=1, source_target_pairs={{0,64},{64,128},{128,192},{192,256},{256,320},{320,384},{384,448},... | collective-permute-start | bytes 73736 | tf_op jit(solution)/shard_map/ppermute | solution.py:234
  73.5 14.8 %collective-permute-start.3 = (f32[48,128]{1,0:T(8,128)S(1)}, f32[48,128]{1,0:T(8,128)S(1)}, u32[]{:S(2)}, u32[]{:S(2)}) collective-permute-start(f32[48,128]{1,0:T(8,128)S(1)} %get-tuple-element.12), channel_id=1, source_target_pairs={{64,0},{128,64},{192,128},{256,192},{320,256},{384,320},{448,384},... | collective-permute-start | bytes 73736 | tf_op jit(solution)/shard_map/ppermute | solution.py:235
  88.3 9.9 %collective-permute-start.5 = (f32[312,128]{1,0:T(8,128)S(1)}, f32[312,128]{1,0:T(8,128)S(1)}, u32[]{:S(2)}, u32[]{:S(2)}) collective-permute-start(f32[312,128]{1,0:T(8,128)S(1)} %pad_maximum_fusion.so_ref), channel_id=1, source_target_pairs={{2,0},{4,2},{6,4},{8,6},{10,8},{12,10},{14,12},{3,1},{5,3},{7,5},{... | collective-permute-start | bytes 479240 | tf_op jit(solution)/shard_map/ppermute | solution.py:237
  89.6 10.5 %collective-permute-start.4 = (f32[312,128]{1,0:T(8,128)S(1)}, f32[312,128]{1,0:T(8,128)S(1)}, u32[]{:S(2)}, u32[]{:S(2)}) collective-permute-start(f32[312,128]{1,0:T(8,128)S(1)} %pad_maximum_fusion.so_ref), channel_id=1, source_target_pairs={{0,2},{2,4},{4,6},{6,8},{8,10},{10,12},{12,14},{1,3},{3,5},{5,7},{... | collective-permute-start | bytes 479240 | tf_op jit(solution)/shard_map/ppermute | solution.py:237
  93.6 9.0 %collective-permute-start.7 = (f32[312,128]{1,0:T(8,128)S(1)}, f32[312,128]{1,0:T(8,128)S(1)}, u32[]{:S(2)}, u32[]{:S(2)}) collective-permute-start(f32[312,128]{1,0:T(8,128)S(1)} %pad_maximum_fusion.so_ref), channel_id=1, source_target_pairs={{0,1},{1,0},{2,3},{3,2},{4,5},{5,4},{6,7},{7,6},{8,9},{9,8},{10,11... | collective-permute-start | bytes 479240 | tf_op jit(solution)/shard_map/ppermute | solution.py:238
  98.2 4.4 %collective-permute-start.8 = (f32[312,128]{1,0:T(8,128)S(1)}, f32[312,128]{1,0:T(8,128)S(1)}, u32[]{:S(2)}, u32[]{:S(2)}) collective-permute-start(f32[312,128]{1,0:T(8,128)S(1)} %collective-permute-done.5.sn_ref), channel_id=1, source_target_pairs={{0,1},{1,0},{2,3},{3,2},{4,5},{5,4},{6,7},{7,6},{8,9},{9,8},{10,11... | collective-permute-start | bytes 479240 | tf_op jit(solution)/shard_map/ppermute | solution.py:238
  100.1 3.4 %collective-permute-start.6 = (f32[312,128]{1,0:T(8,128)S(1)}, f32[312,128]{1,0:T(8,128)S(1)}, u32[]{:S(2)}, u32[]{:S(2)}) collective-permute-start(f32[312,128]{1,0:T(8,128)S(1)} %collective-permute-done.4.sp_ref), channel_id=1, source_target_pairs={{0,1},{1,0},{2,3},{3,2},{4,5},{5,4},{6,7},{7,6},{8,9},{9,8},{10,11... | collective-permute-start | bytes 479240 | tf_op jit(solution)/shard_map/ppermute | solution.py:238
  145.2 13.2 %copy-start.2 = (f32[128,128]{1,0:T(8,128)S(1)}, f32[128,128]{1,0:T(8,128)}, u32[]{:S(2)}) copy-start(f32[128,128]{1,0:T(8,128)} %coef_ref.1) | copy-start | bytes 196612

commit v2 on v1

--- a/solution.py
+++ b/solution.py
@@ -14,6 +14,8 @@
 TALL = STRIP + 2 * HALO
 PEERS = 16
 COEFS = 15
+PAIRS = 8
+GROUP = 8
 f32 = jnp.float32
 
 
@@ -69,49 +71,52 @@
 
 def march_kernel(
     core_ref, prev_ref, own_ref, next_ref, sp_ref, so_ref, sn_ref, tp_ref, to_ref, tn_ref,
-    out_ref, state, middle, base, wet, coef,
+    out_ref, state, middle, base, wet, coef, turn,
 ):
     lane = lax.broadcasted_iota(jnp.int32, (8, LANES), 1)
-    for z, ref in enumerate((prev_ref, own_ref, next_ref)):
-        for c in range(2):
-            for f in range(3):
-                for r in range(8):
+    def place(p, _):
+        for z, ref in enumerate((prev_ref, own_ref, next_ref)):
+            for c in range(2):
+                for f in range(3):
                     for v in range(3):
-                        state[f, z * 16 + c * 8 + r, v] = ref[pl.ds(c * 72 + v * 24 + f * 8 + r, 8, stride=144), :]
+                        at = pl.multiple_of((2 * p + c) * 72 + v * 24 + f * 8, 8)
+                        state[f, p, v, z * 16 + c * 8 : z * 16 + c * 8 + 8, :] = ref[pl.ds(at, 8), :]
+
+    lax.fori_loop(0, PAIRS, place, None)
     core = core_ref[0]
-    for turn, refs in enumerate(((sp_ref, so_ref, sn_ref), (tp_ref, to_ref, tn_ref))):
-        place = core if turn == 0 else 1 - core
+    strips = []
+    for which, refs in enumerate(((sp_ref, so_ref, sn_ref), (tp_ref, to_ref, tn_ref))):
         for z, ref in enumerate(refs):
-            top = pl.multiple_of(place * 8 + z * 16, 8)
-            for v in range(3):
-                wet[v, pl.ds(top, 8), :] = ref[288 + v * 8 : 288 + v * 8 + 8, :] * 0.25
-            for high in range(2):
-                for f in range(3):
-                    at = (high * 3 + f) * 8
-                    quads = [ref[x * 48 + at : x * 48 + at + 8, :] for x in range(4)]
-                    lefts = ref[192 + at : 192 + at + 8, :]
-                    rights = ref[240 + at : 240 + at + 8, :]
-                    for low in range(4):
-                        out = pltpu.roll(quads[0], (128 - 32 * low) % 128, 1) if low else quads[0]
-                        for x in range(1, 4):
-                            turned = pltpu.roll(quads[x], 32 * (x - low) % 128, 1) if x != low else quads[x]
-                            out = jnp.where(lane >= 32 * x, turned, out)
-                        left = pltpu.roll(lefts, (96 - 32 * low) % 128, 1)
-                        left_turned = pltpu.roll(lefts, (160 - 32 * low) % 128, 1)
-                        right = pltpu.roll(rights, (128 - 32 * low) % 128, 1)
-                        right_turned = pltpu.roll(rights, (192 - 32 * low) % 128, 1)
-                        halo = edges(left, right, left_turned, right_turned, lane)
-                        rows = pl.ds(top + 8, 8)
-                        base[high * 4 + low, f, 0, rows, :] = out
-                        base[high * 4 + low, f, 1, rows, :] = pltpu.roll(out, 64, 1)
-                        base[high * 4 + low, f, 2, rows, :] = halo
+            strips.append((ref, pl.multiple_of((core if which == 0 else 1 - core) * 8 + z * 16, 8)))
+    for ref, top in strips:
+        for v in range(3):
+            wet[v, pl.ds(top, 8), :] = ref[288 + v * 8 : 288 + v * 8 + 8, :] * 0.25
+
+    def unpack(part, _):
+        high, f = part // 3, part % 3
+        for ref, top in strips:
+            quads = [ref[pl.ds(pl.multiple_of(x * 48 + part * 8, 8), 8), :] for x in range(6)]
+            for low in range(4):
+                out = pltpu.roll(quads[0], (128 - 32 * low) % 128, 1) if low else quads[0]
+                for x in range(1, 4):
+                    turned = pltpu.roll(quads[x], 32 * (x - low) % 128, 1) if x != low else quads[x]
+                    out = jnp.where(lane >= 32 * x, turned, out)
+                left = pltpu.roll(quads[4], (96 - 32 * low) % 128, 1)
+                right = pltpu.roll(quads[5], (128 - 32 * low) % 128, 1)
+                halo = edges(left, right, pltpu.roll(left, 64, 1), pltpu.roll(right, 64, 1), lane)
+                rows = pl.ds(top + 8, 8)
+                base[high * 4 + low, f, 0, rows, :] = out
+                base[high * 4 + low, f, 1, rows, :] = pltpu.roll(out, 64, 1)
+                base[high * 4 + low, f, 2, rows, :] = halo
+
+    lax.fori_loop(0, 6, unpack, None)
 
     def prepare(step, tile):
-        top = tile * 8
-        w = [wet[v, top : top + 8, :] for v in range(3)]
+        top = pl.multiple_of(tile * 8, 8)
+        w = [wet[v, pl.ds(top, 8), :] for v in range(3)]
 
         def rows(f, shift):
-            return [base[step, f, v, top + 8 + shift : top + 16 + shift, :] for v in range(3)]
+            return [base[step, f, v, pl.ds(top + 8 + shift, 8), :] for v in range(3)]
 
         depth = [x + 1.0 for x in rows(0, 0)]
         b, c = rows(1, 0), rows(2, 0)
@@ -131,70 +136,78 @@
                 q,
             )
             for k, part in enumerate(parts):
-                coef[k, v, top : top + 8, :] = part
-
-    def rates(ref, r):
-        h, u, m = ([ref[f, r, v] for v in range(3)] for f in range(3))
-        hn, un, mn = ([ref[f, r + 1, v] for v in range(3)] for f in range(3))
-        hs, us, ms = ([ref[f, r - 1, v] for v in range(3)] for f in range(3))
-        hp, hm = from_right(h, lane), from_left(h, lane)
-        up, um = from_right(u, lane), from_left(u, lane)
-        mp, mm = from_right(m, lane), from_left(m, lane)
-        fields = ([], [], [])
+                coef[k, v, pl.ds(top, 8), :] = part
+
+    def changes(ref, top, pairs):
+        rows, north, south = (pl.ds(top + k, 8) for k in (0, 1, -1))
+        moved = []
+        for p in pairs:
+            h, u, m = ([ref[f, p, v, rows, :] for v in range(3)] for f in range(3))
+            moved.append(
+                (h, u, m, from_right(h, lane), from_left(h, lane), from_right(u, lane), from_left(u, lane))
+                + ([a - b for a, b in zip(from_right(m, lane), from_left(m, lane))],)
+            )
+        out = [([], [], []) for _ in pairs]
         for v in range(3):
-            k = [coef[i, v, pl.ds(r, 1), :] for i in range(COEFS)]
-            fields[0].append(
-                ((k[0] * up[v] + k[1] * um[v]) + (k[2] * hp[v] + k[3] * hm[v]))
-                + ((k[4] * mn[v] + k[5] * ms[v]) + (k[6] * hn[v] + k[7] * hs[v]))
-            )
-            fields[1].append(
-                (k[8] * (up[v] - um[v]) + k[9] * (un[v] - us[v]))
-                + ((k[10] * u[v] + k[11] * m[v]) - k[14] * (hp[v] - hm[v]))
-            )
-            fields[2].append(
-                (k[8] * (mp[v] - mm[v]) + k[9] * (mn[v] - ms[v]))
-                + ((k[12] * u[v] + k[13] * m[v]) - k[14] * (hn[v] - hs[v]))
-            )
-        return fields
-
-    for step in range(STEPS):
+            k = [coef[i, v, rows, :] for i in range(COEFS)]
+            for p, (h, u, m, hp, hm, up, um, md), fields in zip(pairs, moved, out):
+                hn, un, mn = (ref[f, p, v, north, :] for f in range(3))
+                hs, us, ms = (ref[f, p, v, south, :] for f in range(3))
+                fields[0].append(
+                    ((k[0] * up[v] + k[1] * um[v]) + (k[2] * hp[v] + k[3] * hm[v]))
+                    + ((k[4] * mn + k[5] * ms) + (k[6] * hn + k[7] * hs))
+                )
+                fields[1].append(
+                    (k[8] * (up[v] - um[v]) + k[9] * (un - us)) + ((k[10] * u[v] + k[11] * m[v]) - k[14] * (hp[v] - hm[v]))
+                )
+                fields[2].append((k[8] * md[v] + k[9] * (mn - ms)) + ((k[12] * u[v] + k[13] * m[v]) - k[14] * (hn - hs)))
+        return out
+
+    def sweep(low, high, body):
+        def window(i, _):
+            lax.fori_loop(0, PAIRS // GROUP, lambda g, _: body(low + 8 * i, [g * GROUP + k for k in range(GROUP)]), None)
+
+        lax.fori_loop(0, (high - low + 7) // 8, window, None)
+
+    def first(top, pairs):
+        for p, change in zip(pairs, changes(state, top, pairs)):
+            for f in range(3):
+                for v in range(3):
+                    middle[f, p, v, pl.ds(top, 8), :] = state[f, p, v, pl.ds(top, 8), :] + change[f][v]
+
+    def second(top, pairs):
+        for p, change in zip(pairs, changes(middle, top, pairs)):
+            for f in range(3):
+                for v in range(3):
+                    at = (f, p, v, pl.ds(top, 8), slice(None))
+                    state[at] = 0.5 * ((state[at] + middle[at]) + change[f][v])
+
+    def advance(step, _):
         low, high = 2 * step + 1, TALL - 2 * step - 1
-        for tile in range(low // 8, (high + 7) // 8):
-            prepare(step, tile)
-
-        def first(i, _, low=low):
-            for r in (low + 2 * i, low + 2 * i + 1):
-                change = rates(state, r)
-                for f in range(3):
-                    for v in range(3):
-                        middle[f, r, v] = state[f, r, v] + change[f][v]
-            return _
-
-        lax.fori_loop(0, (high - low) // 2, first, 0)
-
-        def second(i, _, low=low + 1):
-            for r in (low + 2 * i, low + 2 * i + 1):
-                change = rates(middle, r)
-                for f in range(3):
-                    for v in range(3):
-                        state[f, r, v] = 0.5 * ((state[f, r, v] + middle[f, r, v]) + change[f][v])
-            return _
-
-        lax.fori_loop(0, (high - low - 2) // 2, second, 0)
-
-    for c in range(2):
-        for f in range(3):
+        lax.fori_loop(low // 8, (high + 7) // 8, lambda tile, _: prepare(step, tile), None)
+        sweep(low, high, first)
+        sweep(low + 1, high - 1, second)
+
+    lax.fori_loop(0, STEPS, advance, None)
+
+    def deliver(f, _):
+        for c in range(2):
+            for v in range(2):
+                for p in range(PAIRS):
+                    turn[c, v, pl.ds(p, 8, stride=PAIRS), :] = state[f, p, v, HALO + c * 8 : HALO + c * 8 + 8, :]
+        for c in range(2):
             for high in range(2):
                 for v in range(2):
-                    lines = [state[f, HALO + c * 8 + high * 4 + low, v] for low in range(4)]
+                    lines = [turn[c, v, (high * 4 + low) * 8 : (high * 4 + low) * 8 + 8, :] for low in range(4)]
                     for x in range(4):
                         at = (x + 2 * v) % 4
                         out = pltpu.roll(lines[0], (128 - 32 * at) % 128, 1) if at else lines[0]
                         for low in range(1, 4):
                             turned = pltpu.roll(lines[low], 32 * (low - at) % 128, 1) if low != at else lines[low]
                             out = jnp.where(lane >= 32 * low, turned, out)
-                        row = ((f * 2 + high) * 2 + v) * 8
-                        out_ref[x * 2 + c, row : row + 8, :] = out
+                        out_ref[x * 2 + c, pl.ds(pl.multiple_of(f * 32 + (high * 2 + v) * 8, 8), 8), :] = out
+
+    lax.fori_loop(0, 3, deliver, None)
 
 
 def mix_kernel(coef_ref, cells_ref, out_ref, mixing):
@@ -228,17 +241,20 @@
         compiler_params=pltpu.CompilerParams(vmem_limit_bytes=16 * 2**20),
     )(block.reshape(1).astype(jnp.int32), owner_order, tangents, checkpoints, land_mask)
 
-    up = [(i, i + 1) for i in range(7)]
-    down = [(i + 1, i) for i in range(7)]
+    own = lax.all_to_all(send, ("y", "zh", "c"), 0, 0, tiled=True)
     flows = lax.all_to_all(flow, "x", 0, 0, tiled=True)
     left = lax.ppermute(flows[3], ("y", "zh"), [(i, (i + 1) % 8) for i in range(8)])
     right = lax.ppermute(flows[0], ("y", "zh"), [((i + 1) % 8, i) for i in range(8)])
+    own, flows, left, right = lax.optimization_barrier((own, flows, left, right))
+
+    def near(cells, chips, cross):
+        pairs = [(z * 2 + c, (z + chips) * 2 + c ^ cross) for z in range(8) if 0 <= z + chips < 8 for c in range(2)]
+        return lax.ppermute(cells, ("zl", "c"), pairs)
+
     strip = jnp.concatenate([flows.reshape(192, LANES), left, right, wet], axis=0)
-    strips = [lax.ppermute(strip, "zl", up), strip, lax.ppermute(strip, "zl", down)]
-    others = [lax.ppermute(x, "c", [(0, 1), (1, 0)]) for x in strips]
-
-    own = lax.all_to_all(send, ("y", "zh", "c"), 0, 0, tiled=True)
-    parts = [lax.ppermute(own, "zl", up), own, lax.ppermute(own, "zl", down)]
+    parts = [near(own, 1, 0), own, near(own, -1, 0)]
+    strips = [near(strip, 1, 0), strip, near(strip, -1, 0)]
+    others = [near(strip, 1, 1), near(strip, 0, 1), near(strip, -1, 1)]
     parts = [x.reshape(PEERS * 72, LANES) for x in parts]
     out = pl.pallas_call(
         march_kernel,
@@ -246,11 +262,12 @@
         in_specs=[SMEM] + [VMEM] * 9,
         out_specs=VMEM,
         scratch_shapes=[
-            pltpu.VMEM((3, TALL, 3, 8, LANES), f32),
-            pltpu.VMEM((3, TALL, 3, 8, LANES), f32),
+            pltpu.VMEM((3, PAIRS, 3, TALL + 8, LANES), f32),
+            pltpu.VMEM((3, PAIRS, 3, TALL + 8, LANES), f32),
             pltpu.VMEM((STEPS, 3, 3, TALL + 16, LANES), f32),
             pltpu.VMEM((3, TALL, LANES), f32),
-            pltpu.VMEM((COEFS, 3, TALL, LANES), f32),
+            pltpu.VMEM((COEFS, 3, TALL + 8, LANES), f32),
+            pltpu.VMEM((2, 2, 64, LANES), f32),
         ],
         compiler_params=pltpu.CompilerParams(vmem_limit_bytes=32 * 2**20),
     )(core.reshape(1).astype(jnp.int32), *parts, *strips, *others)

time: 160 us -> 146 us (0.912)
  blocking collectives: 57.2 us -> 20.1 us
  waiting for transfers between devices: 1.93 us -> 33.7 us
  Pallas kernels: 44.2 us -> 30.9 us
  starting transfers between devices: 52.8 us -> 57.1 us
    all_to_all x1, blocking collectives: 44.1 us -> 9.28 us  [on_device(): flows = lax.all_to_all(flow, 'x', 0, 0, tiled=True)]
    all_to_all x1, starting transfers between devices: 4.01 us -> 19.8 us  [on_device(): own = lax.all_to_all(send, ('y', 'zh', 'c'), 0, 0, tiled=True)]
    ppermute x1, waiting for transfers between devices: 0.01 us -> 14.1 us  [on_device(): lax.ppermute(flows[3], ('y', 'zh'), [(i, (i + 1) % 8) for i in range(8)])]
    pallas_call x1, Pallas kernels: 41.6 us -> 28.1 us  [on_device(): pl.pallas_call(march_kernel, out_shape=jax.ShapeDtypeStruct((8, 96, LANES...]
    ppermute x7, starting transfers between devices: 32.7 us -> 21.2 us  [near(): return lax.ppermute(cells, ('zl', 'c'), pairs)]
    ppermute x7, waiting for transfers between devices: 0.99 us -> 9.96 us  [near(): return lax.ppermute(cells, ('zl', 'c'), pairs)]
    ppermute x1, waiting for transfers between devices: 0.93 us -> 9.68 us  [on_device(): lax.ppermute(flows[0], ('y', 'zh'), [((i + 1) % 8, i) for i in range(8)])]
    all_to_all x1, blocking collectives: 13.2 us -> 10.8 us  [on_device(): cells = lax.all_to_all(out, ('x', 'c'), 0, 0, tiled=True)]
  transfers between devices with their start and end apart: 10 -> 10, of which waited for: 2 -> 5; matrix products, arithmetic and copies ran while one was open for 0% -> 0% of each run, Pallas kernels for 0% -> 0%
where the time goes in v2:
time: 146 us; the launch traced here: 145 us
  starting transfers between devices  57.1 us (39%)
  waiting for transfers between devices  33.7 us (23%)
  Pallas kernels  30.9 us (21%)
  blocking collectives  20.1 us (14%)
  local copies, waits for them, and re-layouts  3.31 us (2%)
    pallas_call x1, Pallas kernels, on_device(): pl.pallas_call(march_kernel, out_shape=jax.ShapeDtypeStruct((8, 96, LANES...  28.1 us
    ppermute x7, starting transfers between devices, near(): return lax.ppermute(cells, ('zl', 'c'), pairs)  21.2 us
    all_to_all x1, starting transfers between devices, on_device(): own = lax.all_to_all(send, ('y', 'zh', 'c'), 0, 0, tiled=True)  19.8 us
    ppermute x1, starting transfers between devices, on_device(): lax.ppermute(flows[0], ('y', 'zh'), [((i + 1) % 8, i) for i in range(8)])  14.1 us
    ppermute x1, waiting for transfers between devices, on_device(): lax.ppermute(flows[3], ('y', 'zh'), [(i, (i + 1) % 8) for i in range(8)])  14.1 us
    all_to_all x1, blocking collectives, on_device(): cells = lax.all_to_all(out, ('x', 'c'), 0, 0, tiled=True)  10.8 us
    ppermute x7, waiting for transfers between devices, near(): return lax.ppermute(cells, ('zl', 'c'), pairs)  9.96 us
    ppermute x1, waiting for transfers between devices, on_device(): lax.ppermute(flows[0], ('y', 'zh'), [((i + 1) % 8, i) for i in range(8)])  9.68 us
  transfers between devices with their start and end apart: 10, of which 5 were waited for; matrix products, arithmetic and copies ran while one was open for 0% of the time, Pallas kernels for 0%

profile of v2, /device:TPU:1, one launch (start us, length us, event | category | flops | bytes accessed | tf_op | source)
XLA Modules:
  0.0 145.3 jit_solution(13069181699128840335)
XLA Ops:
  0.0 0.0 copy-start.4
  0.0 0.7 copy-done.4
  0.7 0.0 copy-start
  0.7 1.0 copy-done
  1.7 0.0 copy-start.1
  1.7 0.9 copy-done.1
  2.5 0.0 copy-start.3
  2.5 0.8 copy-done.3
  3.3 1.5 %shard_map.55 = (f32[16,72,128]{2,1,0:T(8,128)}, f32[4,48,128]{2,1,0:T(8,128)S(1)}, f32[24,128]{1,0:T(8,128)S(1)}) custom-call(s32[1]{0:T(128)} %bitcast.1.block_ref, s32[8]{0:T(128)S(1)} %copy-done.4, f32[4,3,8,1024]{3,2,1,0:T(8,128)S(1)} %copy-done, f32[8,3,8,32]{3,2,1,0:T(8,128)S(1)} %copy-done.1, s32[8,1024]{1,0:T(8,128)S(1)} %copy-done.3), custom_call_target="tpu_custom_call" | custom-call | tf_op jit(solution)/shard_map/pallas_call | solution.py:232
  4.8 9.3 %all_to_all.15 = f32[4,48,128]{2,1,0:T(8,128)S(1)} all-to-all(f32[4,48,128]{2,1,0:T(8,128)S(1)} %get-tuple-element.13), channel_id=1, replica_groups=mesh['y'=4,'zh'=2,'x'=4,'zl'=8,'c'=2] {'x'}, dimensions={0} | all-to-all | bytes 196608 | tf_op jit(solution)/shard_map/all_to_all | solution.py:245
  14.1 19.8 %all-to-all-start = ((f32[16,72,128]{2,1,0:T(8,128)}), f32[16,72,128]{2,1,0:T(8,128)S(1)}, u32[]{:S(2)}, u32[]{:S(2)}) async-start(f32[16,72,128]{2,1,0:T(8,128)} %get-tuple-element.12), calls=%async_computation | async-start | bytes 1179648 | tf_op jit(solution)/shard_map/all_to_all | solution.py:244
  33.9 14.1 %collective-permute-start.1 = (f32[48,128]{1,0:T(8,128)S(1)}, f32[48,128]{1,0:T(8,128)S(1)}, u32[]{:S(2)}, u32[]{:S(2)}) collective-permute-start(f32[48,128]{1,0:T(8,128)S(1)} %get-tuple-element.19), channel_id=1, source_target_pairs={{64,0},{128,64},{192,128},{256,192},{320,256},{384,320},{448,384},... | collective-permute-start | bytes 73736 | tf_op jit(solution)/shard_map/ppermute | solution.py:247
  48.1 1.9 %collective-permute-start = (f32[48,128]{1,0:T(8,128)S(1)}, f32[48,128]{1,0:T(8,128)S(1)}, u32[]{:S(2)}, u32[]{:S(2)}) collective-permute-start(f32[48,128]{1,0:T(8,128)S(1)} %get-tuple-element.20), channel_id=1, source_target_pairs={{0,64},{64,128},{128,192},{192,256},{256,320},{320,384},{384,448},... | collective-permute-start | bytes 73736 | tf_op jit(solution)/shard_map/ppermute | solution.py:246
  50.0 9.7 %collective-permute-done.1 = f32[48,128]{1,0:T(8,128)S(1)} collective-permute-done((f32[48,128]{1,0:T(8,128)S(1)}, f32[48,128]{1,0:T(8,128)S(1)}, u32[]{:S(2)}, u32[]{:S(2)}) %collective-permute-start.1) | collective-permute-done | bytes 24608 | tf_op jit(solution)/shard_map/ppermute | solution.py:247
  59.7 14.1 %collective-permute-done = f32[48,128]{1,0:T(8,128)S(1)} collective-permute-done((f32[48,128]{1,0:T(8,128)S(1)}, f32[48,128]{1,0:T(8,128)S(1)}, u32[]{:S(2)}, u32[]{:S(2)}) %collective-permute-start) | collective-permute-done | bytes 24608 | tf_op jit(solution)/shard_map/ppermute | solution.py:246
  73.8 0.0 all-to-all-done
  73.8 1.3 collective-permute-start.3
  75.0 5.5 %collective-permute-start.2 = (f32[16,72,128]{2,1,0:T(8,128)S(1)}, f32[16,72,128]{2,1,0:T(8,128)S(1)}, u32[]{:S(2)}, u32[]{:S(2)}) collective-permute-start(f32[16,72,128]{2,1,0:T(8,128)S(1)} %all-to-all-done), channel_id=1, source_target_pairs={{0,2},{1,3},{2,4},{3,5},{4,6},{5,7},{6,8},{7,9},{8,10},{9,11},{10,... | collective-permute-start | bytes 1769480 | tf_op jit(solution)/shard_map/ppermute | solution.py:252
  80.6 1.3 collective-permute-start.8
  81.9 3.2 %collective-permute-start.7 = (f32[312,128]{1,0:T(8,128)S(1)}, f32[312,128]{1,0:T(8,128)S(1)}, u32[]{:S(2)}, u32[]{:S(2)}) collective-permute-start(f32[312,128]{1,0:T(8,128)S(1)} %pad_maximum_fusion.so_ref), channel_id=1, source_target_pairs={{0,1},{1,0},{2,3},{3,2},{4,5},{5,4},{6,7},{7,6},{8,9},{9,8},{10,11... | collective-permute-start | bytes 479240 | tf_op jit(solution)/shard_map/ppermute | solution.py:252
  85.1 4.3 %collective-permute-start.6 = (f32[312,128]{1,0:T(8,128)S(1)}, f32[312,128]{1,0:T(8,128)S(1)}, u32[]{:S(2)}, u32[]{:S(2)}) collective-permute-start(f32[312,128]{1,0:T(8,128)S(1)} %pad_maximum_fusion.so_ref), channel_id=1, source_target_pairs={{0,3},{1,2},{2,5},{3,4},{4,7},{5,6},{6,9},{7,8},{8,11},{9,10},{10,... | collective-permute-start | bytes 479240 | tf_op jit(solution)/shard_map/ppermute | solution.py:252
  89.4 6.2 %collective-permute-done.8.tn_ref = f32[312,128]{1,0:T(8,128)S(1)} collective-permute-done((f32[312,128]{1,0:T(8,128)S(1)}, f32[312,128]{1,0:T(8,128)S(1)}, u32[]{:S(2)}, u32[]{:S(2)}) %collective-permute-start.8) | collective-permute-done | bytes 159776 | tf_op jit(solution)/shard_map/ppermute | solution.py:252
  95.6 1.3 collective-permute-start.5
  96.9 0.0 collective-permute-done.7.to_ref
  96.9 4.3 %collective-permute-start.4 = (f32[312,128]{1,0:T(8,128)S(1)}, f32[312,128]{1,0:T(8,128)S(1)}, u32[]{:S(2)}, u32[]{:S(2)}) collective-permute-start(f32[312,128]{1,0:T(8,128)S(1)} %pad_maximum_fusion.so_ref), channel_id=1, source_target_pairs={{0,2},{1,3},{2,4},{3,5},{4,6},{5,7},{6,8},{7,9},{8,10},{9,11},{10,... | collective-permute-start | bytes 479240 | tf_op jit(solution)/shard_map/ppermute | solution.py:252
  101.2 0.0 collective-permute-done.6.tp_ref
  101.2 2.0 %collective-permute-done.5.sn_ref = f32[312,128]{1,0:T(8,128)S(1)} collective-permute-done((f32[312,128]{1,0:T(8,128)S(1)}, f32[312,128]{1,0:T(8,128)S(1)}, u32[]{:S(2)}, u32[]{:S(2)}) %collective-permute-start.5) | collective-permute-done | bytes 159776 | tf_op jit(solution)/shard_map/ppermute | solution.py:252
  103.2 1.8 %collective-permute-done.4.sp_ref = f32[312,128]{1,0:T(8,128)S(1)} collective-permute-done((f32[312,128]{1,0:T(8,128)S(1)}, f32[312,128]{1,0:T(8,128)S(1)}, u32[]{:S(2)}, u32[]{:S(2)}) %collective-permute-start.4) | collective-permute-done | bytes 159776 | tf_op jit(solution)/shard_map/ppermute | solution.py:252
  105.0 0.0 collective-permute-done.3
  105.0 0.0 collective-permute-done.2
  105.0 28.1 %shard_map.56 = f32[8,96,128]{2,1,0:T(8,128)S(1)} custom-call(s32[1]{0:T(128)} %bitcast.core_ref, f32[1152,128]{1,0:T(8,128)S(1)} %bitcast.17, f32[1152,128]{1,0:T(8,128)S(1)} %bitcast.14, f32[1152,128]{1,0:T(8,128)S(1)} %bitcast.16, f32[312,128]{1,0:T(8,128)S(1)} %collective-permute-done.4.sp_ref, f32[312,128]{1,0:T(8,128)S(1)} %pad_maximum_fusion.so_ref, ...), custom_call_target="tpu_custom_call" | custom-call | tf_op jit(solution)/shard_map/pallas_call | solution.py:259
  133.2 0.0 copy-start.2
  133.2 10.8 %all_to_all.16 = f32[8,96,128]{2,1,0:T(8,128)S(1)} all-to-all(f32[8,96,128]{2,1,0:T(8,128)S(1)} %shard_map.56), channel_id=1, replica_groups=mesh['y'=4,'zh'=2,'x'=4,'zl'=8,'c'=2] {'x','c'}, dimensions={0} | all-to-all | bytes 786432 | tf_op jit(solution)/shard_map/all_to_all | solution.py:274
  144.0 0.0 copy-done.2
  144.0 1.3 shard_map.57
  (2 shorter events, 0.0 us)
Async XLA Ops:
  0.0 0.7 copy-start.4
  0.7 1.0 copy-start
  1.7 0.9 copy-start.1
  2.5 0.8 copy-start.3
  14.1 59.7 %all-to-all-start = ((f32[16,72,128]{2,1,0:T(8,128)}), f32[16,72,128]{2,1,0:T(8,128)S(1)}, u32[]{:S(2)}, u32[]{:S(2)}) async-start(f32[16,72,128]{2,1,0:T(8,128)} %get-tuple-element.12), calls=%async_computation | async-start | bytes 1179648 | tf_op jit(solution)/shard_map/all_to_all | solution.py:244
  33.9 25.7 %collective-permute-start.1 = (f32[48,128]{1,0:T(8,128)S(1)}, f32[48,128]{1,0:T(8,128)S(1)}, u32[]{:S(2)}, u32[]{:S(2)}) collective-permute-start(f32[48,128]{1,0:T(8,128)S(1)} %get-tuple-element.19), channel_id=1, source_target_pairs={{64,0},{128,64},{192,128},{256,192},{320,256},{384,320},{448,384},... | collective-permute-start | bytes 73736 | tf_op jit(solution)/shard_map/ppermute | solution.py:247
  48.1 25.7 %collective-permute-start = (f32[48,128]{1,0:T(8,128)S(1)}, f32[48,128]{1,0:T(8,128)S(1)}, u32[]{:S(2)}, u32[]{:S(2)}) collective-permute-start(f32[48,128]{1,0:T(8,128)S(1)} %get-tuple-element.20), channel_id=1, source_target_pairs={{0,64},{64,128},{128,192},{192,256},{256,320},{320,384},{384,448},... | collective-permute-start | bytes 73736 | tf_op jit(solution)/shard_map/ppermute | solution.py:246
  73.8 31.2 %collective-permute-start.3 = (f32[16,72,128]{2,1,0:T(8,128)S(1)}, f32[16,72,128]{2,1,0:T(8,128)S(1)}, u32[]{:S(2)}, u32[]{:S(2)}) collective-permute-start(f32[16,72,128]{2,1,0:T(8,128)S(1)} %all-to-all-done), channel_id=1, source_target_pairs={{2,0},{3,1},{4,2},{5,3},{6,4},{7,5},{8,6},{9,7},{10,8},{11,9},{12,... | collective-permute-start | bytes 1769480 | tf_op jit(solution)/shard_map/ppermute | solution.py:252
  75.0 30.0 %collective-permute-start.2 = (f32[16,72,128]{2,1,0:T(8,128)S(1)}, f32[16,72,128]{2,1,0:T(8,128)S(1)}, u32[]{:S(2)}, u32[]{:S(2)}) collective-permute-start(f32[16,72,128]{2,1,0:T(8,128)S(1)} %all-to-all-done), channel_id=1, source_target_pairs={{0,2},{1,3},{2,4},{3,5},{4,6},{5,7},{6,8},{7,9},{8,10},{9,11},{10,... | collective-permute-start | bytes 1769480 | tf_op jit(solution)/shard_map/ppermute | solution.py:252
  80.6 15.0 %collective-permute-start.8 = (f32[312,128]{1,0:T(8,128)S(1)}, f32[312,128]{1,0:T(8,128)S(1)}, u32[]{:S(2)}, u32[]{:S(2)}) collective-permute-start(f32[312,128]{1,0:T(8,128)S(1)} %pad_maximum_fusion.so_ref), channel_id=1, source_target_pairs={{2,1},{3,0},{4,3},{5,2},{6,5},{7,4},{8,7},{9,6},{10,9},{11,8},{12,... | collective-permute-start | bytes 479240 | tf_op jit(solution)/shard_map/ppermute | solution.py:252
  81.9 15.0 %collective-permute-start.7 = (f32[312,128]{1,0:T(8,128)S(1)}, f32[312,128]{1,0:T(8,128)S(1)}, u32[]{:S(2)}, u32[]{:S(2)}) collective-permute-start(f32[312,128]{1,0:T(8,128)S(1)} %pad_maximum_fusion.so_ref), channel_id=1, source_target_pairs={{0,1},{1,0},{2,3},{3,2},{4,5},{5,4},{6,7},{7,6},{8,9},{9,8},{10,11... | collective-permute-start | bytes 479240 | tf_op jit(solution)/shard_map/ppermute | solution.py:252
  85.1 16.1 %collective-permute-start.6 = (f32[312,128]{1,0:T(8,128)S(1)}, f32[312,128]{1,0:T(8,128)S(1)}, u32[]{:S(2)}, u32[]{:S(2)}) collective-permute-start(f32[312,128]{1,0:T(8,128)S(1)} %pad_maximum_fusion.so_ref), channel_id=1, source_target_pairs={{0,3},{1,2},{2,5},{3,4},{4,7},{5,6},{6,9},{7,8},{8,11},{9,10},{10,... | collective-permute-start | bytes 479240 | tf_op jit(solution)/shard_map/ppermute | solution.py:252
  95.6 7.6 %collective-permute-start.5 = (f32[312,128]{1,0:T(8,128)S(1)}, f32[312,128]{1,0:T(8,128)S(1)}, u32[]{:S(2)}, u32[]{:S(2)}) collective-permute-start(f32[312,128]{1,0:T(8,128)S(1)} %pad_maximum_fusion.so_ref), channel_id=1, source_target_pairs={{2,0},{3,1},{4,2},{5,3},{6,4},{7,5},{8,6},{9,7},{10,8},{11,9},{12,... | collective-permute-start | bytes 479240 | tf_op jit(solution)/shard_map/ppermute | solution.py:252
  96.9 8.1 %collective-permute-start.4 = (f32[312,128]{1,0:T(8,128)S(1)}, f32[312,128]{1,0:T(8,128)S(1)}, u32[]{:S(2)}, u32[]{:S(2)}) collective-permute-start(f32[312,128]{1,0:T(8,128)S(1)} %pad_maximum_fusion.so_ref), channel_id=1, source_target_pairs={{0,2},{1,3},{2,4},{3,5},{4,6},{5,7},{6,8},{7,9},{8,10},{9,11},{10,... | collective-permute-start | bytes 479240 | tf_op jit(solution)/shard_map/ppermute | solution.py:252
  133.2 10.8 %copy-start.2 = (f32[128,128]{1,0:T(8,128)S(1)}, f32[128,128]{1,0:T(8,128)}, u32[]{:S(2)}) copy-start(f32[128,128]{1,0:T(8,128)} %coef_ref.1) | copy-start | bytes 196612

commit v3 on v2

--- a/solution.py
+++ b/solution.py
@@ -65,12 +65,11 @@
     for high in range(2):
         for f in range(3):
             flow = jnp.concatenate([base_ref[order_ref[high * 4 + low], f] for low in range(4)], axis=1)
-            for k in range(4):
-                flow_ref[k, (high * 3 + f) * 8 : (high * 3 + f) * 8 + 8, :] = flow
+            flow_ref[(high * 3 + f) * 8 : (high * 3 + f) * 8 + 8, :] = flow
 
 
 def march_kernel(
-    core_ref, prev_ref, own_ref, next_ref, sp_ref, so_ref, sn_ref, tp_ref, to_ref, tn_ref,
+    core_ref, prev_ref, own_ref, next_ref, sp_ref, so_ref, sn_ref,
     out_ref, state, middle, base, wet, coef, turn,
 ):
     lane = lax.broadcasted_iota(jnp.int32, (8, LANES), 1)
@@ -85,17 +84,18 @@
     lax.fori_loop(0, PAIRS, place, None)
     core = core_ref[0]
     strips = []
-    for which, refs in enumerate(((sp_ref, so_ref, sn_ref), (tp_ref, to_ref, tn_ref))):
-        for z, ref in enumerate(refs):
-            strips.append((ref, pl.multiple_of((core if which == 0 else 1 - core) * 8 + z * 16, 8)))
-    for ref, top in strips:
-        for v in range(3):
-            wet[v, pl.ds(top, 8), :] = ref[288 + v * 8 : 288 + v * 8 + 8, :] * 0.25
+    for z, ref in enumerate((sp_ref, so_ref, sn_ref)):
+        for other in range(2):
+            top = pl.multiple_of((1 - core if other else core) * 8 + z * 16, 8)
+            strips.append((ref, other * 312, top))
+            for v in range(3):
+                at = other * 312 + 288 + v * 8
+                wet[v, pl.ds(top, 8), :] = ref[at : at + 8, :] * 0.25
 
     def unpack(part, _):
         high, f = part // 3, part % 3
-        for ref, top in strips:
-            quads = [ref[pl.ds(pl.multiple_of(x * 48 + part * 8, 8), 8), :] for x in range(6)]
+        for ref, first, top in strips:
+            quads = [ref[pl.ds(pl.multiple_of(first + at + part * 8, 8), 8), :] for at in (0, 96, 144, 192, 240, 48)]
             for low in range(4):
                 out = pltpu.roll(quads[0], (128 - 32 * low) % 128, 1) if low else quads[0]
                 for x in range(1, 4):
@@ -233,7 +233,7 @@
         pack_kernel,
         out_shape=(
             jax.ShapeDtypeStruct((PEERS, 72, LANES), f32),
-            jax.ShapeDtypeStruct((4, 48, LANES), f32),
+            jax.ShapeDtypeStruct((48, LANES), f32),
             jax.ShapeDtypeStruct((24, LANES), f32),
         ),
         in_specs=[SMEM, SMEM, VMEM, VMEM, VMEM],
@@ -241,25 +241,23 @@
         compiler_params=pltpu.CompilerParams(vmem_limit_bytes=16 * 2**20),
     )(block.reshape(1).astype(jnp.int32), owner_order, tangents, checkpoints, land_mask)
 
+    ring = [(s * 4 + x, (s + step) % 8 * 4 + x) for s in range(8) for x, step in ((3, 1), (0, -1))]
+    halo = lax.ppermute(flow, ("y", "zh", "x"), ring)
     own = lax.all_to_all(send, ("y", "zh", "c"), 0, 0, tiled=True)
-    flows = lax.all_to_all(flow, "x", 0, 0, tiled=True)
-    left = lax.ppermute(flows[3], ("y", "zh"), [(i, (i + 1) % 8) for i in range(8)])
-    right = lax.ppermute(flows[0], ("y", "zh"), [((i + 1) % 8, i) for i in range(8)])
-    own, flows, left, right = lax.optimization_barrier((own, flows, left, right))
-
-    def near(cells, chips, cross):
-        pairs = [(z * 2 + c, (z + chips) * 2 + c ^ cross) for z in range(8) if 0 <= z + chips < 8 for c in range(2)]
-        return lax.ppermute(cells, ("zl", "c"), pairs)
-
-    strip = jnp.concatenate([flows.reshape(192, LANES), left, right, wet], axis=0)
-    parts = [near(own, 1, 0), own, near(own, -1, 0)]
-    strips = [near(strip, 1, 0), strip, near(strip, -1, 0)]
-    others = [near(strip, 1, 1), near(strip, 0, 1), near(strip, -1, 1)]
+    flows = jnp.concatenate([flow, halo], axis=0)
+    flows = lax.all_to_all(jnp.broadcast_to(flows, (4, 96, LANES)), "x", 0, 0, tiled=True)
+    strip = jnp.concatenate([flows[0], flows[1, :48], flows[2, :48], flows[3], wet], axis=0)
+    strip = jnp.concatenate([strip, lax.ppermute(strip, "c", [(0, 1), (1, 0)])], axis=0)
+    up = [(i, i + 1) for i in range(7)]
+    down = [(i + 1, i) for i in range(7)]
+    strips = [lax.ppermute(strip, "zl", up), strip, lax.ppermute(strip, "zl", down)]
+    own, strips = lax.optimization_barrier((own, strips))
+    parts = [lax.ppermute(own, "zl", up), own, lax.ppermute(own, "zl", down)]
     parts = [x.reshape(PEERS * 72, LANES) for x in parts]
     out = pl.pallas_call(
         march_kernel,
         out_shape=jax.ShapeDtypeStruct((8, 96, LANES), f32),
-        in_specs=[SMEM] + [VMEM] * 9,
+        in_specs=[SMEM] + [VMEM] * 6,
         out_specs=VMEM,
         scratch_shapes=[
             pltpu.VMEM((3, PAIRS, 3, TALL + 8, LANES), f32),
@@ -270,7 +268,7 @@
             pltpu.VMEM((2, 2, 64, LANES), f32),
         ],
         compiler_params=pltpu.CompilerParams(vmem_limit_bytes=32 * 2**20),
-    )(core.reshape(1).astype(jnp.int32), *parts, *strips, *others)
+    )(core.reshape(1).astype(jnp.int32), *parts, *strips)
     cells = lax.all_to_all(out, ("x", "c"), 0, 0, tiled=True)
     mixed = pl.pallas_call(
         mix_kernel,

time: 146 us -> 146 us (level)
  starting transfers between devices: 57.1 us -> 50.1 us
  waiting for transfers between devices: 33.7 us -> 38.5 us
  blocking collectives: 20.1 us -> 22.4 us
    ppermute x9 -> x6, waiting for transfers between devices: 33.7 us -> 38.5 us  [the longest x1 25.5 us: on_device(): lax.ppermute(strip, 'zl', down)]
    all_to_all x1, starting transfers between devices: 19.8 us -> 15.5 us  [on_device(): own = lax.all_to_all(send, ('y', 'zh', 'c'), 0, 0, tiled=True)]
    ppermute x9 -> x6, starting transfers between devices: 37.2 us -> 34.5 us  [the longest x1 18.7 us: on_device(): halo = lax.ppermute(flow, ('y', 'zh', 'x'), ring)]
    all_to_all x1, blocking collectives: 10.8 us -> 13.3 us  [on_device(): cells = lax.all_to_all(out, ('x', 'c'), 0, 0, tiled=True)]
    unnamed x10 -> x14, local copies, waits for them, and re-layouts: 3.31 us -> 3.34 us
  transfers between devices with their start and end apart: 10 -> 7, of which waited for: 5 -> 5; matrix products, arithmetic and copies ran while one was open for 0% -> 0% of each run, Pallas kernels for 0% -> 0%
where the time goes in v3:
time: 146 us; the launch traced here: 145 us
  starting transfers between devices  50.1 us (34%)
  waiting for transfers between devices  38.5 us (26%)
  Pallas kernels  30.9 us (21%)
  blocking collectives  22.4 us (15%)
  local copies, waits for them, and re-layouts  3.37 us (2%)
    pallas_call x1, Pallas kernels, on_device(): pl.pallas_call(march_kernel, out_shape=jax.ShapeDtypeStruct((8, 96, LANES...  28.1 us
    ppermute x1, waiting for transfers between devices, on_device(): lax.ppermute(strip, 'zl', down)  25.5 us
    ppermute x1, starting transfers between devices, on_device(): halo = lax.ppermute(flow, ('y', 'zh', 'x'), ring)  18.7 us
    all_to_all x1, starting transfers between devices, on_device(): own = lax.all_to_all(send, ('y', 'zh', 'c'), 0, 0, tiled=True)  15.5 us
    all_to_all x1, blocking collectives, on_device(): cells = lax.all_to_all(out, ('x', 'c'), 0, 0, tiled=True)  13.3 us
    ppermute x2, waiting for transfers between devices, on_device(): parts = [lax.ppermute(own, 'zl', up), own, lax.ppermute(own, 'zl', down)]  10.8 us
    all_to_all x1, blocking collectives, on_device(): lax.all_to_all(jnp.broadcast_to(flows, (4, 96, LANES)), 'x', 0, 0, tiled=...  9.11 us
    ppermute x2, starting transfers between devices, on_device(): parts = [lax.ppermute(own, 'zl', up), own, lax.ppermute(own, 'zl', down)]  8.5 us
  transfers between devices with their start and end apart: 7, of which 5 were waited for; matrix products, arithmetic and copies ran while one was open for 0% of the time, Pallas kernels for 0%

profile of v3, /device:TPU:1, one launch (start us, length us, event | category | flops | bytes accessed | tf_op | source)
XLA Modules:
  0.0 145.3 jit_solution(17951601145675380564)
XLA Ops:
  0.0 0.0 copy-start.4
  0.0 0.7 copy-done.4
  0.7 0.0 copy-start
  0.7 1.0 copy-done
  1.7 0.0 copy-start.1
  1.7 0.9 copy-done.1
  2.5 0.0 copy-start.3
  2.5 0.8 copy-done.3
  3.3 1.5 %shard_map.55 = (f32[16,72,128]{2,1,0:T(8,128)}, f32[48,128]{1,0:T(8,128)S(1)}, f32[24,128]{1,0:T(8,128)S(1)}) custom-call(s32[1]{0:T(128)} %bitcast.1.block_ref, s32[8]{0:T(128)S(1)} %copy-done.4, f32[4,3,8,1024]{3,2,1,0:T(8,128)S(1)} %copy-done, f32[8,3,8,32]{3,2,1,0:T(8,128)S(1)} %copy-done.1, s32[8,1024]{1,0:T(8,128)S(1)} %copy-done.3), custom_call_target="tpu_custom_call" | custom-call | tf_op jit(solution)/shard_map/pallas_call | solution.py:232
  4.8 18.7 %collective-permute-start = (f32[48,128]{1,0:T(8,128)S(1)}, f32[48,128]{1,0:T(8,128)S(1)}, u32[]{:S(2)}, u32[]{:S(2)}) collective-permute-start(f32[48,128]{1,0:T(8,128)S(1)} %get-tuple-element.13), channel_id=1, source_target_pairs={{48,112},{0,448},{112,176},{64,0},{176,240},{128,64},{240,304},{19... | collective-permute-start | bytes 73736 | tf_op jit(solution)/shard_map/ppermute | solution.py:245
  23.5 0.9 collective-permute-done
  24.5 9.1 %all_to_all.15 = f32[4,96,128]{2,1,0:T(8,128)S(1)} all-to-all(f32[4,96,128]{2,1,0:T(8,128)S(1)} %broadcast_in_dim.3), channel_id=1, replica_groups=mesh['y'=4,'zh'=2,'x'=4,'zl'=8,'c'=2] {'x'}, dimensions={0} | all-to-all | bytes 393216 | tf_op jit(solution)/shard_map/all_to_all | solution.py:248
  33.6 15.5 %all-to-all-start = ((f32[16,72,128]{2,1,0:T(8,128)}), f32[16,72,128]{2,1,0:T(8,128)S(1)}, u32[]{:S(2)}, u32[]{:S(2)}) async-start(f32[16,72,128]{2,1,0:T(8,128)} %get-tuple-element.12), calls=%async_computation | async-start | bytes 1179648 | tf_op jit(solution)/shard_map/all_to_all | solution.py:246
  49.2 2.0 %collective-permute-start.1 = (f32[312,128]{1,0:T(8,128)S(1)}, f32[312,128]{1,0:T(8,128)S(1)}, u32[]{:S(2)}, u32[]{:S(2)}) collective-permute-start(f32[312,128]{1,0:T(8,128)S(1)} %get-tuple-element.27), channel_id=1, source_target_pairs={{0,1},{1,0},{2,3},{3,2},{4,5},{5,4},{6,7},{7,6},{8,9},{9,8},{10,11... | collective-permute-start | bytes 479240 | tf_op jit(solution)/shard_map/ppermute | solution.py:250
  51.2 1.3 collective-permute-done.1
  52.5 1.3 collective-permute-start.3
  53.8 4.0 %collective-permute-start.2 = (f32[624,128]{1,0:T(8,128)S(1)}, f32[624,128]{1,0:T(8,128)S(1)}, u32[]{:S(2)}, u32[]{:S(2)}) collective-permute-start(f32[624,128]{1,0:T(8,128)S(1)} %constant_dynamic-update-slice_fusion.3.so_ref), channel_id=1, source_target_pairs={{0,2},{2,4},{4,6},{6,8},{8,10},{10,12},{12,14},{1,3},{3,5},{5,7},{... | collective-permute-start | bytes 958472 | tf_op jit(solution)/shard_map/ppermute | solution.py:253
  57.8 25.5 %collective-permute-done.3.sn_ref = f32[624,128]{1,0:T(8,128)S(1)} collective-permute-done((f32[624,128]{1,0:T(8,128)S(1)}, f32[624,128]{1,0:T(8,128)S(1)}, u32[]{:S(2)}, u32[]{:S(2)}) %collective-permute-start.3) | collective-permute-done | bytes 319520 | tf_op jit(solution)/shard_map/ppermute | solution.py:253
  83.3 0.0 collective-permute-done.2.sp_ref
  83.3 0.0 all-to-all-done
  83.3 1.3 collective-permute-start.5
  84.6 7.2 %collective-permute-start.4 = (f32[16,72,128]{2,1,0:T(8,128)S(1)}, f32[16,72,128]{2,1,0:T(8,128)S(1)}, u32[]{:S(2)}, u32[]{:S(2)}) collective-permute-start(f32[16,72,128]{2,1,0:T(8,128)S(1)} %all-to-all-done), channel_id=1, source_target_pairs={{0,2},{2,4},{4,6},{6,8},{8,10},{10,12},{12,14},{1,3},{3,5},{5,7},{... | collective-permute-start | bytes 1769480 | tf_op jit(solution)/shard_map/ppermute | solution.py:255
  91.8 9.9 %collective-permute-done.5 = f32[16,72,128]{2,1,0:T(8,128)S(1)} collective-permute-done((f32[16,72,128]{2,1,0:T(8,128)S(1)}, f32[16,72,128]{2,1,0:T(8,128)S(1)}, u32[]{:S(2)}, u32[]{:S(2)}) %collective-permute-start.5) | collective-permute-done | bytes 589856 | tf_op jit(solution)/shard_map/ppermute | solution.py:255
  101.7 0.9 collective-permute-done.4
  102.6 28.1 %shard_map.56 = f32[8,96,128]{2,1,0:T(8,128)S(1)} custom-call(s32[1]{0:T(128)} %bitcast.core_ref, f32[1152,128]{1,0:T(8,128)S(1)} %bitcast.36, f32[1152,128]{1,0:T(8,128)S(1)} %bitcast.33, f32[1152,128]{1,0:T(8,128)S(1)} %bitcast.35, f32[624,128]{1,0:T(8,128)S(1)} %collective-permute-done.2.sp_ref, ...), custom_call_target="tpu_custom_call" | custom-call | tf_op jit(solution)/shard_map/pallas_call | solution.py:257
  130.7 0.0 copy-start.2
  130.8 13.3 %all_to_all.16 = f32[8,96,128]{2,1,0:T(8,128)S(1)} all-to-all(f32[8,96,128]{2,1,0:T(8,128)S(1)} %shard_map.56), channel_id=1, replica_groups=mesh['y'=4,'zh'=2,'x'=4,'zl'=8,'c'=2] {'x','c'}, dimensions={0} | all-to-all | bytes 786432 | tf_op jit(solution)/shard_map/all_to_all | solution.py:272
  144.0 0.0 copy-done.2
  144.0 1.3 shard_map.57
  (8 shorter events, 0.1 us)
Async XLA Ops:
  0.0 0.7 copy-start.4
  0.7 1.0 copy-start
  1.7 0.9 copy-start.1
  2.5 0.8 copy-start.3
  4.8 19.6 %collective-permute-start = (f32[48,128]{1,0:T(8,128)S(1)}, f32[48,128]{1,0:T(8,128)S(1)}, u32[]{:S(2)}, u32[]{:S(2)}) collective-permute-start(f32[48,128]{1,0:T(8,128)S(1)} %get-tuple-element.13), channel_id=1, source_target_pairs={{48,112},{0,448},{112,176},{64,0},{176,240},{128,64},{240,304},{19... | collective-permute-start | bytes 73736 | tf_op jit(solution)/shard_map/ppermute | solution.py:245
  33.6 49.7 %all-to-all-start = ((f32[16,72,128]{2,1,0:T(8,128)}), f32[16,72,128]{2,1,0:T(8,128)S(1)}, u32[]{:S(2)}, u32[]{:S(2)}) async-start(f32[16,72,128]{2,1,0:T(8,128)} %get-tuple-element.12), calls=%async_computation | async-start | bytes 1179648 | tf_op jit(solution)/shard_map/all_to_all | solution.py:246
  49.2 3.3 %collective-permute-start.1 = (f32[312,128]{1,0:T(8,128)S(1)}, f32[312,128]{1,0:T(8,128)S(1)}, u32[]{:S(2)}, u32[]{:S(2)}) collective-permute-start(f32[312,128]{1,0:T(8,128)S(1)} %get-tuple-element.27), channel_id=1, source_target_pairs={{0,1},{1,0},{2,3},{3,2},{4,5},{5,4},{6,7},{7,6},{8,9},{9,8},{10,11... | collective-permute-start | bytes 479240 | tf_op jit(solution)/shard_map/ppermute | solution.py:250
  52.5 30.8 %collective-permute-start.3 = (f32[624,128]{1,0:T(8,128)S(1)}, f32[624,128]{1,0:T(8,128)S(1)}, u32[]{:S(2)}, u32[]{:S(2)}) collective-permute-start(f32[624,128]{1,0:T(8,128)S(1)} %constant_dynamic-update-slice_fusion.3.so_ref), channel_id=1, source_target_pairs={{2,0},{4,2},{6,4},{8,6},{10,8},{12,10},{14,12},{3,1},{5,3},{7,5},{... | collective-permute-start | bytes 958472 | tf_op jit(solution)/shard_map/ppermute | solution.py:253
  53.8 29.5 %collective-permute-start.2 = (f32[624,128]{1,0:T(8,128)S(1)}, f32[624,128]{1,0:T(8,128)S(1)}, u32[]{:S(2)}, u32[]{:S(2)}) collective-permute-start(f32[624,128]{1,0:T(8,128)S(1)} %constant_dynamic-update-slice_fusion.3.so_ref), channel_id=1, source_target_pairs={{0,2},{2,4},{4,6},{6,8},{8,10},{10,12},{12,14},{1,3},{3,5},{5,7},{... | collective-permute-start | bytes 958472 | tf_op jit(solution)/shard_map/ppermute | solution.py:253
  83.3 18.4 %collective-permute-start.5 = (f32[16,72,128]{2,1,0:T(8,128)S(1)}, f32[16,72,128]{2,1,0:T(8,128)S(1)}, u32[]{:S(2)}, u32[]{:S(2)}) collective-permute-start(f32[16,72,128]{2,1,0:T(8,128)S(1)} %all-to-all-done), channel_id=1, source_target_pairs={{2,0},{4,2},{6,4},{8,6},{10,8},{12,10},{14,12},{3,1},{5,3},{7,5},{... | collective-permute-start | bytes 1769480 | tf_op jit(solution)/shard_map/ppermute | solution.py:255
  84.6 18.0 %collective-permute-start.4 = (f32[16,72,128]{2,1,0:T(8,128)S(1)}, f32[16,72,128]{2,1,0:T(8,128)S(1)}, u32[]{:S(2)}, u32[]{:S(2)}) collective-permute-start(f32[16,72,128]{2,1,0:T(8,128)S(1)} %all-to-all-done), channel_id=1, source_target_pairs={{0,2},{2,4},{4,6},{6,8},{8,10},{10,12},{12,14},{1,3},{3,5},{5,7},{... | collective-permute-start | bytes 1769480 | tf_op jit(solution)/shard_map/ppermute | solution.py:255
  130.7 13.3 %copy-start.2 = (f32[128,128]{1,0:T(8,128)S(1)}, f32[128,128]{1,0:T(8,128)}, u32[]{:S(2)}) copy-start(f32[128,128]{1,0:T(8,128)} %coef_ref.1) | copy-start | bytes 196612

commit v4 on v3

--- a/solution.py
+++ b/solution.py
@@ -39,37 +39,71 @@
     return jnp.where(first, c, a), jnp.where(mid, c, b), jnp.where(first, a, jnp.where(mid, b, c))
 
 
-def pack_kernel(block_ref, order_ref, tan_ref, base_ref, mask_ref, send_ref, flow_ref, wet_ref):
+def flow_kernel(order_ref, base_ref, flow_ref):
+    for high in range(2):
+        for f in range(3):
+            flow = jnp.concatenate([base_ref[order_ref[high * 4 + low], f] for low in range(4)], axis=1)
+            for k in range(4):
+                flow_ref[k, (high * 3 + f) * 8 : (high * 3 + f) * 8 + 8, :] = flow
+
+
+def pack_kernel(block_ref, tan_ref, mask_ref, flows_ref, send_ref, strip_ref):
     lane = lax.broadcasted_iota(jnp.int32, (8, LANES), 1)
+    s = block_ref[0]
     wet = [mask_ref[:, k * LANES : (k + 1) * LANES].astype(f32) for k in range(8)]
-    for core in range(2):
-        for f in range(3):
+
+    def fields(f, _):
+        at = f * 8
+        early = lane % 32 < 16
+        last = [flows_ref[3, pl.ds(pl.multiple_of(high * 24 + at, 8), 8), :] for high in range(2)]
+        head = [flows_ref[0, pl.ds(pl.multiple_of(high * 24 + at, 8), 8), :] for high in range(2)]
+        to_right = jnp.where(early, pltpu.roll(last[0], LANES - 16, 1), last[1])
+        to_left = jnp.where(early, head[0], pltpu.roll(head[1], 16, 1))
+        for core in range(2):
             one = [tan_ref[2 * core, f, :, k * LANES : (k + 1) * LANES] * wet[k] for k in range(8)]
             two = [
                 pltpu.roll(tan_ref[2 * core + 1, f, :, k * LANES : (k + 1) * LANES] * wet[k], 64, 1) for k in range(8)
             ]
-            for s in range(8):
-                left, right = (s + 7) % 8, (s + 1) % 8
+            for k in range(8):
+                left, right = (k + 7) % 8, (k + 1) % 8
                 halo = edges(one[left], one[right], two[left], two[right], lane)
-                for v, part in enumerate((one[s], two[s], halo)):
-                    send_ref[2 * s + core, v * 24 + f * 8 : v * 24 + f * 8 + 8, :] = part
-    s = block_ref[0]
+                border = jnp.where(lax.rem(s + 7, 8) == k, to_left, to_right)
+                for v, part in enumerate((one[k], two[k], halo, border)):
+                    send_ref[2 * k + core, pl.ds(pl.multiple_of(v * 24 + at, 8), 8), :] = part
+
+    lax.fori_loop(0, 3, fields, None)
 
     def column(k):
         return mask_ref[:, pl.ds(pl.multiple_of(k * LANES, LANES), LANES)].astype(f32)
 
     here, left, right = column(s), column(lax.rem(s + 7, 8)), column(lax.rem(s + 1, 8))
-    wet_ref[0:8, :] = here
-    wet_ref[8:16, :] = pltpu.roll(here, 64, 1)
-    wet_ref[16:24, :] = edges(left, right, pltpu.roll(left, 64, 1), pltpu.roll(right, 64, 1), lane)
-    for high in range(2):
-        for f in range(3):
-            flow = jnp.concatenate([base_ref[order_ref[high * 4 + low], f] for low in range(4)], axis=1)
-            flow_ref[(high * 3 + f) * 8 : (high * 3 + f) * 8 + 8, :] = flow
+    strip_ref[192:200, :] = here
+    strip_ref[200:208, :] = pltpu.roll(here, 64, 1)
+    strip_ref[208:216, :] = edges(left, right, pltpu.roll(left, 64, 1), pltpu.roll(right, 64, 1), lane)
+    for x in range(4):
+        strip_ref[x * 48 : x * 48 + 48, :] = flows_ref[x]
+
+
+CELLS = PEERS * 72
+BORDER = CELLS + 2 * 216
+NEAR = BORDER + 4 * 24
+
+
+def near_kernel(block_ref, own_ref, strip_ref, other_ref, near_ref):
+    s = block_ref[0]
+    for p in range(PEERS):
+        near_ref[p * 72 : p * 72 + 72, :] = own_ref[p * 96 : p * 96 + 72, :]
+    near_ref[CELLS : CELLS + 216, :] = strip_ref[...]
+    near_ref[CELLS + 216 : CELLS + 432, :] = other_ref[...]
+    for c in range(2):
+        for side, block in enumerate((lax.rem(s + 7, 8), lax.rem(s + 1, 8))):
+            at = BORDER + (c * 2 + side) * 24
+            start = pl.multiple_of((block * 2 + c) * 96 + 72, 8)
+            near_ref[at : at + 24, :] = own_ref[pl.ds(start, 24), :]
 
 
 def march_kernel(
-    core_ref, prev_ref, own_ref, next_ref, sp_ref, so_ref, sn_ref,
+    core_ref, prev_ref, own_ref, next_ref,
     out_ref, state, middle, base, wet, coef, turn,
 ):
     lane = lax.broadcasted_iota(jnp.int32, (8, LANES), 1)
@@ -84,32 +118,34 @@
     lax.fori_loop(0, PAIRS, place, None)
     core = core_ref[0]
     strips = []
-    for z, ref in enumerate((sp_ref, so_ref, sn_ref)):
+    for z, ref in enumerate((prev_ref, own_ref, next_ref)):
         for other in range(2):
-            top = pl.multiple_of((1 - core if other else core) * 8 + z * 16, 8)
-            strips.append((ref, other * 312, top))
+            which = 1 - core if other else core
+            first, top = CELLS + other * 216, pl.multiple_of(which * 8 + z * 16, 8)
+            strips.append((ref, first, BORDER + which * 48, top))
             for v in range(3):
-                at = other * 312 + 288 + v * 8
+                at = first + 192 + v * 8
                 wet[v, pl.ds(top, 8), :] = ref[at : at + 8, :] * 0.25
 
-    def unpack(part, _):
-        high, f = part // 3, part % 3
-        for ref, first, top in strips:
-            quads = [ref[pl.ds(pl.multiple_of(first + at + part * 8, 8), 8), :] for at in (0, 96, 144, 192, 240, 48)]
-            for low in range(4):
-                out = pltpu.roll(quads[0], (128 - 32 * low) % 128, 1) if low else quads[0]
-                for x in range(1, 4):
-                    turned = pltpu.roll(quads[x], 32 * (x - low) % 128, 1) if x != low else quads[x]
-                    out = jnp.where(lane >= 32 * x, turned, out)
-                left = pltpu.roll(quads[4], (96 - 32 * low) % 128, 1)
-                right = pltpu.roll(quads[5], (128 - 32 * low) % 128, 1)
-                halo = edges(left, right, pltpu.roll(left, 64, 1), pltpu.roll(right, 64, 1), lane)
-                rows = pl.ds(top + 8, 8)
-                base[high * 4 + low, f, 0, rows, :] = out
-                base[high * 4 + low, f, 1, rows, :] = pltpu.roll(out, 64, 1)
-                base[high * 4 + low, f, 2, rows, :] = halo
-
-    lax.fori_loop(0, 6, unpack, None)
+    def unpack(f, _):
+        for ref, first, border, top in strips:
+            left, right = (ref[pl.ds(pl.multiple_of(border + side * 24 + f * 8, 8), 8), :] for side in range(2))
+            for high in range(2):
+                quads = [ref[pl.ds(pl.multiple_of(first + x * 48 + high * 24 + f * 8, 8), 8), :] for x in range(4)]
+                for low in range(4):
+                    out = pltpu.roll(quads[0], (128 - 32 * low) % 128, 1) if low else quads[0]
+                    for x in range(1, 4):
+                        turned = pltpu.roll(quads[x], 32 * (x - low) % 128, 1) if x != low else quads[x]
+                        out = jnp.where(lane >= 32 * x, turned, out)
+                    shift = low * 32 + high * 16
+                    sides = [pltpu.roll(cells, (to - shift) % 128, 1) if to != shift else cells
+                             for to, cells in ((112, left), (0, right), (48, left), (64, right))]
+                    rows = pl.ds(top + 8, 8)
+                    base[high * 4 + low, f, 0, rows, :] = out
+                    base[high * 4 + low, f, 1, rows, :] = pltpu.roll(out, 64, 1)
+                    base[high * 4 + low, f, 2, rows, :] = edges(*sides, lane)
+
+    lax.fori_loop(0, 3, unpack, None)
 
     def prepare(step, tile):
         top = pl.multiple_of(tile * 8, 8)
@@ -229,35 +265,40 @@
 def on_device(tangents, checkpoints, owner_order, land_mask, coefficients):
     block = lax.axis_index("y") * 2 + lax.axis_index("zh")
     core = lax.axis_index("c")
-    send, flow, wet = pl.pallas_call(
+    s = block.reshape(1).astype(jnp.int32)
+    flow = pl.pallas_call(
+        flow_kernel,
+        out_shape=jax.ShapeDtypeStruct((4, 48, LANES), f32),
+        in_specs=[SMEM, VMEM],
+        out_specs=VMEM,
+        compiler_params=pltpu.CompilerParams(vmem_limit_bytes=16 * 2**20),
+    )(owner_order, checkpoints)
+    flows = lax.all_to_all(flow, "x", 0, 0, tiled=True)
+    send, strip = pl.pallas_call(
         pack_kernel,
-        out_shape=(
-            jax.ShapeDtypeStruct((PEERS, 72, LANES), f32),
-            jax.ShapeDtypeStruct((48, LANES), f32),
-            jax.ShapeDtypeStruct((24, LANES), f32),
-        ),
-        in_specs=[SMEM, SMEM, VMEM, VMEM, VMEM],
-        out_specs=(VMEM, VMEM, VMEM),
+        out_shape=(jax.ShapeDtypeStruct((PEERS, 96, LANES), f32), jax.ShapeDtypeStruct((216, LANES), f32)),
+        in_specs=[SMEM, VMEM, VMEM, VMEM],
+        out_specs=(VMEM, VMEM),
         compiler_params=pltpu.CompilerParams(vmem_limit_bytes=16 * 2**20),
-    )(block.reshape(1).astype(jnp.int32), owner_order, tangents, checkpoints, land_mask)
-
-    ring = [(s * 4 + x, (s + step) % 8 * 4 + x) for s in range(8) for x, step in ((3, 1), (0, -1))]
-    halo = lax.ppermute(flow, ("y", "zh", "x"), ring)
+    )(s, tangents, land_mask, flows)
     own = lax.all_to_all(send, ("y", "zh", "c"), 0, 0, tiled=True)
-    flows = jnp.concatenate([flow, halo], axis=0)
-    flows = lax.all_to_all(jnp.broadcast_to(flows, (4, 96, LANES)), "x", 0, 0, tiled=True)
-    strip = jnp.concatenate([flows[0], flows[1, :48], flows[2, :48], flows[3], wet], axis=0)
-    strip = jnp.concatenate([strip, lax.ppermute(strip, "c", [(0, 1), (1, 0)])], axis=0)
-    up = [(i, i + 1) for i in range(7)]
-    down = [(i + 1, i) for i in range(7)]
-    strips = [lax.ppermute(strip, "zl", up), strip, lax.ppermute(strip, "zl", down)]
-    own, strips = lax.optimization_barrier((own, strips))
-    parts = [lax.ppermute(own, "zl", up), own, lax.ppermute(own, "zl", down)]
-    parts = [x.reshape(PEERS * 72, LANES) for x in parts]
+    other = lax.ppermute(strip, "c", [(0, 1), (1, 0)])
+    near = pl.pallas_call(
+        near_kernel,
+        out_shape=jax.ShapeDtypeStruct((NEAR, LANES), f32),
+        in_specs=[SMEM, VMEM, VMEM, VMEM],
+        out_specs=VMEM,
+        compiler_params=pltpu.CompilerParams(vmem_limit_bytes=16 * 2**20),
+    )(s, own.reshape(PEERS * 96, LANES), strip, other)
+    parts = [
+        lax.ppermute(near, "zl", [(i, i + 1) for i in range(7)]),
+        near,
+        lax.ppermute(near, "zl", [(i + 1, i) for i in range(7)]),
+    ]
     out = pl.pallas_call(
         march_kernel,
         out_shape=jax.ShapeDtypeStruct((8, 96, LANES), f32),
-        in_specs=[SMEM] + [VMEM] * 6,
+        in_specs=[SMEM] + [VMEM] * 3,
         out_specs=VMEM,
         scratch_shapes=[
             pltpu.VMEM((3, PAIRS, 3, TALL + 8, LANES), f32),
@@ -268,7 +309,7 @@
             pltpu.VMEM((2, 2, 64, LANES), f32),
         ],
         compiler_params=pltpu.CompilerParams(vmem_limit_bytes=32 * 2**20),
-    )(core.reshape(1).astype(jnp.int32), *parts, *strips)
+    )(core.reshape(1).astype(jnp.int32), *parts)
     cells = lax.all_to_all(out, ("x", "c"), 0, 0, tiled=True)
     mixed = pl.pallas_call(
         mix_kernel,

time: 146 us -> 148 us (1.014)
  blocking collectives: 22.4 us -> 12.5 us
  waiting for transfers between devices: 38.5 us -> 46.7 us
  Pallas kernels: 30.9 us -> 34.3 us
    all_to_all x1, waiting for transfers between devices: 0.01 us -> 23.5 us  [on_device(): own = lax.all_to_all(send, ('y', 'zh', 'c'), 0, 0, tiled=True)]
    ppermute x6 -> x3, waiting for transfers between devices: 38.5 us -> 18.5 us  [the longest x1 16.4 us: on_device(): lax.ppermute(near, 'zl', [(i + 1, i) for i in range(7)])]
    all_to_all x1 -> x0, blocking collectives: 9.11 us -> none  [on_device(): lax.all_to_all(jnp.broadcast_to(flows, (4, 96, LANES)), 'x', 0, 0, tiled=...]
    ppermute x6 -> x3, starting transfers between devices: 34.5 us -> 26.8 us  [the longest x1 23.5 us: on_device(): lax.ppermute(near, 'zl', [(i, i + 1) for i in range(7)])]
    all_to_all x0 -> x1, starting transfers between devices: none -> 4.84 us  [on_device(): flows = lax.all_to_all(flow, 'x', 0, 0, tiled=True)]
    all_to_all x0 -> x1, waiting for transfers between devices: none -> 4.65 us  [on_device(): flows = lax.all_to_all(flow, 'x', 0, 0, tiled=True)]
    all_to_all x1, starting transfers between devices: 15.5 us -> 19.8 us  [on_device(): own = lax.all_to_all(send, ('y', 'zh', 'c'), 0, 0, tiled=True)]
    pallas_call x1, Pallas kernels: 28.1 us -> 30.5 us  [on_device(): pl.pallas_call(march_kernel, out_shape=jax.ShapeDtypeStruct((8, 96, LANES...]
  transfers between devices with their start and end apart: 7 -> 5, of which waited for: 5 -> 5; matrix products, arithmetic and copies ran while one was open for 0% -> 0% of each run, Pallas kernels for 0% -> 0%
where the time goes in v4:
time: 148 us; the launch traced here: 147 us
  starting transfers between devices  51.5 us (35%)
  waiting for transfers between devices  46.7 us (32%)
  Pallas kernels  34.3 us (23%)
  blocking collectives  12.5 us (8%)
  local copies, waits for them, and re-layouts  2.37 us (2%)
    pallas_call x1, Pallas kernels, on_device(): pl.pallas_call(march_kernel, out_shape=jax.ShapeDtypeStruct((8, 96, LANES...  30.5 us
    all_to_all x1, waiting for transfers between devices, on_device(): own = lax.all_to_all(send, ('y', 'zh', 'c'), 0, 0, tiled=True)  23.5 us
    ppermute x1, starting transfers between devices, on_device(): lax.ppermute(near, 'zl', [(i, i + 1) for i in range(7)])  23.5 us
    all_to_all x1, starting transfers between devices, on_device(): own = lax.all_to_all(send, ('y', 'zh', 'c'), 0, 0, tiled=True)  19.8 us
    ppermute x1, waiting for transfers between devices, on_device(): lax.ppermute(near, 'zl', [(i + 1, i) for i in range(7)])  16.4 us
    all_to_all x1, blocking collectives, on_device(): cells = lax.all_to_all(out, ('x', 'c'), 0, 0, tiled=True)  12.5 us
    all_to_all x1, starting transfers between devices, on_device(): flows = lax.all_to_all(flow, 'x', 0, 0, tiled=True)  4.84 us
    all_to_all x1, waiting for transfers between devices, on_device(): flows = lax.all_to_all(flow, 'x', 0, 0, tiled=True)  4.65 us
  transfers between devices with their start and end apart: 5, of which 5 were waited for; matrix products, arithmetic and copies ran while one was open for 0% of the time, Pallas kernels for 0%

profile of v4, /device:TPU:1, one launch (start us, length us, event | category | flops | bytes accessed | tf_op | source)
XLA Modules:
  0.0 147.4 jit_solution(18398227696346570886)
XLA Ops:
  0.0 0.0 copy-start
  0.0 0.0 copy-start.1
  0.0 0.9 copy-done.1
  0.9 0.0 copy-start.4
  0.9 0.7 copy-done.4
  1.6 1.3 shard_map.55
  2.9 4.8 %all-to-all-start = ((f32[4,48,128]{2,1,0:T(8,128)}), f32[4,48,128]{2,1,0:T(8,128)S(1)}, u32[]{:S(2)}, u32[]{:S(2)}) async-start(f32[4,48,128]{2,1,0:T(8,128)} %shard_map.55), calls=%async_computation | async-start | bytes 196608 | tf_op jit(solution)/shard_map/all_to_all | solution.py:276
  7.7 4.7 %all-to-all-done.flows_ref = f32[4,48,128]{2,1,0:T(8,128)S(1)} async-done(((f32[4,48,128]{2,1,0:T(8,128)}), f32[4,48,128]{2,1,0:T(8,128)S(1)}, u32[]{:S(2)}, u32[]{:S(2)}) %all-to-all-start) | async-done | bytes 98336 | tf_op jit(solution)/shard_map/all_to_all | solution.py:276
  12.4 0.0 copy-done
  12.4 0.0 copy-start.3
  12.4 0.8 copy-done.3
  13.1 1.2 shard_map.56
  14.3 19.8 %all-to-all-start.1 = ((f32[16,96,128]{2,1,0:T(8,128)}), f32[16,96,128]{2,1,0:T(8,128)S(1)}, u32[]{:S(2)}, u32[]{:S(2)}) async-start(f32[16,96,128]{2,1,0:T(8,128)} %get-tuple-element.7), calls=%async_computation.1 | async-start | bytes 1572864 | tf_op jit(solution)/shard_map/all_to_all | solution.py:284
  34.2 2.0 %collective-permute-start = (f32[216,128]{1,0:T(8,128)S(1)}, f32[216,128]{1,0:T(8,128)S(1)}, u32[]{:S(2)}, u32[]{:S(2)}) collective-permute-start(f32[216,128]{1,0:T(8,128)S(1)} %get-tuple-element.8.strip_ref), channel_id=1, source_target_pairs={{0,1},{1,0},{2,3},{3,2},{4,5},{5,4},{6,7},{7,6},{8,9},{9,8},{10,11... | collective-permute-start | bytes 331784 | tf_op jit(solution)/shard_map/ppermute | solution.py:285
  36.2 1.2 collective-permute-done.other_ref
  37.4 23.5 %all-to-all-done.1 = f32[16,96,128]{2,1,0:T(8,128)S(1)} async-done(((f32[16,96,128]{2,1,0:T(8,128)}), f32[16,96,128]{2,1,0:T(8,128)S(1)}, u32[]{:S(2)}, u32[]{:S(2)}) %all-to-all-start.1) | async-done | bytes 786464 | tf_op jit(solution)/shard_map/all_to_all | solution.py:284
  60.9 0.1 shard_map.57.own_ref
  61.0 1.3 collective-permute-start.2
  62.3 23.5 %collective-permute-start.1 = (f32[1680,128]{1,0:T(8,128)S(1)}, f32[1680,128]{1,0:T(8,128)S(1)}, u32[]{:S(2)}, u32[]{:S(2)}) collective-permute-start(f32[1680,128]{1,0:T(8,128)S(1)} %shard_map.57.own_ref), channel_id=1, source_target_pairs={{0,2},{2,4},{4,6},{6,8},{8,10},{10,12},{12,14},{1,3},{3,5},{5,7},{... | collective-permute-start | bytes 2580488 | tf_op jit(solution)/shard_map/ppermute | solution.py:294
  85.7 16.4 %collective-permute-done.2.next_ref = f32[1680,128]{1,0:T(8,128)S(1)} collective-permute-done((f32[1680,128]{1,0:T(8,128)S(1)}, f32[1680,128]{1,0:T(8,128)S(1)}, u32[]{:S(2)}, u32[]{:S(2)}) %collective-permute-start.2) | collective-permute-done | bytes 860192 | tf_op jit(solution)/shard_map/ppermute | solution.py:296
  102.2 0.9 collective-permute-done.1.prev_ref
  103.1 30.5 %shard_map.58 = f32[8,96,128]{2,1,0:T(8,128)S(1)} custom-call(s32[1]{0:T(128)} %bitcast.core_ref, f32[1680,128]{1,0:T(8,128)S(1)} %collective-permute-done.1.prev_ref, f32[1680,128]{1,0:T(8,128)S(1)} %shard_map.57.own_ref, f32[1680,128]{1,0:T(8,128)S(1)} %collective-permute-done.2.next_ref), custom_call_target="tpu_custom_call" | custom-call | tf_op jit(solution)/shard_map/pallas_call | solution.py:298
  133.6 0.0 copy-start.2
  133.6 12.5 %all_to_all.15 = f32[8,96,128]{2,1,0:T(8,128)S(1)} all-to-all(f32[8,96,128]{2,1,0:T(8,128)S(1)} %shard_map.58), channel_id=1, replica_groups=mesh['y'=4,'zh'=2,'x'=4,'zl'=8,'c'=2] {'x','c'}, dimensions={0} | all-to-all | bytes 786432 | tf_op jit(solution)/shard_map/all_to_all | solution.py:313
  146.2 0.0 copy-done.2
  146.2 1.3 shard_map.59
Async XLA Ops:
  0.0 12.4 %copy-start = (f32[4,3,8,1024]{3,2,1,0:T(8,128)S(1)}, f32[4,3,8,1024]{3,2,1,0:T(8,128)}, u32[]{:S(2)}) copy-start(f32[4,3,8,1024]{3,2,1,0:T(8,128)} %tan_ref.1) | copy-start | bytes 1179652
  0.0 0.9 copy-start.1
  0.9 0.7 copy-start.4
  2.9 9.5 %all-to-all-start = ((f32[4,48,128]{2,1,0:T(8,128)}), f32[4,48,128]{2,1,0:T(8,128)S(1)}, u32[]{:S(2)}, u32[]{:S(2)}) async-start(f32[4,48,128]{2,1,0:T(8,128)} %shard_map.55), calls=%async_computation | async-start | bytes 196608 | tf_op jit(solution)/shard_map/all_to_all | solution.py:276
  12.4 0.8 copy-start.3
  14.3 46.6 %all-to-all-start.1 = ((f32[16,96,128]{2,1,0:T(8,128)}), f32[16,96,128]{2,1,0:T(8,128)S(1)}, u32[]{:S(2)}, u32[]{:S(2)}) async-start(f32[16,96,128]{2,1,0:T(8,128)} %get-tuple-element.7), calls=%async_computation.1 | async-start | bytes 1572864 | tf_op jit(solution)/shard_map/all_to_all | solution.py:284
  34.2 3.2 %collective-permute-start = (f32[216,128]{1,0:T(8,128)S(1)}, f32[216,128]{1,0:T(8,128)S(1)}, u32[]{:S(2)}, u32[]{:S(2)}) collective-permute-start(f32[216,128]{1,0:T(8,128)S(1)} %get-tuple-element.8.strip_ref), channel_id=1, source_target_pairs={{0,1},{1,0},{2,3},{3,2},{4,5},{5,4},{6,7},{7,6},{8,9},{9,8},{10,11... | collective-permute-start | bytes 331784 | tf_op jit(solution)/shard_map/ppermute | solution.py:285
  61.0 41.2 %collective-permute-start.2 = (f32[1680,128]{1,0:T(8,128)S(1)}, f32[1680,128]{1,0:T(8,128)S(1)}, u32[]{:S(2)}, u32[]{:S(2)}) collective-permute-start(f32[1680,128]{1,0:T(8,128)S(1)} %shard_map.57.own_ref), channel_id=1, source_target_pairs={{2,0},{4,2},{6,4},{8,6},{10,8},{12,10},{14,12},{3,1},{5,3},{7,5},{... | collective-permute-start | bytes 2580488 | tf_op jit(solution)/shard_map/ppermute | solution.py:296
  62.3 40.8 %collective-permute-start.1 = (f32[1680,128]{1,0:T(8,128)S(1)}, f32[1680,128]{1,0:T(8,128)S(1)}, u32[]{:S(2)}, u32[]{:S(2)}) collective-permute-start(f32[1680,128]{1,0:T(8,128)S(1)} %shard_map.57.own_ref), channel_id=1, source_target_pairs={{0,2},{2,4},{4,6},{6,8},{8,10},{10,12},{12,14},{1,3},{3,5},{5,7},{... | collective-permute-start | bytes 2580488 | tf_op jit(solution)/shard_map/ppermute | solution.py:294
  133.6 12.6 %copy-start.2 = (f32[128,128]{1,0:T(8,128)S(1)}, f32[128,128]{1,0:T(8,128)}, u32[]{:S(2)}) copy-start(f32[128,128]{1,0:T(8,128)} %coef_ref.1) | copy-start | bytes 196612

commit v5 on v3

--- a/solution.py
+++ b/solution.py
@@ -39,37 +39,44 @@
     return jnp.where(first, c, a), jnp.where(mid, c, b), jnp.where(first, a, jnp.where(mid, b, c))
 
 
-def pack_kernel(block_ref, order_ref, tan_ref, base_ref, mask_ref, send_ref, flow_ref, wet_ref):
+def flow_kernel(block_ref, order_ref, base_ref, mask_ref, raw_ref):
+    lane = lax.broadcasted_iota(jnp.int32, (8, LANES), 1)
+    s = block_ref[0]
+    for high in range(2):
+        for f in range(3):
+            flow = jnp.concatenate([base_ref[order_ref[high * 4 + low], f] for low in range(4)], axis=1)
+            raw_ref[(high * 3 + f) * 8 : (high * 3 + f) * 8 + 8, :] = flow
+
+    def column(k):
+        return mask_ref[:, pl.ds(pl.multiple_of(k * LANES, LANES), LANES)].astype(f32)
+
+    here, left, right = column(s), column(lax.rem(s + 7, 8)), column(lax.rem(s + 1, 8))
+    raw_ref[48:56, :] = here
+    raw_ref[56:64, :] = pltpu.roll(here, 64, 1)
+    raw_ref[64:72, :] = edges(left, right, pltpu.roll(left, 64, 1), pltpu.roll(right, 64, 1), lane)
+
+
+def pack_kernel(tan_ref, mask_ref, send_ref):
     lane = lax.broadcasted_iota(jnp.int32, (8, LANES), 1)
     wet = [mask_ref[:, k * LANES : (k + 1) * LANES].astype(f32) for k in range(8)]
-    for core in range(2):
-        for f in range(3):
+
+    def fields(f, _):
+        for core in range(2):
             one = [tan_ref[2 * core, f, :, k * LANES : (k + 1) * LANES] * wet[k] for k in range(8)]
             two = [
                 pltpu.roll(tan_ref[2 * core + 1, f, :, k * LANES : (k + 1) * LANES] * wet[k], 64, 1) for k in range(8)
             ]
-            for s in range(8):
-                left, right = (s + 7) % 8, (s + 1) % 8
+            for k in range(8):
+                left, right = (k + 7) % 8, (k + 1) % 8
                 halo = edges(one[left], one[right], two[left], two[right], lane)
-                for v, part in enumerate((one[s], two[s], halo)):
-                    send_ref[2 * s + core, v * 24 + f * 8 : v * 24 + f * 8 + 8, :] = part
-    s = block_ref[0]
-
-    def column(k):
-        return mask_ref[:, pl.ds(pl.multiple_of(k * LANES, LANES), LANES)].astype(f32)
-
-    here, left, right = column(s), column(lax.rem(s + 7, 8)), column(lax.rem(s + 1, 8))
-    wet_ref[0:8, :] = here
-    wet_ref[8:16, :] = pltpu.roll(here, 64, 1)
-    wet_ref[16:24, :] = edges(left, right, pltpu.roll(left, 64, 1), pltpu.roll(right, 64, 1), lane)
-    for high in range(2):
-        for f in range(3):
-            flow = jnp.concatenate([base_ref[order_ref[high * 4 + low], f] for low in range(4)], axis=1)
-            flow_ref[(high * 3 + f) * 8 : (high * 3 + f) * 8 + 8, :] = flow
+                for v, part in enumerate((one[k], two[k], halo)):
+                    send_ref[2 * k + core, pl.ds(pl.multiple_of(v * 24 + f * 8, 8), 8), :] = part
+
+    lax.fori_loop(0, 3, fields, None)
 
 
 def march_kernel(
-    core_ref, prev_ref, own_ref, next_ref, sp_ref, so_ref, sn_ref,
+    core_ref, prev_ref, own_ref, next_ref, strip_ref, other_ref,
     out_ref, state, middle, base, wet, coef, turn,
 ):
     lane = lax.broadcasted_iota(jnp.int32, (8, LANES), 1)
@@ -82,20 +89,22 @@
                         state[f, p, v, z * 16 + c * 8 : z * 16 + c * 8 + 8, :] = ref[pl.ds(at, 8), :]
 
     lax.fori_loop(0, PAIRS, place, None)
-    core = core_ref[0]
+    core, me = core_ref[0], core_ref[1]
+    blocks = [lax.rem(me - x + 4, 4) * 288 for x in range(4)]
+    places = blocks + [blocks[3] + 144, blocks[0] + 144]
     strips = []
-    for z, ref in enumerate((sp_ref, so_ref, sn_ref)):
-        for other in range(2):
+    for other, ref in enumerate((strip_ref, other_ref)):
+        for z in range(3):
             top = pl.multiple_of((1 - core if other else core) * 8 + z * 16, 8)
-            strips.append((ref, other * 312, top))
+            strips.append((ref, z * 48, top))
             for v in range(3):
-                at = other * 312 + 288 + v * 8
+                at = 1152 + z * 24 + v * 8
                 wet[v, pl.ds(top, 8), :] = ref[at : at + 8, :] * 0.25
 
     def unpack(part, _):
         high, f = part // 3, part % 3
         for ref, first, top in strips:
-            quads = [ref[pl.ds(pl.multiple_of(first + at + part * 8, 8), 8), :] for at in (0, 96, 144, 192, 240, 48)]
+            quads = [ref[pl.ds(pl.multiple_of(first + at + part * 8, 8), 8), :] for at in places]
             for low in range(4):
                 out = pltpu.roll(quads[0], (128 - 32 * low) % 128, 1) if low else quads[0]
                 for x in range(1, 4):
@@ -229,35 +238,40 @@
 def on_device(tangents, checkpoints, owner_order, land_mask, coefficients):
     block = lax.axis_index("y") * 2 + lax.axis_index("zh")
     core = lax.axis_index("c")
-    send, flow, wet = pl.pallas_call(
+    raw = pl.pallas_call(
+        flow_kernel,
+        out_shape=jax.ShapeDtypeStruct((72, LANES), f32),
+        in_specs=[SMEM, SMEM, VMEM, VMEM],
+        out_specs=VMEM,
+        compiler_params=pltpu.CompilerParams(vmem_limit_bytes=16 * 2**20),
+    )(block.reshape(1).astype(jnp.int32), owner_order, checkpoints, land_mask)
+    send = pl.pallas_call(
         pack_kernel,
-        out_shape=(
-            jax.ShapeDtypeStruct((PEERS, 72, LANES), f32),
-            jax.ShapeDtypeStruct((48, LANES), f32),
-            jax.ShapeDtypeStruct((24, LANES), f32),
-        ),
-        in_specs=[SMEM, SMEM, VMEM, VMEM, VMEM],
-        out_specs=(VMEM, VMEM, VMEM),
+        out_shape=jax.ShapeDtypeStruct((PEERS, 72, LANES), f32),
+        in_specs=[VMEM, VMEM],
+        out_specs=VMEM,
         compiler_params=pltpu.CompilerParams(vmem_limit_bytes=16 * 2**20),
-    )(block.reshape(1).astype(jnp.int32), owner_order, tangents, checkpoints, land_mask)
-
+    )(tangents, land_mask)
+    up = [(i, i + 1) for i in range(7)]
+    down = [(i + 1, i) for i in range(7)]
+    chips = [lax.ppermute(raw, "zl", up), raw, lax.ppermute(raw, "zl", down)]
+    flow = jnp.concatenate([x[:48] for x in chips], axis=0)
+    wet = [x[48:] for x in chips]
     ring = [(s * 4 + x, (s + step) % 8 * 4 + x) for s in range(8) for x, step in ((3, 1), (0, -1))]
     halo = lax.ppermute(flow, ("y", "zh", "x"), ring)
+    send, halo = lax.optimization_barrier((send, halo))
     own = lax.all_to_all(send, ("y", "zh", "c"), 0, 0, tiled=True)
-    flows = jnp.concatenate([flow, halo], axis=0)
-    flows = lax.all_to_all(jnp.broadcast_to(flows, (4, 96, LANES)), "x", 0, 0, tiled=True)
-    strip = jnp.concatenate([flows[0], flows[1, :48], flows[2, :48], flows[3], wet], axis=0)
-    strip = jnp.concatenate([strip, lax.ppermute(strip, "c", [(0, 1), (1, 0)])], axis=0)
-    up = [(i, i + 1) for i in range(7)]
-    down = [(i + 1, i) for i in range(7)]
-    strips = [lax.ppermute(strip, "zl", up), strip, lax.ppermute(strip, "zl", down)]
-    own, strips = lax.optimization_barrier((own, strips))
+    flow = jnp.concatenate([flow, halo], axis=0)
+    flows = [lax.ppermute(flow, "x", [(i, (i + k) % 4) for i in range(4)]) for k in (1, 2, 3)]
+    strip = jnp.concatenate([flow, *flows, *wet], axis=0)
+    other = lax.ppermute(strip, "c", [(0, 1), (1, 0)])
+    own, other = lax.optimization_barrier((own, other))
     parts = [lax.ppermute(own, "zl", up), own, lax.ppermute(own, "zl", down)]
     parts = [x.reshape(PEERS * 72, LANES) for x in parts]
     out = pl.pallas_call(
         march_kernel,
         out_shape=jax.ShapeDtypeStruct((8, 96, LANES), f32),
-        in_specs=[SMEM] + [VMEM] * 6,
+        in_specs=[SMEM] + [VMEM] * 5,
         out_specs=VMEM,
         scratch_shapes=[
             pltpu.VMEM((3, PAIRS, 3, TALL + 8, LANES), f32),
@@ -268,7 +282,7 @@
             pltpu.VMEM((2, 2, 64, LANES), f32),
         ],
         compiler_params=pltpu.CompilerParams(vmem_limit_bytes=32 * 2**20),
-    )(core.reshape(1).astype(jnp.int32), *parts, *strips)
+    )(jnp.stack([core, lax.axis_index("x")]).astype(jnp.int32), *parts, strip, other)
     cells = lax.all_to_all(out, ("x", "c"), 0, 0, tiled=True)
     mixed = pl.pallas_call(
         mix_kernel,

time: 146 us -> 149 us (1.021)
  starting transfers between devices: 50.1 us -> 77.6 us
  waiting for transfers between devices: 38.5 us -> 24.2 us
  blocking collectives: 22.4 us -> 12.2 us
    ppermute x3 -> x6, waiting for transfers between devices: 26.7 us -> 10.7 us  [the longest x3 5.53 us: on_device(): lax.ppermute(flow, 'x', [(i, (i + k) % 4) for i in range(4)])]
    ppermute x2, starting transfers between devices: 8.5 us -> 24 us  [on_device(): parts = [lax.ppermute(own, 'zl', up), own, lax.ppermute(own, 'zl', down)]]
    ppermute x3 -> x6, starting transfers between devices: 7.31 us -> 18.2 us  [the longest x3 9.09 us: on_device(): lax.ppermute(flow, 'x', [(i, (i + k) % 4) for i in range(4)])]
    all_to_all x1 -> x0, blocking collectives: 9.11 us -> none  [on_device(): lax.all_to_all(jnp.broadcast_to(flows, (4, 96, LANES)), 'x', 0, 0, tiled=...]
    all_to_all x1, starting transfers between devices: 15.5 us -> 18.6 us  [on_device(): own = lax.all_to_all(send, ('y', 'zh', 'c'), 0, 0, tiled=True)]
    ppermute x1, starting transfers between devices: 18.7 us -> 16.8 us  [on_device(): halo = lax.ppermute(flow, ('y', 'zh', 'x'), ring)]
    unnamed x14 -> x19, local copies, waits for them, and re-layouts: 3.34 us -> 2.43 us
  transfers between devices with their start and end apart: 7 -> 10, of which waited for: 5 -> 7; matrix products, arithmetic and copies ran while one was open for 0% -> 0% of each run, Pallas kernels for 0% -> 1%
where the time goes in v5:
time: 149 us; the launch traced here: 148 us
  starting transfers between devices  77.6 us (52%)
  Pallas kernels  31.7 us (21%)
  waiting for transfers between devices  24.2 us (16%)
  blocking collectives  12.2 us (8%)
  local copies, waits for them, and re-layouts  2.44 us (2%)
    pallas_call x1, Pallas kernels, on_device(): pl.pallas_call(march_kernel, out_shape=jax.ShapeDtypeStruct((8, 96, LANES...  28.7 us
    ppermute x2, starting transfers between devices, on_device(): parts = [lax.ppermute(own, 'zl', up), own, lax.ppermute(own, 'zl', down)]  24 us
    all_to_all x1, starting transfers between devices, on_device(): own = lax.all_to_all(send, ('y', 'zh', 'c'), 0, 0, tiled=True)  18.6 us
    ppermute x1, starting transfers between devices, on_device(): halo = lax.ppermute(flow, ('y', 'zh', 'x'), ring)  16.8 us
    all_to_all x1, blocking collectives, on_device(): cells = lax.all_to_all(out, ('x', 'c'), 0, 0, tiled=True)  12.2 us
    ppermute x2, waiting for transfers between devices, on_device(): parts = [lax.ppermute(own, 'zl', up), own, lax.ppermute(own, 'zl', down)]  11.8 us
    ppermute x3, starting transfers between devices, on_device(): lax.ppermute(flow, 'x', [(i, (i + k) % 4) for i in range(4)])  9.09 us
    ppermute x2, starting transfers between devices, on_device(): chips = [lax.ppermute(raw, 'zl', up), raw, lax.ppermute(raw, 'zl', down)]  5.67 us
  transfers between devices with their start and end apart: 10, of which 7 were waited for; matrix products, arithmetic and copies ran while one was open for 0% of the time, Pallas kernels for 1%

profile of v5, /device:TPU:1, one launch (start us, length us, event | category | flops | bytes accessed | tf_op | source)
XLA Modules:
  0.0 148.5 jit_solution(17640497067741788400)
XLA Ops:
  0.0 0.0 copy-start
  0.0 0.0 copy-start.1
  0.0 0.8 copy-done.1
  0.8 0.0 copy-start.2
  0.8 0.9 copy-done.2
  1.7 0.0 copy-start.4
  1.7 0.7 copy-done.4
  2.4 0.6 shard_map.56
  3.0 4.4 %collective-permute-start = (f32[72,128]{1,0:T(8,128)S(1)}, f32[72,128]{1,0:T(8,128)S(1)}, u32[]{:S(2)}, u32[]{:S(2)}) collective-permute-start(f32[72,128]{1,0:T(8,128)S(1)} %shard_map.56), channel_id=1, source_target_pairs={{0,2},{2,4},{4,6},{6,8},{8,10},{10,12},{12,14},{1,3},{3,5},{5,7},{... | collective-permute-start | bytes 110600 | tf_op jit(solution)/shard_map/ppermute | solution.py:257
  7.4 1.3 collective-permute-start.1
  8.7 0.0 collective-permute-done
  8.7 3.6 %collective-permute-done.1 = f32[72,128]{1,0:T(8,128)S(1)} collective-permute-done((f32[72,128]{1,0:T(8,128)S(1)}, f32[72,128]{1,0:T(8,128)S(1)}, u32[]{:S(2)}, u32[]{:S(2)}) %collective-permute-start.1) | collective-permute-done | bytes 36896 | tf_op jit(solution)/shard_map/ppermute | solution.py:257
  12.3 16.8 %collective-permute-start.2 = (f32[144,128]{1,0:T(8,128)S(1)}, f32[144,128]{1,0:T(8,128)S(1)}, u32[]{:S(2)}, u32[]{:S(2)}) collective-permute-start(f32[144,128]{1,0:T(8,128)S(1)} %pad_maximum_fusion.1), channel_id=1, source_target_pairs={{48,112},{0,448},{112,176},{64,0},{176,240},{128,64},{240,304},{19... | collective-permute-start | bytes 221192 | tf_op jit(solution)/shard_map/ppermute | solution.py:261
  29.1 0.0 copy-done
  29.1 1.1 shard_map.55
  30.2 0.6 collective-permute-done.2
  30.8 18.6 %all-to-all-start = ((f32[16,72,128]{2,1,0:T(8,128)}), f32[16,72,128]{2,1,0:T(8,128)S(1)}, u32[]{:S(2)}, u32[]{:S(2)}) async-start(f32[16,72,128]{2,1,0:T(8,128)} %shard_map.55), calls=%async_computation | async-start | bytes 1179648 | tf_op jit(solution)/shard_map/all_to_all | solution.py:263
  49.4 1.9 %collective-permute-start.3 = (f32[288,128]{1,0:T(8,128)S(1)}, f32[288,128]{1,0:T(8,128)S(1)}, u32[]{:S(2)}, u32[]{:S(2)}) collective-permute-start(f32[288,128]{1,0:T(8,128)S(1)} %pad_maximum_fusion), channel_id=1, source_target_pairs={{0,16},{16,32},{32,48},{48,0},{1,17},{17,33},{33,49},{49,1},{2,18}... | collective-permute-start | bytes 442376 | tf_op jit(solution)/shard_map/ppermute | solution.py:265
  51.3 4.6 %collective-permute-start.5 = (f32[288,128]{1,0:T(8,128)S(1)}, f32[288,128]{1,0:T(8,128)S(1)}, u32[]{:S(2)}, u32[]{:S(2)}) collective-permute-start(f32[288,128]{1,0:T(8,128)S(1)} %pad_maximum_fusion), channel_id=1, source_target_pairs={{0,48},{16,0},{32,16},{48,32},{1,49},{17,1},{33,17},{49,33},{2,50}... | collective-permute-start | bytes 442376 | tf_op jit(solution)/shard_map/ppermute | solution.py:265
  55.9 2.6 %collective-permute-start.4 = (f32[288,128]{1,0:T(8,128)S(1)}, f32[288,128]{1,0:T(8,128)S(1)}, u32[]{:S(2)}, u32[]{:S(2)}) collective-permute-start(f32[288,128]{1,0:T(8,128)S(1)} %pad_maximum_fusion), channel_id=1, source_target_pairs={{0,32},{16,48},{32,0},{48,16},{1,33},{17,49},{33,1},{49,17},{2,34}... | collective-permute-start | bytes 442376 | tf_op jit(solution)/shard_map/ppermute | solution.py:265
  58.5 0.0 collective-permute-done.3
  58.6 5.5 %collective-permute-done.4 = f32[288,128]{1,0:T(8,128)S(1)} collective-permute-done((f32[288,128]{1,0:T(8,128)S(1)}, f32[288,128]{1,0:T(8,128)S(1)}, u32[]{:S(2)}, u32[]{:S(2)}) %collective-permute-start.4) | collective-permute-done | bytes 147488 | tf_op jit(solution)/shard_map/ppermute | solution.py:265
  64.1 0.0 collective-permute-done.5
  64.2 3.4 %collective-permute-start.6 = (f32[1224,128]{1,0:T(8,128)S(1)}, f32[1224,128]{1,0:T(8,128)S(1)}, u32[]{:S(2)}, u32[]{:S(2)}) collective-permute-start(f32[1224,128]{1,0:T(8,128)S(1)} %constant_dynamic-update-slice_fusion.strip_ref), channel_id=1, source_target_pairs={{0,1},{1,0},{2,3},{3,2},{4,5},{5,4},{6,7},{7,6},{8,9},{9,8},{10,11... | collective-permute-start | bytes 1880072 | tf_op jit(solution)/shard_map/ppermute | solution.py:267
  67.6 1.7 %collective-permute-done.6.other_ref = f32[1224,128]{1,0:T(8,128)S(1)} collective-permute-done((f32[1224,128]{1,0:T(8,128)S(1)}, f32[1224,128]{1,0:T(8,128)S(1)}, u32[]{:S(2)}, u32[]{:S(2)}) %collective-permute-start.6) | collective-permute-done | bytes 626720 | tf_op jit(solution)/shard_map/ppermute | solution.py:267
  69.3 1.1 all-to-all-done
  70.4 1.3 collective-permute-start.8
  71.7 22.7 %collective-permute-start.7 = (f32[16,72,128]{2,1,0:T(8,128)S(1)}, f32[16,72,128]{2,1,0:T(8,128)S(1)}, u32[]{:S(2)}, u32[]{:S(2)}) collective-permute-start(f32[16,72,128]{2,1,0:T(8,128)S(1)} %all-to-all-done), channel_id=1, source_target_pairs={{0,2},{2,4},{4,6},{6,8},{8,10},{10,12},{12,14},{1,3},{3,5},{5,7},{... | collective-permute-start | bytes 1769480 | tf_op jit(solution)/shard_map/ppermute | solution.py:269
  94.4 0.1 pad_add_fusion.core_ref
  94.5 10.9 %collective-permute-done.8 = f32[16,72,128]{2,1,0:T(8,128)S(1)} collective-permute-done((f32[16,72,128]{2,1,0:T(8,128)S(1)}, f32[16,72,128]{2,1,0:T(8,128)S(1)}, u32[]{:S(2)}, u32[]{:S(2)}) %collective-permute-start.8) | collective-permute-done | bytes 589856 | tf_op jit(solution)/shard_map/ppermute | solution.py:269
  105.4 0.9 collective-permute-done.7
  106.3 28.7 %shard_map.57 = f32[8,96,128]{2,1,0:T(8,128)S(1)} custom-call(s32[2]{0:T(128)S(1)} %pad_add_fusion.core_ref, f32[1152,128]{1,0:T(8,128)S(1)} %bitcast.13, f32[1152,128]{1,0:T(8,128)S(1)} %bitcast.10, f32[1152,128]{1,0:T(8,128)S(1)} %bitcast.12, f32[1224,128]{1,0:T(8,128)S(1)} %constant_dynamic-update-slice_fusion.strip_ref, ...), custom_call_target="tpu_custom_call" | custom-call | tf_op jit(solution)/shard_map/pallas_call | solution.py:271
  135.0 0.0 copy-start.3
  135.0 12.2 %all_to_all.10 = f32[8,96,128]{2,1,0:T(8,128)S(1)} all-to-all(f32[8,96,128]{2,1,0:T(8,128)S(1)} %shard_map.57), channel_id=1, replica_groups=mesh['y'=4,'zh'=2,'x'=4,'zl'=8,'c'=2] {'x','c'}, dimensions={0} | all-to-all | bytes 786432 | tf_op jit(solution)/shard_map/all_to_all | solution.py:286
  147.2 0.0 copy-done.3
  147.2 1.3 shard_map.58
  (12 shorter events, 0.1 us)
Async XLA Ops:
  0.0 29.1 %copy-start = (f32[4,3,8,1024]{3,2,1,0:T(8,128)S(1)}, f32[4,3,8,1024]{3,2,1,0:T(8,128)}, u32[]{:S(2)}) copy-start(f32[4,3,8,1024]{3,2,1,0:T(8,128)} %tan_ref.1) | copy-start | bytes 1179652
  0.0 0.8 copy-start.1
  0.8 0.9 copy-start.2
  1.7 0.7 copy-start.4
  3.0 5.7 %collective-permute-start = (f32[72,128]{1,0:T(8,128)S(1)}, f32[72,128]{1,0:T(8,128)S(1)}, u32[]{:S(2)}, u32[]{:S(2)}) collective-permute-start(f32[72,128]{1,0:T(8,128)S(1)} %shard_map.56), channel_id=1, source_target_pairs={{0,2},{2,4},{4,6},{6,8},{8,10},{10,12},{12,14},{1,3},{3,5},{5,7},{... | collective-permute-start | bytes 110600 | tf_op jit(solution)/shard_map/ppermute | solution.py:257
  7.4 4.9 %collective-permute-start.1 = (f32[72,128]{1,0:T(8,128)S(1)}, f32[72,128]{1,0:T(8,128)S(1)}, u32[]{:S(2)}, u32[]{:S(2)}) collective-permute-start(f32[72,128]{1,0:T(8,128)S(1)} %shard_map.56), channel_id=1, source_target_pairs={{2,0},{4,2},{6,4},{8,6},{10,8},{12,10},{14,12},{3,1},{5,3},{7,5},{... | collective-permute-start | bytes 110600 | tf_op jit(solution)/shard_map/ppermute | solution.py:257
  12.3 18.5 %collective-permute-start.2 = (f32[144,128]{1,0:T(8,128)S(1)}, f32[144,128]{1,0:T(8,128)S(1)}, u32[]{:S(2)}, u32[]{:S(2)}) collective-permute-start(f32[144,128]{1,0:T(8,128)S(1)} %pad_maximum_fusion.1), channel_id=1, source_target_pairs={{48,112},{0,448},{112,176},{64,0},{176,240},{128,64},{240,304},{19... | collective-permute-start | bytes 221192 | tf_op jit(solution)/shard_map/ppermute | solution.py:261
  30.8 39.6 %all-to-all-start = ((f32[16,72,128]{2,1,0:T(8,128)}), f32[16,72,128]{2,1,0:T(8,128)S(1)}, u32[]{:S(2)}, u32[]{:S(2)}) async-start(f32[16,72,128]{2,1,0:T(8,128)} %shard_map.55), calls=%async_computation | async-start | bytes 1179648 | tf_op jit(solution)/shard_map/all_to_all | solution.py:263
  49.4 9.1 %collective-permute-start.3 = (f32[288,128]{1,0:T(8,128)S(1)}, f32[288,128]{1,0:T(8,128)S(1)}, u32[]{:S(2)}, u32[]{:S(2)}) collective-permute-start(f32[288,128]{1,0:T(8,128)S(1)} %pad_maximum_fusion), channel_id=1, source_target_pairs={{0,16},{16,32},{32,48},{48,0},{1,17},{17,33},{33,49},{49,1},{2,18}... | collective-permute-start | bytes 442376 | tf_op jit(solution)/shard_map/ppermute | solution.py:265
  51.3 12.8 %collective-permute-start.5 = (f32[288,128]{1,0:T(8,128)S(1)}, f32[288,128]{1,0:T(8,128)S(1)}, u32[]{:S(2)}, u32[]{:S(2)}) collective-permute-start(f32[288,128]{1,0:T(8,128)S(1)} %pad_maximum_fusion), channel_id=1, source_target_pairs={{0,48},{16,0},{32,16},{48,32},{1,49},{17,1},{33,17},{49,33},{2,50}... | collective-permute-start | bytes 442376 | tf_op jit(solution)/shard_map/ppermute | solution.py:265
  55.9 8.2 %collective-permute-start.4 = (f32[288,128]{1,0:T(8,128)S(1)}, f32[288,128]{1,0:T(8,128)S(1)}, u32[]{:S(2)}, u32[]{:S(2)}) collective-permute-start(f32[288,128]{1,0:T(8,128)S(1)} %pad_maximum_fusion), channel_id=1, source_target_pairs={{0,32},{16,48},{32,0},{48,16},{1,33},{17,49},{33,1},{49,17},{2,34}... | collective-permute-start | bytes 442376 | tf_op jit(solution)/shard_map/ppermute | solution.py:265
  64.2 5.1 %collective-permute-start.6 = (f32[1224,128]{1,0:T(8,128)S(1)}, f32[1224,128]{1,0:T(8,128)S(1)}, u32[]{:S(2)}, u32[]{:S(2)}) collective-permute-start(f32[1224,128]{1,0:T(8,128)S(1)} %constant_dynamic-update-slice_fusion.strip_ref), channel_id=1, source_target_pairs={{0,1},{1,0},{2,3},{3,2},{4,5},{5,4},{6,7},{7,6},{8,9},{9,8},{10,11... | collective-permute-start | bytes 1880072 | tf_op jit(solution)/shard_map/ppermute | solution.py:267
  70.4 35.0 %collective-permute-start.8 = (f32[16,72,128]{2,1,0:T(8,128)S(1)}, f32[16,72,128]{2,1,0:T(8,128)S(1)}, u32[]{:S(2)}, u32[]{:S(2)}) collective-permute-start(f32[16,72,128]{2,1,0:T(8,128)S(1)} %all-to-all-done), channel_id=1, source_target_pairs={{2,0},{4,2},{6,4},{8,6},{10,8},{12,10},{14,12},{3,1},{5,3},{7,5},{... | collective-permute-start | bytes 1769480 | tf_op jit(solution)/shard_map/ppermute | solution.py:269
  71.7 34.6 %collective-permute-start.7 = (f32[16,72,128]{2,1,0:T(8,128)S(1)}, f32[16,72,128]{2,1,0:T(8,128)S(1)}, u32[]{:S(2)}, u32[]{:S(2)}) collective-permute-start(f32[16,72,128]{2,1,0:T(8,128)S(1)} %all-to-all-done), channel_id=1, source_target_pairs={{0,2},{2,4},{4,6},{6,8},{8,10},{10,12},{12,14},{1,3},{3,5},{5,7},{... | collective-permute-start | bytes 1769480 | tf_op jit(solution)/shard_map/ppermute | solution.py:269
  135.0 12.2 %copy-start.3 = (f32[128,128]{1,0:T(8,128)S(1)}, f32[128,128]{1,0:T(8,128)}, u32[]{:S(2)}) copy-start(f32[128,128]{1,0:T(8,128)} %coef_ref.1) | copy-start | bytes 196612

commit v6 on v5

--- a/solution.py
+++ b/solution.py
@@ -75,8 +75,28 @@
     lax.fori_loop(0, 3, fields, None)
 
 
+def from_block(me, x):
+    return lax.rem(me - x + 4, 4) * 216
+
+
+def border_kernel(core_ref, strip_ref, other_ref, to_right_ref, to_left_ref):
+    early = lax.broadcasted_iota(jnp.int32, (8, LANES), 1) % 32 < 16
+    core, me = core_ref[0], core_ref[1]
+    head, last = from_block(me, 0), from_block(me, 3)
+    for other, ref in enumerate((strip_ref, other_ref)):
+        which = 1 - core if other else core
+        for z in range(3):
+            for f in range(3):
+                to = pl.ds(pl.multiple_of((which * 3 + z) * 24 + f * 8, 8), 8)
+                rows = [z * 72 + high * 24 + f * 8 for high in range(2)]
+                a, b = (ref[pl.ds(pl.multiple_of(last + k, 8), 8), :] for k in rows)
+                to_right_ref[to, :] = jnp.where(early, pltpu.roll(a, LANES - 16, 1), b)
+                a, b = (ref[pl.ds(pl.multiple_of(head + k, 8), 8), :] for k in rows)
+                to_left_ref[to, :] = jnp.where(early, a, pltpu.roll(b, 16, 1))
+
+
 def march_kernel(
-    core_ref, prev_ref, own_ref, next_ref, strip_ref, other_ref,
+    core_ref, prev_ref, own_ref, next_ref, strip_ref, other_ref, left_ref, right_ref,
     out_ref, state, middle, base, wet, coef, turn,
 ):
     lane = lax.broadcasted_iota(jnp.int32, (8, LANES), 1)
@@ -90,35 +110,37 @@
 
     lax.fori_loop(0, PAIRS, place, None)
     core, me = core_ref[0], core_ref[1]
-    blocks = [lax.rem(me - x + 4, 4) * 288 for x in range(4)]
-    places = blocks + [blocks[3] + 144, blocks[0] + 144]
+    blocks = [from_block(me, x) for x in range(4)]
     strips = []
     for other, ref in enumerate((strip_ref, other_ref)):
         for z in range(3):
-            top = pl.multiple_of((1 - core if other else core) * 8 + z * 16, 8)
-            strips.append((ref, z * 48, top))
+            which = 1 - core if other else core
+            top = pl.multiple_of(which * 8 + z * 16, 8)
+            strips.append((ref, z * 72, (which * 3 + z) * 24, top))
             for v in range(3):
-                at = 1152 + z * 24 + v * 8
+                at = z * 72 + 48 + v * 8
                 wet[v, pl.ds(top, 8), :] = ref[at : at + 8, :] * 0.25
 
-    def unpack(part, _):
-        high, f = part // 3, part % 3
-        for ref, first, top in strips:
-            quads = [ref[pl.ds(pl.multiple_of(first + at + part * 8, 8), 8), :] for at in places]
-            for low in range(4):
-                out = pltpu.roll(quads[0], (128 - 32 * low) % 128, 1) if low else quads[0]
-                for x in range(1, 4):
-                    turned = pltpu.roll(quads[x], 32 * (x - low) % 128, 1) if x != low else quads[x]
-                    out = jnp.where(lane >= 32 * x, turned, out)
-                left = pltpu.roll(quads[4], (96 - 32 * low) % 128, 1)
-                right = pltpu.roll(quads[5], (128 - 32 * low) % 128, 1)
-                halo = edges(left, right, pltpu.roll(left, 64, 1), pltpu.roll(right, 64, 1), lane)
-                rows = pl.ds(top + 8, 8)
-                base[high * 4 + low, f, 0, rows, :] = out
-                base[high * 4 + low, f, 1, rows, :] = pltpu.roll(out, 64, 1)
-                base[high * 4 + low, f, 2, rows, :] = halo
-
-    lax.fori_loop(0, 6, unpack, None)
+    def unpack(f, _):
+        for ref, first, border, top in strips:
+            at = pl.multiple_of(border + f * 8, 8)
+            left, right = left_ref[pl.ds(at, 8), :], right_ref[pl.ds(at, 8), :]
+            for high in range(2):
+                quads = [ref[pl.ds(pl.multiple_of(first + at + high * 24 + f * 8, 8), 8), :] for at in blocks]
+                for low in range(4):
+                    out = pltpu.roll(quads[0], (128 - 32 * low) % 128, 1) if low else quads[0]
+                    for x in range(1, 4):
+                        turned = pltpu.roll(quads[x], 32 * (x - low) % 128, 1) if x != low else quads[x]
+                        out = jnp.where(lane >= 32 * x, turned, out)
+                    shift = low * 32 + high * 16
+                    sides = [pltpu.roll(cells, (to - shift) % 128, 1) if to != shift else cells
+                             for to, cells in ((112, left), (0, right), (48, left), (64, right))]
+                    rows = pl.ds(top + 8, 8)
+                    base[high * 4 + low, f, 0, rows, :] = out
+                    base[high * 4 + low, f, 1, rows, :] = pltpu.roll(out, 64, 1)
+                    base[high * 4 + low, f, 2, rows, :] = edges(*sides, lane)
+
+    lax.fori_loop(0, 3, unpack, None)
 
     def prepare(step, tile):
         top = pl.multiple_of(tile * 8, 8)
@@ -254,24 +276,29 @@
     )(tangents, land_mask)
     up = [(i, i + 1) for i in range(7)]
     down = [(i + 1, i) for i in range(7)]
-    chips = [lax.ppermute(raw, "zl", up), raw, lax.ppermute(raw, "zl", down)]
-    flow = jnp.concatenate([x[:48] for x in chips], axis=0)
-    wet = [x[48:] for x in chips]
-    ring = [(s * 4 + x, (s + step) % 8 * 4 + x) for s in range(8) for x, step in ((3, 1), (0, -1))]
-    halo = lax.ppermute(flow, ("y", "zh", "x"), ring)
-    send, halo = lax.optimization_barrier((send, halo))
     own = lax.all_to_all(send, ("y", "zh", "c"), 0, 0, tiled=True)
-    flow = jnp.concatenate([flow, halo], axis=0)
-    flows = [lax.ppermute(flow, "x", [(i, (i + k) % 4) for i in range(4)]) for k in (1, 2, 3)]
-    strip = jnp.concatenate([flow, *flows, *wet], axis=0)
+    chips = jnp.concatenate([lax.ppermute(raw, "zl", up), raw, lax.ppermute(raw, "zl", down)], axis=0)
+    strip = jnp.concatenate(
+        [chips] + [lax.ppermute(chips, "x", [(i, (i + k) % 4) for i in range(4)]) for k in (1, 2, 3)], axis=0
+    )
     other = lax.ppermute(strip, "c", [(0, 1), (1, 0)])
-    own, other = lax.optimization_barrier((own, other))
+    here = jnp.stack([core, lax.axis_index("x")]).astype(jnp.int32)
+    borders = pl.pallas_call(
+        border_kernel,
+        out_shape=(jax.ShapeDtypeStruct((144, LANES), f32), jax.ShapeDtypeStruct((144, LANES), f32)),
+        in_specs=[SMEM, VMEM, VMEM],
+        out_specs=(VMEM, VMEM),
+        compiler_params=pltpu.CompilerParams(vmem_limit_bytes=16 * 2**20),
+    )(here, strip, other)
+    own, borders = lax.optimization_barrier((own, borders))
     parts = [lax.ppermute(own, "zl", up), own, lax.ppermute(own, "zl", down)]
+    left = lax.ppermute(borders[0], ("y", "zh"), [(i, (i + 1) % 8) for i in range(8)])
+    right = lax.ppermute(borders[1], ("y", "zh"), [((i + 1) % 8, i) for i in range(8)])
     parts = [x.reshape(PEERS * 72, LANES) for x in parts]
     out = pl.pallas_call(
         march_kernel,
         out_shape=jax.ShapeDtypeStruct((8, 96, LANES), f32),
-        in_specs=[SMEM] + [VMEM] * 5,
+        in_specs=[SMEM] + [VMEM] * 7,
         out_specs=VMEM,
         scratch_shapes=[
             pltpu.VMEM((3, PAIRS, 3, TALL + 8, LANES), f32),
@@ -282,7 +309,7 @@
             pltpu.VMEM((2, 2, 64, LANES), f32),
         ],
         compiler_params=pltpu.CompilerParams(vmem_limit_bytes=32 * 2**20),
-    )(jnp.stack([core, lax.axis_index("x")]).astype(jnp.int32), *parts, strip, other)
+    )(here, *parts, strip, other, left, right)
     cells = lax.all_to_all(out, ("x", "c"), 0, 0, tiled=True)
     mixed = pl.pallas_call(
         mix_kernel,

time: 149 us -> 158 us (1.060)
  waiting for transfers between devices: 24.2 us -> 47.2 us
  starting transfers between devices: 77.6 us -> 58.9 us
  Pallas kernels: 31.7 us -> 34.7 us
    ppermute x6 -> x7, waiting for transfers between devices: 9.64 us -> 45.9 us  [the longest x1 21.5 us: on_device(): lax.ppermute(raw, 'zl', down)]
    ppermute x2, starting transfers between devices: 24 us -> 5.32 us  [on_device(): parts = [lax.ppermute(own, 'zl', up), own, lax.ppermute(own, 'zl', down)]]
    ppermute x2, waiting for transfers between devices: 11.8 us -> 0.01 us  [on_device(): parts = [lax.ppermute(own, 'zl', up), own, lax.ppermute(own, 'zl', down)]]
    pallas_call x1, Pallas kernels: 28.7 us -> 31.1 us  [on_device(): pl.pallas_call(march_kernel, out_shape=jax.ShapeDtypeStruct((8, 96, LANES...]
    ppermute x6 -> x7, starting transfers between devices: 31.6 us -> 30.7 us  [the longest x1 11.9 us: on_device(): lax.ppermute(borders[0], ('y', 'zh'), [(i, (i + 1) % 8) for i in range(8)])]
  transfers between devices with their start and end apart: 10 -> 11, of which waited for: 7 -> 4; matrix products, arithmetic and copies ran while one was open for 0% -> 0% of each run, Pallas kernels for 1% -> 1%
where the time goes in v6:
time: 158 us; the launch traced here: 157 us
  starting transfers between devices  58.9 us (37%)
  waiting for transfers between devices  47.2 us (30%)
  Pallas kernels  34.7 us (22%)
  blocking collectives  13.4 us (8%)
  local copies, waits for them, and re-layouts  2.44 us (2%)
    pallas_call x1, Pallas kernels, on_device(): pl.pallas_call(march_kernel, out_shape=jax.ShapeDtypeStruct((8, 96, LANES...  31.1 us
    ppermute x1, waiting for transfers between devices, on_device(): lax.ppermute(raw, 'zl', down)  21.5 us
    ppermute x1, waiting for transfers between devices, on_device(): lax.ppermute(borders[0], ('y', 'zh'), [(i, (i + 1) % 8) for i in range(8)])  19.5 us
    all_to_all x1, starting transfers between devices, on_device(): own = lax.all_to_all(send, ('y', 'zh', 'c'), 0, 0, tiled=True)  19.4 us
    all_to_all x1, blocking collectives, on_device(): cells = lax.all_to_all(out, ('x', 'c'), 0, 0, tiled=True)  13.4 us
    ppermute x1, starting transfers between devices, on_device(): lax.ppermute(borders[0], ('y', 'zh'), [(i, (i + 1) % 8) for i in range(8)])  11.9 us
    ppermute x3, starting transfers between devices, on_device(): lax.ppermute(chips, 'x', [(i, (i + k) % 4) for i in range(4)])  9.33 us
    ppermute x2, starting transfers between devices, on_device(): parts = [lax.ppermute(own, 'zl', up), own, lax.ppermute(own, 'zl', down)]  5.32 us
  transfers between devices with their start and end apart: 11, of which 4 were waited for; matrix products, arithmetic and copies ran while one was open for 0% of the time, Pallas kernels for 1%

profile of v6, /device:TPU:1, one launch (start us, length us, event | category | flops | bytes accessed | tf_op | source)
XLA Modules:
  0.0 157.0 jit_solution(7056018517490373373)
XLA Ops:
  0.0 0.0 copy-start
  0.0 1.0 copy-done
  1.0 0.0 copy-start.1
  1.0 0.8 copy-done.1
  1.8 1.1 shard_map.55
  2.8 0.0 copy-start.2
  2.9 0.0 copy-start.3
  2.9 19.4 %all-to-all-start = ((f32[16,72,128]{2,1,0:T(8,128)}), f32[16,72,128]{2,1,0:T(8,128)S(1)}, u32[]{:S(2)}, u32[]{:S(2)}) async-start(f32[16,72,128]{2,1,0:T(8,128)} %shard_map.55), calls=%async_computation | async-start | bytes 1179648 | tf_op jit(solution)/shard_map/all_to_all | solution.py:279
  22.2 0.0 copy-start.5
  22.2 0.0 copy-done.2
  22.2 0.0 copy-done.3
  22.2 0.6 copy-done.5
  22.9 0.6 shard_map.56
  23.5 1.3 collective-permute-start.1
  24.8 4.0 %collective-permute-start = (f32[72,128]{1,0:T(8,128)S(1)}, f32[72,128]{1,0:T(8,128)S(1)}, u32[]{:S(2)}, u32[]{:S(2)}) collective-permute-start(f32[72,128]{1,0:T(8,128)S(1)} %shard_map.56), channel_id=1, source_target_pairs={{0,2},{2,4},{4,6},{6,8},{8,10},{10,12},{12,14},{1,3},{3,5},{5,7},{... | collective-permute-start | bytes 110600 | tf_op jit(solution)/shard_map/ppermute | solution.py:280
  28.8 21.5 %collective-permute-done.1 = f32[72,128]{1,0:T(8,128)S(1)} collective-permute-done((f32[72,128]{1,0:T(8,128)S(1)}, f32[72,128]{1,0:T(8,128)S(1)}, u32[]{:S(2)}, u32[]{:S(2)}) %collective-permute-start.1) | collective-permute-done | bytes 36896 | tf_op jit(solution)/shard_map/ppermute | solution.py:280
  50.3 0.0 collective-permute-done
  50.3 4.4 %collective-permute-start.4 = (f32[216,128]{1,0:T(8,128)S(1)}, f32[216,128]{1,0:T(8,128)S(1)}, u32[]{:S(2)}, u32[]{:S(2)}) collective-permute-start(f32[216,128]{1,0:T(8,128)S(1)} %pad_maximum_fusion), channel_id=1, source_target_pairs={{0,48},{16,0},{32,16},{48,32},{1,49},{17,1},{33,17},{49,33},{2,50}... | collective-permute-start | bytes 331784 | tf_op jit(solution)/shard_map/ppermute | solution.py:282
  54.7 2.4 %collective-permute-start.3 = (f32[216,128]{1,0:T(8,128)S(1)}, f32[216,128]{1,0:T(8,128)S(1)}, u32[]{:S(2)}, u32[]{:S(2)}) collective-permute-start(f32[216,128]{1,0:T(8,128)S(1)} %pad_maximum_fusion), channel_id=1, source_target_pairs={{0,32},{16,48},{32,0},{48,16},{1,33},{17,49},{33,1},{49,17},{2,34}... | collective-permute-start | bytes 331784 | tf_op jit(solution)/shard_map/ppermute | solution.py:282
  57.2 2.5 %collective-permute-start.2 = (f32[216,128]{1,0:T(8,128)S(1)}, f32[216,128]{1,0:T(8,128)S(1)}, u32[]{:S(2)}, u32[]{:S(2)}) collective-permute-start(f32[216,128]{1,0:T(8,128)S(1)} %pad_maximum_fusion), channel_id=1, source_target_pairs={{0,16},{16,32},{32,48},{48,0},{1,17},{17,33},{33,49},{49,1},{2,18}... | collective-permute-start | bytes 331784 | tf_op jit(solution)/shard_map/ppermute | solution.py:282
  59.7 5.0 %collective-permute-done.2 = f32[216,128]{1,0:T(8,128)S(1)} collective-permute-done((f32[216,128]{1,0:T(8,128)S(1)}, f32[216,128]{1,0:T(8,128)S(1)}, u32[]{:S(2)}, u32[]{:S(2)}) %collective-permute-start.2) | collective-permute-done | bytes 110624 | tf_op jit(solution)/shard_map/ppermute | solution.py:282
  64.7 0.0 collective-permute-done.3
  64.7 0.0 collective-permute-done.4
  64.8 3.5 %collective-permute-start.5 = (f32[864,128]{1,0:T(8,128)S(1)}, f32[864,128]{1,0:T(8,128)S(1)}, u32[]{:S(2)}, u32[]{:S(2)}) collective-permute-start(f32[864,128]{1,0:T(8,128)S(1)} %constant_dynamic-update-slice_fusion.strip_ref), channel_id=1, source_target_pairs={{0,1},{1,0},{2,3},{3,2},{4,5},{5,4},{6,7},{7,6},{8,9},{9,8},{10,11... | collective-permute-start | bytes 1327112 | tf_op jit(solution)/shard_map/ppermute | solution.py:284
  68.2 0.1 pad_add_fusion.core_ref
  68.3 1.3 collective-permute-done.5.other_ref
  69.6 0.7 shard_map.57
  70.3 0.0 all-to-all-done
  70.3 1.3 collective-permute-start.7
  71.6 4.0 %collective-permute-start.6 = (f32[16,72,128]{2,1,0:T(8,128)S(1)}, f32[16,72,128]{2,1,0:T(8,128)S(1)}, u32[]{:S(2)}, u32[]{:S(2)}) collective-permute-start(f32[16,72,128]{2,1,0:T(8,128)S(1)} %all-to-all-done), channel_id=1, source_target_pairs={{0,2},{2,4},{4,6},{6,8},{8,10},{10,12},{12,14},{1,3},{3,5},{5,7},{... | collective-permute-start | bytes 1769480 | tf_op jit(solution)/shard_map/ppermute | solution.py:294
  75.6 11.9 %collective-permute-start.8 = (f32[144,128]{1,0:T(8,128)S(1)}, f32[144,128]{1,0:T(8,128)S(1)}, u32[]{:S(2)}, u32[]{:S(2)}) collective-permute-start(f32[144,128]{1,0:T(8,128)S(1)} %get-tuple-element.13), channel_id=1, source_target_pairs={{0,64},{64,128},{128,192},{192,256},{256,320},{320,384},{384,448},... | collective-permute-start | bytes 221192 | tf_op jit(solution)/shard_map/ppermute | solution.py:295
  87.5 4.2 %collective-permute-start.9 = (f32[144,128]{1,0:T(8,128)S(1)}, f32[144,128]{1,0:T(8,128)S(1)}, u32[]{:S(2)}, u32[]{:S(2)}) collective-permute-start(f32[144,128]{1,0:T(8,128)S(1)} %get-tuple-element.14), channel_id=1, source_target_pairs={{64,0},{128,64},{192,128},{256,192},{320,256},{384,320},{448,384},... | collective-permute-start | bytes 221192 | tf_op jit(solution)/shard_map/ppermute | solution.py:296
  91.8 19.5 %collective-permute-done.8.left_ref = f32[144,128]{1,0:T(8,128)S(1)} collective-permute-done((f32[144,128]{1,0:T(8,128)S(1)}, f32[144,128]{1,0:T(8,128)S(1)}, u32[]{:S(2)}, u32[]{:S(2)}) %collective-permute-start.8) | collective-permute-done | bytes 73760 | tf_op jit(solution)/shard_map/ppermute | solution.py:295
  111.2 0.0 collective-permute-done.9.right_ref
  111.2 0.0 collective-permute-done.7
  111.2 0.0 collective-permute-done.6
  111.2 31.1 %shard_map.58 = f32[8,96,128]{2,1,0:T(8,128)S(1)} custom-call(s32[2]{0:T(128)S(1)} %pad_add_fusion.core_ref, f32[1152,128]{1,0:T(8,128)S(1)} %bitcast.13, f32[1152,128]{1,0:T(8,128)S(1)} %bitcast.10, f32[1152,128]{1,0:T(8,128)S(1)} %bitcast.12, f32[864,128]{1,0:T(8,128)S(1)} %constant_dynamic-update-slice_fusion.strip_ref, ...), custom_call_target="tpu_custom_call" | custom-call | tf_op jit(solution)/shard_map/pallas_call | solution.py:298
  142.3 0.0 copy-start.4
  142.3 13.4 %all_to_all.10 = f32[8,96,128]{2,1,0:T(8,128)S(1)} all-to-all(f32[8,96,128]{2,1,0:T(8,128)S(1)} %shard_map.58), channel_id=1, replica_groups=mesh['y'=4,'zh'=2,'x'=4,'zl'=8,'c'=2] {'x','c'}, dimensions={0} | all-to-all | bytes 786432 | tf_op jit(solution)/shard_map/all_to_all | solution.py:313
  155.7 0.0 copy-done.4
  155.7 1.3 shard_map.59
  (7 shorter events, 0.1 us)
Async XLA Ops:
  0.0 1.0 copy-start
  1.0 0.8 copy-start.1
  2.8 19.4 %copy-start.2 = (s32[8,1024]{1,0:T(8,128)S(1)}, s32[8,1024]{1,0:T(8,128)}, u32[]{:S(2)}) copy-start(s32[8,1024]{1,0:T(8,128)} %mask_ref.3) | copy-start | bytes 98308
  2.9 19.4 %copy-start.3 = (f32[8,3,8,32]{3,2,1,0:T(8,128)S(1)}, f32[8,3,8,32]{3,2,1,0:T(8,128)}, u32[]{:S(2)}) copy-start(f32[8,3,8,32]{3,2,1,0:T(8,128)} %base_ref.1) | copy-start | bytes 73732
  2.9 67.4 %all-to-all-start = ((f32[16,72,128]{2,1,0:T(8,128)}), f32[16,72,128]{2,1,0:T(8,128)S(1)}, u32[]{:S(2)}, u32[]{:S(2)}) async-start(f32[16,72,128]{2,1,0:T(8,128)} %shard_map.55), calls=%async_computation | async-start | bytes 1179648 | tf_op jit(solution)/shard_map/all_to_all | solution.py:279
  22.2 0.7 copy-start.5
  23.5 26.8 %collective-permute-start.1 = (f32[72,128]{1,0:T(8,128)S(1)}, f32[72,128]{1,0:T(8,128)S(1)}, u32[]{:S(2)}, u32[]{:S(2)}) collective-permute-start(f32[72,128]{1,0:T(8,128)S(1)} %shard_map.56), channel_id=1, source_target_pairs={{2,0},{4,2},{6,4},{8,6},{10,8},{12,10},{14,12},{3,1},{5,3},{7,5},{... | collective-permute-start | bytes 110600 | tf_op jit(solution)/shard_map/ppermute | solution.py:280
  24.8 25.5 %collective-permute-start = (f32[72,128]{1,0:T(8,128)S(1)}, f32[72,128]{1,0:T(8,128)S(1)}, u32[]{:S(2)}, u32[]{:S(2)}) collective-permute-start(f32[72,128]{1,0:T(8,128)S(1)} %shard_map.56), channel_id=1, source_target_pairs={{0,2},{2,4},{4,6},{6,8},{8,10},{10,12},{12,14},{1,3},{3,5},{5,7},{... | collective-permute-start | bytes 110600 | tf_op jit(solution)/shard_map/ppermute | solution.py:280
  50.3 14.4 %collective-permute-start.4 = (f32[216,128]{1,0:T(8,128)S(1)}, f32[216,128]{1,0:T(8,128)S(1)}, u32[]{:S(2)}, u32[]{:S(2)}) collective-permute-start(f32[216,128]{1,0:T(8,128)S(1)} %pad_maximum_fusion), channel_id=1, source_target_pairs={{0,48},{16,0},{32,16},{48,32},{1,49},{17,1},{33,17},{49,33},{2,50}... | collective-permute-start | bytes 331784 | tf_op jit(solution)/shard_map/ppermute | solution.py:282
  54.7 10.0 %collective-permute-start.3 = (f32[216,128]{1,0:T(8,128)S(1)}, f32[216,128]{1,0:T(8,128)S(1)}, u32[]{:S(2)}, u32[]{:S(2)}) collective-permute-start(f32[216,128]{1,0:T(8,128)S(1)} %pad_maximum_fusion), channel_id=1, source_target_pairs={{0,32},{16,48},{32,0},{48,16},{1,33},{17,49},{33,1},{49,17},{2,34}... | collective-permute-start | bytes 331784 | tf_op jit(solution)/shard_map/ppermute | solution.py:282
  57.2 7.5 %collective-permute-start.2 = (f32[216,128]{1,0:T(8,128)S(1)}, f32[216,128]{1,0:T(8,128)S(1)}, u32[]{:S(2)}, u32[]{:S(2)}) collective-permute-start(f32[216,128]{1,0:T(8,128)S(1)} %pad_maximum_fusion), channel_id=1, source_target_pairs={{0,16},{16,32},{32,48},{48,0},{1,17},{17,33},{33,49},{49,1},{2,18}... | collective-permute-start | bytes 331784 | tf_op jit(solution)/shard_map/ppermute | solution.py:282
  64.8 4.9 %collective-permute-start.5 = (f32[864,128]{1,0:T(8,128)S(1)}, f32[864,128]{1,0:T(8,128)S(1)}, u32[]{:S(2)}, u32[]{:S(2)}) collective-permute-start(f32[864,128]{1,0:T(8,128)S(1)} %constant_dynamic-update-slice_fusion.strip_ref), channel_id=1, source_target_pairs={{0,1},{1,0},{2,3},{3,2},{4,5},{5,4},{6,7},{7,6},{8,9},{9,8},{10,11... | collective-permute-start | bytes 1327112 | tf_op jit(solution)/shard_map/ppermute | solution.py:284
  70.3 40.9 %collective-permute-start.7 = (f32[16,72,128]{2,1,0:T(8,128)S(1)}, f32[16,72,128]{2,1,0:T(8,128)S(1)}, u32[]{:S(2)}, u32[]{:S(2)}) collective-permute-start(f32[16,72,128]{2,1,0:T(8,128)S(1)} %all-to-all-done), channel_id=1, source_target_pairs={{2,0},{4,2},{6,4},{8,6},{10,8},{12,10},{14,12},{3,1},{5,3},{7,5},{... | collective-permute-start | bytes 1769480 | tf_op jit(solution)/shard_map/ppermute | solution.py:294
  71.6 39.6 %collective-permute-start.6 = (f32[16,72,128]{2,1,0:T(8,128)S(1)}, f32[16,72,128]{2,1,0:T(8,128)S(1)}, u32[]{:S(2)}, u32[]{:S(2)}) collective-permute-start(f32[16,72,128]{2,1,0:T(8,128)S(1)} %all-to-all-done), channel_id=1, source_target_pairs={{0,2},{2,4},{4,6},{6,8},{8,10},{10,12},{12,14},{1,3},{3,5},{5,7},{... | collective-permute-start | bytes 1769480 | tf_op jit(solution)/shard_map/ppermute | solution.py:294
  75.6 35.6 %collective-permute-start.8 = (f32[144,128]{1,0:T(8,128)S(1)}, f32[144,128]{1,0:T(8,128)S(1)}, u32[]{:S(2)}, u32[]{:S(2)}) collective-permute-start(f32[144,128]{1,0:T(8,128)S(1)} %get-tuple-element.13), channel_id=1, source_target_pairs={{0,64},{64,128},{128,192},{192,256},{256,320},{320,384},{384,448},... | collective-permute-start | bytes 221192 | tf_op jit(solution)/shard_map/ppermute | solution.py:295
  87.5 23.7 %collective-permute-start.9 = (f32[144,128]{1,0:T(8,128)S(1)}, f32[144,128]{1,0:T(8,128)S(1)}, u32[]{:S(2)}, u32[]{:S(2)}) collective-permute-start(f32[144,128]{1,0:T(8,128)S(1)} %get-tuple-element.14), channel_id=1, source_target_pairs={{64,0},{128,64},{192,128},{256,192},{320,256},{384,320},{448,384},... | collective-permute-start | bytes 221192 | tf_op jit(solution)/shard_map/ppermute | solution.py:296
  142.3 13.4 %copy-start.4 = (f32[128,128]{1,0:T(8,128)S(1)}, f32[128,128]{1,0:T(8,128)}, u32[]{:S(2)}) copy-start(f32[128,128]{1,0:T(8,128)} %coef_ref.1) | copy-start | bytes 196612

commit v7 on v5

v7 whole, which is shorter than its diff:
```python
import jax
import jax.numpy as jnp
from jax import lax
from jax.experimental import pallas as pl
from jax.experimental.pallas import tpu as pltpu
from jax.sharding import PartitionSpec as P

SIZES = (4, 2, 4, 8, 2)
AXES = ("y", "zh", "x", "zl", "c")
STEPS = 8
LANES = 128
HALO = 16
STRIP = 16
TALL = STRIP + 2 * HALO
PEERS = 16
COEFS = 15
QUADS = 4
GROUP = 4
f32 = jnp.float32


PARTS = 5


def halo_columns(left, right, lane):
    return jnp.where(lane >= 112, left, right)


def spread(inner, halo, part, lane):
    column = (lane % 32) * PARTS + (part - HALO)
    index = (column + LANES) % LANES
    a, b = (jnp.take_along_axis(x, index, axis=1) for x in (inner, halo))
    return jnp.where((column >= 0) & (column < LANES), a, b)


def gathered(parts, quarter, lane):
    column = lane + HALO
    index, rest = column // PARTS + quarter * 32, column % PARTS
    out = jnp.take_along_axis(parts[0], index, axis=1)
    for j in range(1, PARTS):
        out = jnp.where(rest == j, jnp.take_along_axis(parts[j], index, axis=1), out)
    return out


def from_right(cells):
    return [*cells[1:], pltpu.roll(cells[0], LANES - 1, 1)]


def from_left(cells):
    return [pltpu.roll(cells[-1], 1, 1), *cells[:-1]]


def flow_kernel(block_ref, order_ref, base_ref, mask_ref, raw_ref):
    lane = lax.broadcasted_iota(jnp.int32, (8, LANES), 1)
    s = block_ref[0]
    for high in range(2):
        for f in range(3):
            flow = jnp.concatenate([base_ref[order_ref[high * 4 + low], f] for low in range(4)], axis=1)
            raw_ref[(high * 3 + f) * 8 : (high * 3 + f) * 8 + 8, :] = flow

    def column(k):
        return mask_ref[:, pl.ds(pl.multiple_of(k * LANES, LANES), LANES)].astype(f32)

    raw_ref[48:56, :] = column(s)
    raw_ref[56:64, :] = halo_columns(column(lax.rem(s + 7, 8)), column(lax.rem(s + 1, 8)), lane)


def pack_kernel(tan_ref, mask_ref, send_ref):
    lane = lax.broadcasted_iota(jnp.int32, (8, LANES), 1)
    wet = [mask_ref[:, k * LANES : (k + 1) * LANES].astype(f32) for k in range(8)]

    def send(core, _):
        cells = [
            [[tan_ref[2 * core + q, f, :, k * LANES : (k + 1) * LANES] * wet[k] for k in range(8)] for f in range(3)]
            for q in range(2)
        ]
        for k in range(8):
            lines = []
            for f in range(3):
                for j in range(PARTS):
                    for q in range(2):
                        row = cells[q][f]
                        halo = halo_columns(row[(k + 7) % 8], row[(k + 1) % 8], lane)
                        lines.append(spread(row[k], halo, j, lane))
            lines += lines[:2]
            for i in range(8):
                a, b, c, d = lines[4 * i : 4 * i + 4]
                out = jnp.where(lane < 32, a, jnp.where(lane < 64, b, jnp.where(lane < 96, c, d)))
                send_ref[2 * k + core, i * 8 : i * 8 + 8, :] = out

    lax.fori_loop(0, 2, send, None)


def march_kernel(
    core_ref, prev_ref, own_ref, next_ref, strip_ref, other_ref,
    out_ref, state, middle, base, wet, coef, turn,
):
    lane = lax.broadcasted_iota(jnp.int32, (8, LANES), 1)
    def place(quad, _):
        for z, ref in enumerate((prev_ref, own_ref, next_ref)):
            for c in range(2):
                for f in range(3):
                    for j in range(PARTS):
                        i, odd = divmod(f * PARTS + j, 2)
                        one, two = (
                            ref[pl.ds(pl.multiple_of((4 * quad + 2 * p + c) * 64 + i * 8, 8), 8), :] for p in range(2)
                        )
                        one, two = (pltpu.roll(one, 64, 1), two) if odd else (one, pltpu.roll(two, 64, 1))
                        rows = slice(z * 16 + c * 8, z * 16 + c * 8 + 8)
                        state[f, quad, j, rows, :] = jnp.where(lane < 64, one, two)

    lax.fori_loop(0, QUADS, place, None)
    core, me = core_ref[0], core_ref[1]
    blocks = [lax.rem(me - x + 4, 4) * 288 for x in range(4)]
    places = blocks + [blocks[3] + 144, blocks[0] + 144]
    strips = []
    for other, ref in enumerate((strip_ref, other_ref)):
        for z in range(3):
            top = pl.multiple_of((1 - core if other else core) * 8 + z * 16, 8)
            strips.append((ref, z * 48, top))
            at = 1152 + z * 16
            for j in range(PARTS):
                wet[j, pl.ds(top, 8), :] = spread(ref[at : at + 8, :], ref[at + 8 : at + 16, :], j, lane) * 0.25

    def unpack(part, _):
        high, f = part // 3, part % 3
        for ref, first, top in strips:
            quads = [ref[pl.ds(pl.multiple_of(first + at + part * 8, 8), 8), :] for at in places]
            for low in range(4):
                out = pltpu.roll(quads[0], (128 - 32 * low) % 128, 1) if low else quads[0]
                for x in range(1, 4):
                    turned = pltpu.roll(quads[x], 32 * (x - low) % 128, 1) if x != low else quads[x]
                    out = jnp.where(lane >= 32 * x, turned, out)
                left = pltpu.roll(quads[4], (96 - 32 * low) % 128, 1)
                right = pltpu.roll(quads[5], (128 - 32 * low) % 128, 1)
                halo = halo_columns(left, right, lane)
                for j in range(PARTS):
                    base[high * 4 + low, f, j, pl.ds(top + 8, 8), :] = spread(out, halo, j, lane)

    lax.fori_loop(0, 6, unpack, None)

    def prepare(step, tile):
        top = pl.multiple_of(tile * 8, 8)
        w = [wet[v, pl.ds(top, 8), :] for v in range(PARTS)]

        def rows(f, shift):
            return [base[step, f, v, pl.ds(top + 8 + shift, 8), :] for v in range(PARTS)]

        depth = [x + 1.0 for x in rows(0, 0)]
        b, c = rows(1, 0), rows(2, 0)
        hp, hm = from_right(depth), from_left(depth)
        bp, bm = from_right(b), from_left(b)
        cp, cm = from_right(c), from_left(c)
        hn, hs = rows(0, 1), rows(0, -1)
        bn, bs = rows(1, 1), rows(1, -1)
        cn, cs = rows(2, 1), rows(2, -1)
        for v in range(PARTS):
            q = w[v]
            parts = (
                -q * hp[v], q * hm[v], -q * bp[v], q * bm[v],
                -q * (hn[v] + 1.0), q * (hs[v] + 1.0), -q * cn[v], q * cs[v],
                -q * b[v], -q * c[v],
                -q * (bp[v] - bm[v]), q * (1.0 - (bn[v] - bs[v])), -q * (1.0 + (cp[v] - cm[v])), -q * (cn[v] - cs[v]),
                q,
            )
            for k, part in enumerate(parts):
                coef[k, v, pl.ds(top, 8), :] = part

    def changes(ref, top, pairs):
        rows, north, south = (pl.ds(top + k, 8) for k in (0, 1, -1))
        moved = []
        for p in pairs:
            h, u, m = ([ref[f, p, v, rows, :] for v in range(PARTS)] for f in range(3))
            moved.append(
                (h, u, m, from_right(h), from_left(h), from_right(u), from_left(u))
                + ([a - b for a, b in zip(from_right(m), from_left(m))],)
            )
        out = [([], [], []) for _ in pairs]
        for v in range(PARTS):
            k = [coef[i, v, rows, :] for i in range(COEFS)]
            for p, (h, u, m, hp, hm, up, um, md), fields in zip(pairs, moved, out):
                hn, un, mn = (ref[f, p, v, north, :] for f in range(3))
                hs, us, ms = (ref[f, p, v, south, :] for f in range(3))
                fields[0].append(
                    ((k[0] * up[v] + k[1] * um[v]) + (k[2] * hp[v] + k[3] * hm[v]))
                    + ((k[4] * mn + k[5] * ms) + (k[6] * hn + k[7] * hs))
                )
                fields[1].append(
                    (k[8] * (up[v] - um[v]) + k[9] * (un - us)) + ((k[10] * u[v] + k[11] * m[v]) - k[14] * (hp[v] - hm[v]))
                )
                fields[2].append((k[8] * md[v] + k[9] * (mn - ms)) + ((k[12] * u[v] + k[13] * m[v]) - k[14] * (hn - hs)))
        return out

    def sweep(low, high, body):
        def window(i, _):
            lax.fori_loop(0, QUADS // GROUP, lambda g, _: body(low + 8 * i, [g * GROUP + k for k in range(GROUP)]), None)

        lax.fori_loop(0, (high - low + 7) // 8, window, None)

    def first(top, pairs):
        for p, change in zip(pairs, changes(state, top, pairs)):
            for f in range(3):
                for v in range(PARTS):
                    middle[f, p, v, pl.ds(top, 8), :] = state[f, p, v, pl.ds(top, 8), :] + change[f][v]

    def second(top, pairs):
        for p, change in zip(pairs, changes(middle, top, pairs)):
            for f in range(3):
                for v in range(PARTS):
                    at = (f, p, v, pl.ds(top, 8), slice(None))
                    state[at] = 0.5 * ((state[at] + middle[at]) + change[f][v])

    def advance(step, _):
        low, high = 2 * step + 1, TALL - 2 * step - 1
        lax.fori_loop(low // 8, (high + 7) // 8, lambda tile, _: prepare(step, tile), None)
        sweep(low, high, first)
        sweep(low + 1, high - 1, second)

    lax.fori_loop(0, STEPS, advance, None)

    def deliver(f, _):
        for c in range(2):
            for quad in range(QUADS):
                rows = slice(HALO + c * 8, HALO + c * 8 + 8)
                parts = [state[f, quad, j, rows, :] for j in range(PARTS)]
                for quarter in range(4):
                    at = pl.ds(2 * quad + quarter // 2, 8, stride=8)
                    turn[c, quarter % 2, at, :] = gathered(parts, quarter, lane)
        for c in range(2):
            for high in range(2):
                for v in range(2):
                    lines = [turn[c, v, (high * 4 + low) * 8 : (high * 4 + low) * 8 + 8, :] for low in range(4)]
                    for x in range(4):
                        out = pltpu.roll(lines[0], 128 - 32 * x, 1) if x else lines[0]
                        for low in range(1, 4):
                            turned = pltpu.roll(lines[low], 32 * (low - x) % 128, 1) if low != x else lines[low]
                            out = jnp.where(lane >= 32 * low, turned, out)
                        out_ref[x * 2 + c, pl.ds(pl.multiple_of(f * 32 + (high * 2 + v) * 8, 8), 8), :] = out

    lax.fori_loop(0, 3, deliver, None)


def mix_kernel(coef_ref, cells_ref, out_ref, mixing):
    row = lax.broadcasted_iota(jnp.int32, (128, 128), 0)
    col = lax.broadcasted_iota(jnp.int32, (128, 128), 1)
    mixing[...] = jnp.where(row <= col, coef_ref[...], 0.0) + jnp.where(row == col, 1.0, 0.0)
    matrix = jnp.concatenate([mixing[pl.ds(t, 8, stride=16), :] for t in range(16)], axis=0)
    for k in range(6):
        cells = jnp.concatenate([cells_ref[p * 96 + k * 16 : p * 96 + k * 16 + 16, :] for p in range(8)], axis=0)
        out_ref[k * 128 : (k + 1) * 128, :] = lax.dot_general(
            cells, matrix, (((0,), (0,)), ((), ())), precision=lax.Precision.HIGHEST, preferred_element_type=f32
        )


VMEM = pl.BlockSpec(memory_space=pltpu.VMEM)
SMEM = pl.BlockSpec(memory_space=pltpu.SMEM)


def on_device(tangents, checkpoints, owner_order, land_mask, coefficients):
    block = lax.axis_index("y") * 2 + lax.axis_index("zh")
    core = lax.axis_index("c")
    raw = pl.pallas_call(
        flow_kernel,
        out_shape=jax.ShapeDtypeStruct((64, LANES), f32),
        in_specs=[SMEM, SMEM, VMEM, VMEM],
        out_specs=VMEM,
        compiler_params=pltpu.CompilerParams(vmem_limit_bytes=16 * 2**20),
    )(block.reshape(1).astype(jnp.int32), owner_order, checkpoints, land_mask)
    send = pl.pallas_call(
        pack_kernel,
        out_shape=jax.ShapeDtypeStruct((PEERS, 64, LANES), f32),
        in_specs=[VMEM, VMEM],
        out_specs=VMEM,
        compiler_params=pltpu.CompilerParams(vmem_limit_bytes=16 * 2**20),
    )(tangents, land_mask)
    up = [(i, i + 1) for i in range(7)]
    down = [(i + 1, i) for i in range(7)]
    chips = [lax.ppermute(raw, "zl", up), raw, lax.ppermute(raw, "zl", down)]
    flow = [x[:48] for x in chips]
    wet = [x[48:] for x in chips]

    def ring(chip):
        ends = [(s, (s + step) % 8, x) for s in range(8) for x, step in ((3, 1), (0, -1))]
        return [
            ((s * 4 + x) * 8 + z, (t * 4 + x) * 8 + z + chip) for s, t, x in ends for z in range(8) if 0 <= z + chip < 8
        ]

    halo = [lax.ppermute(raw[:48], ("y", "zh", "x", "zl"), ring(chip)) for chip in (1, 0, -1)]
    send, flow, halo = lax.optimization_barrier((send, flow, halo))
    own = lax.all_to_all(send, ("y", "zh", "c"), 0, 0, tiled=True)
    flow = jnp.concatenate([*flow, *halo], axis=0)
    flows = [lax.ppermute(flow, "x", [(i, (i + k) % 4) for i in range(4)]) for k in (1, 2, 3)]
    strip = jnp.concatenate([flow, *flows, *wet], axis=0)
    other = lax.ppermute(strip, "c", [(0, 1), (1, 0)])
    own, other = lax.optimization_barrier((own, other))
    parts = [lax.ppermute(own, "zl", up), own, lax.ppermute(own, "zl", down)]
    parts = [x.reshape(PEERS * 64, LANES) for x in parts]
    out = pl.pallas_call(
        march_kernel,
        out_shape=jax.ShapeDtypeStruct((8, 96, LANES), f32),
        in_specs=[SMEM] + [VMEM] * 5,
        out_specs=VMEM,
        scratch_shapes=[
            pltpu.VMEM((3, QUADS, PARTS, TALL + 8, LANES), f32),
            pltpu.VMEM((3, QUADS, PARTS, TALL + 8, LANES), f32),
            pltpu.VMEM((STEPS, 3, PARTS, TALL + 16, LANES), f32),
            pltpu.VMEM((PARTS, TALL, LANES), f32),
            pltpu.VMEM((COEFS, PARTS, TALL + 8, LANES), f32),
            pltpu.VMEM((2, 2, 64, LANES), f32),
        ],
        compiler_params=pltpu.CompilerParams(vmem_limit_bytes=32 * 2**20),
    )(jnp.stack([core, lax.axis_index("x")]).astype(jnp.int32), *parts, strip, other)
    cells = lax.all_to_all(out, ("x", "c"), 0, 0, tiled=True)
    mixed = pl.pallas_call(
        mix_kernel,
        out_shape=jax.ShapeDtypeStruct((768, 128), f32),
        in_specs=[VMEM, VMEM],
        out_specs=VMEM,
        scratch_shapes=[pltpu.VMEM((128, 128), f32)],
        compiler_params=pltpu.CompilerParams(vmem_limit_bytes=16 * 2**20),
    )(coefficients, cells.reshape(768, LANES))
    return mixed.reshape(3, 8, 32, 128).transpose(3, 0, 1, 2)


def solution(mesh):
    fine = jax.sharding.Mesh(mesh.devices.reshape(SIZES), AXES)
    mode, rows = ("y", "zh", "x"), ("zl", "c")
    placed = (
        P(mode, None, rows, None),
        P(None, None, rows, mode),
        P(),
        P(rows, None),
        P(),
    )
    return jax.shard_map(
        on_device, mesh=fine, in_specs=placed, out_specs=P(None, None, rows, mode), check_vma=False
    )
```

time: 149 us -> 155 us (1.040)
  waiting for transfers between devices: 24.2 us -> 16.4 us
  Pallas kernels: 31.7 us -> 36.8 us
  starting transfers between devices: 77.6 us -> 81.7 us
  local copies, waits for them, and re-layouts: 2.44 us -> 6.07 us
    ppermute x1 -> x3, starting transfers between devices: 16.8 us -> 31 us  [on_device(): lax.ppermute(raw[:48], ('y', 'zh', 'x', 'zl'), ring(chip))]
    all_to_all x1, starting transfers between devices: 18.6 us -> 5.45 us  [on_device(): own = lax.all_to_all(send, ('y', 'zh', 'c'), 0, 0, tiled=True)]
    ppermute x2, waiting for transfers between devices: 3.55 us -> 0.01 us  [on_device(): chips = [lax.ppermute(raw, 'zl', up), raw, lax.ppermute(raw, 'zl', down)]]
    pallas_call x1, Pallas kernels: 28.7 us -> 32.1 us  [on_device(): pl.pallas_call(march_kernel, out_shape=jax.ShapeDtypeStruct((8, 96, LANES...]
    ppermute x2, starting transfers between devices: 24 us -> 27 us  [on_device(): parts = [lax.ppermute(own, 'zl', up), own, lax.ppermute(own, 'zl', down)]]
    unnamed x19 -> x30, local copies, waits for them, and re-layouts: 2.43 us -> 5.34 us
    ppermute x2, waiting for transfers between devices: 11.8 us -> 9.81 us  [on_device(): parts = [lax.ppermute(own, 'zl', up), own, lax.ppermute(own, 'zl', down)]]
    pallas_call x2, Pallas kernels: 1.73 us -> 3.38 us  [the longest x1 2.75 us: on_device(): pl.pallas_call(pack_kernel, out_shape=jax.ShapeDtypeStruct((PEERS, 64, LA...]
  transfers between devices with their start and end apart: 10 -> 12, of which waited for: 7 -> 5; matrix products, arithmetic and copies ran while one was open for 0% -> 0% of each run, Pallas kernels for 1% -> 2%
where the time goes in v7:
time: 155 us; the launch traced here: 154 us
  starting transfers between devices  81.7 us (53%)
  Pallas kernels  36.8 us (24%)
  waiting for transfers between devices  16.4 us (11%)
  blocking collectives  12.8 us (8%)
  local copies, waits for them, and re-layouts  6.07 us (4%)
    pallas_call x1, Pallas kernels, on_device(): pl.pallas_call(march_kernel, out_shape=jax.ShapeDtypeStruct((8, 96, LANES...  32.1 us
    ppermute x3, starting transfers between devices, on_device(): lax.ppermute(raw[:48], ('y', 'zh', 'x', 'zl'), ring(chip))  31 us
    ppermute x2, starting transfers between devices, on_device(): parts = [lax.ppermute(own, 'zl', up), own, lax.ppermute(own, 'zl', down)]  27 us
    all_to_all x1, blocking collectives, on_device(): cells = lax.all_to_all(out, ('x', 'c'), 0, 0, tiled=True)  12.8 us
    ppermute x2, waiting for transfers between devices, on_device(): parts = [lax.ppermute(own, 'zl', up), own, lax.ppermute(own, 'zl', down)]  9.81 us
    ppermute x3, starting transfers between devices, on_device(): lax.ppermute(flow, 'x', [(i, (i + k) % 4) for i in range(4)])  8.63 us
    ppermute x2, starting transfers between devices, on_device(): chips = [lax.ppermute(raw, 'zl', up), raw, lax.ppermute(raw, 'zl', down)]  6.29 us
    all_to_all x1, starting transfers between devices, on_device(): own = lax.all_to_all(send, ('y', 'zh', 'c'), 0, 0, tiled=True)  5.45 us
  transfers between devices with their start and end apart: 12, of which 5 were waited for; matrix products, arithmetic and copies ran while one was open for 0% of the time, Pallas kernels for 2%

profile of v7, /device:TPU:1, one launch (start us, length us, event | category | flops | bytes accessed | tf_op | source)
XLA Modules:
  0.0 154.1 jit_solution(13127883792447459512)
XLA Ops:
  0.0 0.0 copy-start.5
  0.0 0.7 copy-done.5
  0.7 0.8 copy-done.1
  1.4 0.9 copy-done.3
  2.3 0.6 shard_map.56
  2.9 1.3 collective-permute-start.1
  4.2 5.0 %collective-permute-start = (f32[64,128]{1,0:T(8,128)S(1)}, f32[64,128]{1,0:T(8,128)S(1)}, u32[]{:S(2)}, u32[]{:S(2)}) collective-permute-start(f32[64,128]{1,0:T(8,128)S(1)} %shard_map.56), channel_id=1, source_target_pairs={{0,2},{2,4},{4,6},{6,8},{8,10},{10,12},{12,14},{1,3},{3,5},{5,7},{... | collective-permute-start | bytes 98312 | tf_op jit(solution)/shard_map/ppermute | solution.py:278
  9.3 1.3 collective-permute-start.4
  10.6 17.7 %collective-permute-start.3 = (f32[48,128]{1,0:T(8,128)S(1)}, f32[48,128]{1,0:T(8,128)S(1)}, u32[]{:S(2)}, u32[]{:S(2)}) collective-permute-start(f32[48,128]{1,0:T(8,128)S(1)} %slice.28), channel_id=1, source_target_pairs={{48,112},{50,114},{52,116},{54,118},{56,120},{58,122},{60,124},{62... | collective-permute-start | bytes 73736 | tf_op jit(solution)/shard_map/ppermute | solution.py:288
  28.3 12.0 %collective-permute-start.2 = (f32[48,128]{1,0:T(8,128)S(1)}, f32[48,128]{1,0:T(8,128)S(1)}, u32[]{:S(2)}, u32[]{:S(2)}) collective-permute-start(f32[48,128]{1,0:T(8,128)S(1)} %slice.28), channel_id=1, source_target_pairs={{48,114},{50,116},{52,118},{54,120},{56,122},{58,124},{60,126},{0,... | collective-permute-start | bytes 73736 | tf_op jit(solution)/shard_map/ppermute | solution.py:288
  40.3 0.0 copy-done.2
  40.3 0.0 copy-start
  40.3 1.0 copy-done
  41.3 2.8 %shard_map.55 = f32[16,64,128]{2,1,0:T(8,128)} custom-call(f32[4,3,8,1024]{3,2,1,0:T(8,128)S(1)} %copy-done, s32[8,1024]{1,0:T(8,128)S(1)} %copy-done.2), custom_call_target="tpu_custom_call" | custom-call | tf_op jit(solution)/shard_map/pallas_call | solution.py:269
  44.0 0.0 collective-permute-done.1
  44.0 0.6 copy-done.6
  44.7 0.0 collective-permute-done
  44.7 0.6 copy-done.8
  45.3 0.0 collective-permute-done.4
  45.3 0.0 collective-permute-done.3
  45.3 0.0 collective-permute-done.2
  45.3 5.4 %all-to-all-start = ((f32[16,64,128]{2,1,0:T(8,128)}), f32[16,64,128]{2,1,0:T(8,128)S(1)}, u32[]{:S(2)}, u32[]{:S(2)}) async-start(f32[16,64,128]{2,1,0:T(8,128)} %shard_map.55), calls=%async_computation | async-start | bytes 1048576 | tf_op jit(solution)/shard_map/all_to_all | solution.py:290
  50.7 0.0 slice-done.1
  50.8 0.0 slice-start
  50.8 0.7 slice-done
  51.5 1.9 %collective-permute-start.5 = (f32[288,128]{1,0:T(8,128)S(1)}, f32[288,128]{1,0:T(8,128)S(1)}, u32[]{:S(2)}, u32[]{:S(2)}) collective-permute-start(f32[288,128]{1,0:T(8,128)S(1)} %get-tuple-element.23), channel_id=1, source_target_pairs={{0,16},{16,32},{32,48},{48,0},{1,17},{17,33},{33,49},{49,1},{2,18}... | collective-permute-start | bytes 442376 | tf_op jit(solution)/shard_map/ppermute | solution.py:292
  53.5 4.8 %collective-permute-start.6 = (f32[288,128]{1,0:T(8,128)S(1)}, f32[288,128]{1,0:T(8,128)S(1)}, u32[]{:S(2)}, u32[]{:S(2)}) collective-permute-start(f32[288,128]{1,0:T(8,128)S(1)} %get-tuple-element.23), channel_id=1, source_target_pairs={{0,32},{16,48},{32,0},{48,16},{1,33},{17,49},{33,1},{49,17},{2,34}... | collective-permute-start | bytes 442376 | tf_op jit(solution)/shard_map/ppermute | solution.py:292
  58.3 1.9 %collective-permute-start.7 = (f32[288,128]{1,0:T(8,128)S(1)}, f32[288,128]{1,0:T(8,128)S(1)}, u32[]{:S(2)}, u32[]{:S(2)}) collective-permute-start(f32[288,128]{1,0:T(8,128)S(1)} %get-tuple-element.23), channel_id=1, source_target_pairs={{0,48},{16,0},{32,16},{48,32},{1,49},{17,1},{33,17},{49,33},{2,50}... | collective-permute-start | bytes 442376 | tf_op jit(solution)/shard_map/ppermute | solution.py:292
  60.2 0.0 collective-permute-done.5
  60.2 3.2 %collective-permute-done.6 = f32[288,128]{1,0:T(8,128)S(1)} collective-permute-done((f32[288,128]{1,0:T(8,128)S(1)}, f32[288,128]{1,0:T(8,128)S(1)}, u32[]{:S(2)}, u32[]{:S(2)}) %collective-permute-start.6) | collective-permute-done | bytes 147488 | tf_op jit(solution)/shard_map/ppermute | solution.py:292
  63.4 0.0 copy-start.9
  63.4 1.7 %collective-permute-done.7 = f32[288,128]{1,0:T(8,128)S(1)} collective-permute-done((f32[288,128]{1,0:T(8,128)S(1)}, f32[288,128]{1,0:T(8,128)S(1)}, u32[]{:S(2)}, u32[]{:S(2)}) %collective-permute-start.7) | collective-permute-done | bytes 147488 | tf_op jit(solution)/shard_map/ppermute | solution.py:292
  65.2 0.0 copy-done.9
  65.2 0.0 copy-start.7
  65.2 0.7 copy-done.7
  66.0 3.3 %collective-permute-start.8 = (f32[1200,128]{1,0:T(8,128)S(1)}, f32[1200,128]{1,0:T(8,128)S(1)}, u32[]{:S(2)}, u32[]{:S(2)}) collective-permute-start(f32[1200,128]{1,0:T(8,128)S(1)} %constant_dynamic-update-slice_fusion.6.strip_ref), channel_id=1, source_target_pairs={{0,1},{1,0},{2,3},{3,2},{4,5},{5,4},{6,7},{7,6},{8,9},{9,8},{10,11... | collective-permute-start | bytes 1843208 | tf_op jit(solution)/shard_map/ppermute | solution.py:294
  69.3 1.6 %collective-permute-done.8.other_ref = f32[1200,128]{1,0:T(8,128)S(1)} collective-permute-done((f32[1200,128]{1,0:T(8,128)S(1)}, f32[1200,128]{1,0:T(8,128)S(1)}, u32[]{:S(2)}, u32[]{:S(2)}) %collective-permute-start.8) | collective-permute-done | bytes 614432 | tf_op jit(solution)/shard_map/ppermute | solution.py:294
  70.9 0.0 all-to-all-done
  70.9 1.3 collective-permute-start.10
  72.2 25.8 %collective-permute-start.9 = (f32[16,64,128]{2,1,0:T(8,128)S(1)}, f32[16,64,128]{2,1,0:T(8,128)S(1)}, u32[]{:S(2)}, u32[]{:S(2)}) collective-permute-start(f32[16,64,128]{2,1,0:T(8,128)S(1)} %all-to-all-done), channel_id=1, source_target_pairs={{0,2},{2,4},{4,6},{6,8},{8,10},{10,12},{12,14},{1,3},{3,5},{5,7},{... | collective-permute-start | bytes 1572872 | tf_op jit(solution)/shard_map/ppermute | solution.py:296
  98.0 0.1 pad_add_fusion.core_ref
  98.0 8.9 %collective-permute-done.10 = f32[16,64,128]{2,1,0:T(8,128)S(1)} collective-permute-done((f32[16,64,128]{2,1,0:T(8,128)S(1)}, f32[16,64,128]{2,1,0:T(8,128)S(1)}, u32[]{:S(2)}, u32[]{:S(2)}) %collective-permute-start.10) | collective-permute-done | bytes 524320 | tf_op jit(solution)/shard_map/ppermute | solution.py:296
  107.0 0.9 collective-permute-done.9
  107.8 32.1 %shard_map.57 = f32[8,96,128]{2,1,0:T(8,128)S(1)} custom-call(s32[2]{0:T(128)S(1)} %pad_add_fusion.core_ref, f32[1024,128]{1,0:T(8,128)S(1)} %bitcast.13, f32[1024,128]{1,0:T(8,128)S(1)} %bitcast.10, f32[1024,128]{1,0:T(8,128)S(1)} %bitcast.12, f32[1200,128]{1,0:T(8,128)S(1)} %constant_dynamic-update-slice_fusion.6.strip_ref, ...), custom_call_target="tpu_custom_call" | custom-call | tf_op jit(solution)/shard_map/pallas_call | solution.py:298
  140.0 0.0 copy-start.4
  140.0 12.8 %all_to_all.10 = f32[8,96,128]{2,1,0:T(8,128)S(1)} all-to-all(f32[8,96,128]{2,1,0:T(8,128)S(1)} %shard_map.57), channel_id=1, replica_groups=mesh['y'=4,'zh'=2,'x'=4,'zl'=8,'c'=2] {'x','c'}, dimensions={0} | all-to-all | bytes 786432 | tf_op jit(solution)/shard_map/all_to_all | solution.py:313
  152.8 0.0 copy-done.4
  152.8 1.3 shard_map.58
  (19 shorter events, 0.1 us)
Async XLA Ops:
  0.0 0.7 copy-start.5
  0.7 0.8 copy-start.1
  1.4 0.9 copy-start.3
  2.9 37.3 %copy-start.2 = (s32[8,1024]{1,0:T(8,128)S(1)}, s32[8,1024]{1,0:T(8,128)}, u32[]{:S(2)}) copy-start(s32[8,1024]{1,0:T(8,128)} %mask_ref.3) | copy-start | bytes 98308
  2.9 41.1 %collective-permute-start.1 = (f32[64,128]{1,0:T(8,128)S(1)}, f32[64,128]{1,0:T(8,128)S(1)}, u32[]{:S(2)}, u32[]{:S(2)}) collective-permute-start(f32[64,128]{1,0:T(8,128)S(1)} %shard_map.56), channel_id=1, source_target_pairs={{2,0},{4,2},{6,4},{8,6},{10,8},{12,10},{14,12},{3,1},{5,3},{7,5},{... | collective-permute-start | bytes 98312 | tf_op jit(solution)/shard_map/ppermute | solution.py:278
  4.2 40.4 %collective-permute-start = (f32[64,128]{1,0:T(8,128)S(1)}, f32[64,128]{1,0:T(8,128)S(1)}, u32[]{:S(2)}, u32[]{:S(2)}) collective-permute-start(f32[64,128]{1,0:T(8,128)S(1)} %shard_map.56), channel_id=1, source_target_pairs={{0,2},{2,4},{4,6},{6,8},{8,10},{10,12},{12,14},{1,3},{3,5},{5,7},{... | collective-permute-start | bytes 98312 | tf_op jit(solution)/shard_map/ppermute | solution.py:278
  9.3 36.0 %collective-permute-start.4 = (f32[48,128]{1,0:T(8,128)S(1)}, f32[48,128]{1,0:T(8,128)S(1)}, u32[]{:S(2)}, u32[]{:S(2)}) collective-permute-start(f32[48,128]{1,0:T(8,128)S(1)} %slice.28), channel_id=1, source_target_pairs={{50,112},{52,114},{54,116},{56,118},{58,120},{60,122},{62,124},{2,... | collective-permute-start | bytes 73736 | tf_op jit(solution)/shard_map/ppermute | solution.py:288
  10.6 34.7 %collective-permute-start.3 = (f32[48,128]{1,0:T(8,128)S(1)}, f32[48,128]{1,0:T(8,128)S(1)}, u32[]{:S(2)}, u32[]{:S(2)}) collective-permute-start(f32[48,128]{1,0:T(8,128)S(1)} %slice.28), channel_id=1, source_target_pairs={{48,112},{50,114},{52,116},{54,118},{56,120},{58,122},{60,124},{62... | collective-permute-start | bytes 73736 | tf_op jit(solution)/shard_map/ppermute | solution.py:288
  28.3 17.0 %collective-permute-start.2 = (f32[48,128]{1,0:T(8,128)S(1)}, f32[48,128]{1,0:T(8,128)S(1)}, u32[]{:S(2)}, u32[]{:S(2)}) collective-permute-start(f32[48,128]{1,0:T(8,128)S(1)} %slice.28), channel_id=1, source_target_pairs={{48,114},{50,116},{52,118},{54,120},{56,122},{58,124},{60,126},{0,... | collective-permute-start | bytes 73736 | tf_op jit(solution)/shard_map/ppermute | solution.py:288
  40.3 1.0 copy-start
  44.0 0.6 copy-start.6
  44.7 0.6 copy-start.8
  45.3 5.5 %slice-start.1 = ((f32[64,128]{1,0:T(8,128)}), f32[48,128]{1,0:T(8,128)S(1)}, s32[]{:S(2)}) async-start(f32[64,128]{1,0:T(8,128)} %copy-done.8), calls=%async_computation.3 | async-start | bytes 49152 | tf_op jit(solution)/shard_map/slice | solution.py:279
  45.3 25.6 %all-to-all-start = ((f32[16,64,128]{2,1,0:T(8,128)}), f32[16,64,128]{2,1,0:T(8,128)S(1)}, u32[]{:S(2)}, u32[]{:S(2)}) async-start(f32[16,64,128]{2,1,0:T(8,128)} %shard_map.55), calls=%async_computation | async-start | bytes 1048576 | tf_op jit(solution)/shard_map/all_to_all | solution.py:290
  50.8 0.7 slice-start
  51.5 8.7 %collective-permute-start.5 = (f32[288,128]{1,0:T(8,128)S(1)}, f32[288,128]{1,0:T(8,128)S(1)}, u32[]{:S(2)}, u32[]{:S(2)}) collective-permute-start(f32[288,128]{1,0:T(8,128)S(1)} %get-tuple-element.23), channel_id=1, source_target_pairs={{0,16},{16,32},{32,48},{48,0},{1,17},{17,33},{33,49},{49,1},{2,18}... | collective-permute-start | bytes 442376 | tf_op jit(solution)/shard_map/ppermute | solution.py:292
  53.5 9.9 %collective-permute-start.6 = (f32[288,128]{1,0:T(8,128)S(1)}, f32[288,128]{1,0:T(8,128)S(1)}, u32[]{:S(2)}, u32[]{:S(2)}) collective-permute-start(f32[288,128]{1,0:T(8,128)S(1)} %get-tuple-element.23), channel_id=1, source_target_pairs={{0,32},{16,48},{32,0},{48,16},{1,33},{17,49},{33,1},{49,17},{2,34}... | collective-permute-start | bytes 442376 | tf_op jit(solution)/shard_map/ppermute | solution.py:292
  58.3 6.9 %collective-permute-start.7 = (f32[288,128]{1,0:T(8,128)S(1)}, f32[288,128]{1,0:T(8,128)S(1)}, u32[]{:S(2)}, u32[]{:S(2)}) collective-permute-start(f32[288,128]{1,0:T(8,128)S(1)} %get-tuple-element.23), channel_id=1, source_target_pairs={{0,48},{16,0},{32,16},{48,32},{1,49},{17,1},{33,17},{49,33},{2,50}... | collective-permute-start | bytes 442376 | tf_op jit(solution)/shard_map/ppermute | solution.py:292
  63.4 1.8 %copy-start.9 = (f32[64,128]{1,0:T(8,128)S(1)}, f32[64,128]{1,0:T(8,128)}, u32[]{:S(2)}) copy-start(f32[64,128]{1,0:T(8,128)} %copy-done.8) | copy-start | bytes 98308
  65.2 0.8 copy-start.7
  66.0 4.9 %collective-permute-start.8 = (f32[1200,128]{1,0:T(8,128)S(1)}, f32[1200,128]{1,0:T(8,128)S(1)}, u32[]{:S(2)}, u32[]{:S(2)}) collective-permute-start(f32[1200,128]{1,0:T(8,128)S(1)} %constant_dynamic-update-slice_fusion.6.strip_ref), channel_id=1, source_target_pairs={{0,1},{1,0},{2,3},{3,2},{4,5},{5,4},{6,7},{7,6},{8,9},{9,8},{10,11... | collective-permute-start | bytes 1843208 | tf_op jit(solution)/shard_map/ppermute | solution.py:294
  70.9 36.0 %collective-permute-start.10 = (f32[16,64,128]{2,1,0:T(8,128)S(1)}, f32[16,64,128]{2,1,0:T(8,128)S(1)}, u32[]{:S(2)}, u32[]{:S(2)}) collective-permute-start(f32[16,64,128]{2,1,0:T(8,128)S(1)} %all-to-all-done), channel_id=1, source_target_pairs={{2,0},{4,2},{6,4},{8,6},{10,8},{12,10},{14,12},{3,1},{5,3},{7,5},{... | collective-permute-start | bytes 1572872 | tf_op jit(solution)/shard_map/ppermute | solution.py:296
  72.2 35.7 %collective-permute-start.9 = (f32[16,64,128]{2,1,0:T(8,128)S(1)}, f32[16,64,128]{2,1,0:T(8,128)S(1)}, u32[]{:S(2)}, u32[]{:S(2)}) collective-permute-start(f32[16,64,128]{2,1,0:T(8,128)S(1)} %all-to-all-done), channel_id=1, source_target_pairs={{0,2},{2,4},{4,6},{6,8},{8,10},{10,12},{12,14},{1,3},{3,5},{5,7},{... | collective-permute-start | bytes 1572872 | tf_op jit(solution)/shard_map/ppermute | solution.py:296
  140.0 12.8 %copy-start.4 = (f32[128,128]{1,0:T(8,128)S(1)}, f32[128,128]{1,0:T(8,128)}, u32[]{:S(2)}) copy-start(f32[128,128]{1,0:T(8,128)} %coef_ref.1) | copy-start | bytes 196612

commit v8 on v7

--- a/solution.py
+++ b/solution.py
@@ -1,3 +1,5 @@
+import functools
+
 import jax
 import jax.numpy as jnp
 from jax import lax
@@ -91,34 +93,17 @@
     lax.fori_loop(0, 2, send, None)
 
 
-def march_kernel(
-    core_ref, prev_ref, own_ref, next_ref, strip_ref, other_ref,
-    out_ref, state, middle, base, wet, coef, turn,
-):
+def coef_kernel(core_ref, strip_ref, other_ref, coef, base, wet):
     lane = lax.broadcasted_iota(jnp.int32, (8, LANES), 1)
-    def place(quad, _):
-        for z, ref in enumerate((prev_ref, own_ref, next_ref)):
-            for c in range(2):
-                for f in range(3):
-                    for j in range(PARTS):
-                        i, odd = divmod(f * PARTS + j, 2)
-                        one, two = (
-                            ref[pl.ds(pl.multiple_of((4 * quad + 2 * p + c) * 64 + i * 8, 8), 8), :] for p in range(2)
-                        )
-                        one, two = (pltpu.roll(one, 64, 1), two) if odd else (one, pltpu.roll(two, 64, 1))
-                        rows = slice(z * 16 + c * 8, z * 16 + c * 8 + 8)
-                        state[f, quad, j, rows, :] = jnp.where(lane < 64, one, two)
-
-    lax.fori_loop(0, QUADS, place, None)
     core, me = core_ref[0], core_ref[1]
-    blocks = [lax.rem(me - x + 4, 4) * 288 for x in range(4)]
-    places = blocks + [blocks[3] + 144, blocks[0] + 144]
+    blocks = [lax.rem(me - x + 4, 4) * 336 for x in range(4)]
+    places = blocks + [blocks[3] + 64, blocks[0] + 64]
     strips = []
     for other, ref in enumerate((strip_ref, other_ref)):
         for z in range(3):
             top = pl.multiple_of((1 - core if other else core) * 8 + z * 16, 8)
-            strips.append((ref, z * 48, top))
-            at = 1152 + z * 16
+            strips.append((ref, z * 112, top))
+            at = z * 112 + 48
             for j in range(PARTS):
                 wet[j, pl.ds(top, 8), :] = spread(ref[at : at + 8, :], ref[at + 8 : at + 16, :], j, lane) * 0.25
 
@@ -164,9 +149,31 @@
                 q,
             )
             for k, part in enumerate(parts):
-                coef[k, v, pl.ds(top, 8), :] = part
-
-    def changes(ref, top, pairs):
+                coef[step, k, v, pl.ds(top, 8), :] = part
+
+    def tiles(step, _):
+        lax.fori_loop((2 * step + 1) // 8, (TALL - 2 * step + 6) // 8, lambda tile, _: prepare(step, tile), None)
+
+    lax.fori_loop(0, STEPS, tiles, None)
+
+
+def march_kernel(prev_ref, own_ref, next_ref, coef, out_ref, state, middle, turn):
+    lane = lax.broadcasted_iota(jnp.int32, (8, LANES), 1)
+    def place(quad, _):
+        for z, ref in enumerate((prev_ref, own_ref, next_ref)):
+            for c in range(2):
+                for f in range(3):
+                    for j in range(PARTS):
+                        i, odd = divmod(f * PARTS + j, 2)
+                        one, two = (
+                            ref[pl.ds(pl.multiple_of((4 * quad + 2 * p + c) * 64 + i * 8, 8), 8), :] for p in range(2)
+                        )
+                        one, two = (pltpu.roll(one, 64, 1), two) if odd else (one, pltpu.roll(two, 64, 1))
+                        rows = slice(z * 16 + c * 8, z * 16 + c * 8 + 8)
+                        state[f, quad, j, rows, :] = jnp.where(lane < 64, one, two)
+
+    lax.fori_loop(0, QUADS, place, None)
+    def changes(ref, step, top, pairs):
         rows, north, south = (pl.ds(top + k, 8) for k in (0, 1, -1))
         moved = []
         for p in pairs:
@@ -177,7 +184,7 @@
             )
         out = [([], [], []) for _ in pairs]
         for v in range(PARTS):
-            k = [coef[i, v, rows, :] for i in range(COEFS)]
+            k = [coef[step, i, v, rows, :] for i in range(COEFS)]
             for p, (h, u, m, hp, hm, up, um, md), fields in zip(pairs, moved, out):
                 hn, un, mn = (ref[f, p, v, north, :] for f in range(3))
                 hs, us, ms = (ref[f, p, v, south, :] for f in range(3))
@@ -197,14 +204,14 @@
 
         lax.fori_loop(0, (high - low + 7) // 8, window, None)
 
-    def first(top, pairs):
-        for p, change in zip(pairs, changes(state, top, pairs)):
+    def first(step, top, pairs):
+        for p, change in zip(pairs, changes(state, step, top, pairs)):
             for f in range(3):
                 for v in range(PARTS):
                     middle[f, p, v, pl.ds(top, 8), :] = state[f, p, v, pl.ds(top, 8), :] + change[f][v]
 
-    def second(top, pairs):
-        for p, change in zip(pairs, changes(middle, top, pairs)):
+    def second(step, top, pairs):
+        for p, change in zip(pairs, changes(middle, step, top, pairs)):
             for f in range(3):
                 for v in range(PARTS):
                     at = (f, p, v, pl.ds(top, 8), slice(None))
@@ -212,9 +219,8 @@
 
     def advance(step, _):
         low, high = 2 * step + 1, TALL - 2 * step - 1
-        lax.fori_loop(low // 8, (high + 7) // 8, lambda tile, _: prepare(step, tile), None)
-        sweep(low, high, first)
-        sweep(low + 1, high - 1, second)
+        sweep(low, high, functools.partial(first, step))
+        sweep(low + 1, high - 1, functools.partial(second, step))
 
     lax.fori_loop(0, STEPS, advance, None)
 
@@ -266,6 +272,12 @@
         out_specs=VMEM,
         compiler_params=pltpu.CompilerParams(vmem_limit_bytes=16 * 2**20),
     )(block.reshape(1).astype(jnp.int32), owner_order, checkpoints, land_mask)
+    up = [(i, i + 1) for i in range(7)]
+    down = [(i + 1, i) for i in range(7)]
+    ring = [(s * 4 + x, (s + step) % 8 * 4 + x) for s in range(8) for x, step in ((3, 1), (0, -1))]
+    halo = lax.ppermute(raw[:48], ("y", "zh", "x"), ring)
+    wide = jnp.concatenate([raw, halo], axis=0)
+    above, below = lax.ppermute(wide, "zl", up), lax.ppermute(wide, "zl", down)
     send = pl.pallas_call(
         pack_kernel,
         out_shape=jax.ShapeDtypeStruct((PEERS, 64, LANES), f32),
@@ -273,43 +285,40 @@
         out_specs=VMEM,
         compiler_params=pltpu.CompilerParams(vmem_limit_bytes=16 * 2**20),
     )(tangents, land_mask)
-    up = [(i, i + 1) for i in range(7)]
-    down = [(i + 1, i) for i in range(7)]
-    chips = [lax.ppermute(raw, "zl", up), raw, lax.ppermute(raw, "zl", down)]
-    flow = [x[:48] for x in chips]
-    wet = [x[48:] for x in chips]
-
-    def ring(chip):
-        ends = [(s, (s + step) % 8, x) for s in range(8) for x, step in ((3, 1), (0, -1))]
-        return [
-            ((s * 4 + x) * 8 + z, (t * 4 + x) * 8 + z + chip) for s, t, x in ends for z in range(8) if 0 <= z + chip < 8
-        ]
-
-    halo = [lax.ppermute(raw[:48], ("y", "zh", "x", "zl"), ring(chip)) for chip in (1, 0, -1)]
-    send, flow, halo = lax.optimization_barrier((send, flow, halo))
+    send, above, below = lax.optimization_barrier((send, above, below))
     own = lax.all_to_all(send, ("y", "zh", "c"), 0, 0, tiled=True)
-    flow = jnp.concatenate([*flow, *halo], axis=0)
-    flows = [lax.ppermute(flow, "x", [(i, (i + k) % 4) for i in range(4)]) for k in (1, 2, 3)]
-    strip = jnp.concatenate([flow, *flows, *wet], axis=0)
+    chips = jnp.concatenate([above, wide, below], axis=0)
+    strip = jnp.concatenate(
+        [chips] + [lax.ppermute(chips, "x", [(i, (i + k) % 4) for i in range(4)]) for k in (1, 2, 3)], axis=0
+    )
     other = lax.ppermute(strip, "c", [(0, 1), (1, 0)])
-    own, other = lax.optimization_barrier((own, other))
+    own, strip, other = lax.optimization_barrier((own, strip, other))
+    coef = pl.pallas_call(
+        coef_kernel,
+        out_shape=jax.ShapeDtypeStruct((STEPS, COEFS, PARTS, TALL + 8, LANES), f32),
+        in_specs=[SMEM, VMEM, VMEM],
+        out_specs=VMEM,
+        scratch_shapes=[
+            pltpu.VMEM((STEPS, 3, PARTS, TALL + 16, LANES), f32),
+            pltpu.VMEM((PARTS, TALL, LANES), f32),
+        ],
+        compiler_params=pltpu.CompilerParams(vmem_limit_bytes=32 * 2**20),
+        cost_estimate=pl.CostEstimate(flops=2 * 10**9, bytes_accessed=50 * 10**6, transcendentals=0),
+    )(jnp.stack([core, lax.axis_index("x")]).astype(jnp.int32), strip, other)
     parts = [lax.ppermute(own, "zl", up), own, lax.ppermute(own, "zl", down)]
     parts = [x.reshape(PEERS * 64, LANES) for x in parts]
     out = pl.pallas_call(
         march_kernel,
         out_shape=jax.ShapeDtypeStruct((8, 96, LANES), f32),
-        in_specs=[SMEM] + [VMEM] * 5,
+        in_specs=[VMEM] * 4,
         out_specs=VMEM,
         scratch_shapes=[
             pltpu.VMEM((3, QUADS, PARTS, TALL + 8, LANES), f32),
             pltpu.VMEM((3, QUADS, PARTS, TALL + 8, LANES), f32),
-            pltpu.VMEM((STEPS, 3, PARTS, TALL + 16, LANES), f32),
-            pltpu.VMEM((PARTS, TALL, LANES), f32),
-            pltpu.VMEM((COEFS, PARTS, TALL + 8, LANES), f32),
             pltpu.VMEM((2, 2, 64, LANES), f32),
         ],
-        compiler_params=pltpu.CompilerParams(vmem_limit_bytes=32 * 2**20),
-    )(jnp.stack([core, lax.axis_index("x")]).astype(jnp.int32), *parts, strip, other)
+        compiler_params=pltpu.CompilerParams(vmem_limit_bytes=26 * 2**20),
+    )(*parts, coef)
     cells = lax.all_to_all(out, ("x", "c"), 0, 0, tiled=True)
     mixed = pl.pallas_call(
         mix_kernel,

time: 155 us -> 134 us (0.86)
  starting transfers between devices: 81.7 us -> 71.6 us
  waiting for transfers between devices: 16.4 us -> 9.03 us
  local copies, waits for them, and re-layouts: 6.07 us -> 4.12 us
    pallas_call x1, Pallas kernels: 32.1 us -> 13.8 us  [on_device(): pl.pallas_call(march_kernel, out_shape=jax.ShapeDtypeStruct((8, 96, LANES...]
    pallas_call x0 -> x1, Pallas kernels: none -> 17.6 us  [on_device(): pl.pallas_call(coef_kernel, out_shape=jax.ShapeDtypeStruct((STEPS, COEFS,...]
    ppermute x8 -> x6, starting transfers between devices: 45.9 us -> 31.1 us  [the longest x1 18.7 us: on_device(): halo = lax.ppermute(raw[:48], ('y', 'zh', 'x'), ring)]
    all_to_all x1, starting transfers between devices: 5.45 us -> 16.5 us  [on_device(): own = lax.all_to_all(send, ('y', 'zh', 'c'), 0, 0, tiled=True)]
    ppermute x2, waiting for transfers between devices: 9.81 us -> 0.01 us  [on_device(): parts = [lax.ppermute(own, 'zl', up), own, lax.ppermute(own, 'zl', down)]]
    ppermute x2, starting transfers between devices: 27 us -> 20.9 us  [on_device(): parts = [lax.ppermute(own, 'zl', up), own, lax.ppermute(own, 'zl', down)]]
    ppermute x8 -> x6, waiting for transfers between devices: 4.94 us -> 7.28 us  [the longest x3 6.35 us: on_device(): lax.ppermute(chips, 'x', [(i, (i + k) % 4) for i in range(4)])]
    unnamed x30 -> x18, local copies, waits for them, and re-layouts: 5.34 us -> 4.11 us
  transfers between devices with their start and end apart: 12 -> 10, of which waited for: 5 -> 4; matrix products, arithmetic and copies ran while one was open for 0% -> 0% of each run, Pallas kernels for 2% -> 15%
where the time goes in v8:
time: 134 us; the launch traced here: 133 us
  starting transfers between devices  71.6 us (53%)
  Pallas kernels  36.1 us (27%)
  blocking collectives  11.9 us (9%)
  waiting for transfers between devices  9.03 us (7%)
  local copies, waits for them, and re-layouts  4.12 us (3%)
    ppermute x2, starting transfers between devices, on_device(): parts = [lax.ppermute(own, 'zl', up), own, lax.ppermute(own, 'zl', down)]  20.9 us
    ppermute x1, starting transfers between devices, on_device(): halo = lax.ppermute(raw[:48], ('y', 'zh', 'x'), ring)  18.7 us
    pallas_call x1, Pallas kernels, on_device(): pl.pallas_call(coef_kernel, out_shape=jax.ShapeDtypeStruct((STEPS, COEFS,...  17.6 us
    all_to_all x1, starting transfers between devices, on_device(): own = lax.all_to_all(send, ('y', 'zh', 'c'), 0, 0, tiled=True)  16.5 us
    pallas_call x1, Pallas kernels, on_device(): pl.pallas_call(march_kernel, out_shape=jax.ShapeDtypeStruct((8, 96, LANES...  13.8 us
    all_to_all x1, blocking collectives, on_device(): cells = lax.all_to_all(out, ('x', 'c'), 0, 0, tiled=True)  11.9 us
    ppermute x3, starting transfers between devices, on_device(): lax.ppermute(chips, 'x', [(i, (i + k) % 4) for i in range(4)])  8.44 us
    ppermute x3, waiting for transfers between devices, on_device(): lax.ppermute(chips, 'x', [(i, (i + k) % 4) for i in range(4)])  6.35 us
  transfers between devices with their start and end apart: 10, of which 4 were waited for; matrix products, arithmetic and copies ran while one was open for 0% of the time, Pallas kernels for 15%

profile of v8, /device:TPU:1, one launch (start us, length us, event | category | flops | bytes accessed | tf_op | source)
XLA Modules:
  0.0 133.0 jit_solution(15861097667245859822)
XLA Ops:
  0.0 0.0 copy-start.1
  0.0 0.8 copy-done.1
  0.8 0.0 copy-start.3
  0.8 0.9 copy-done.3
  1.7 0.0 copy-start.5
  1.7 0.7 copy-done.5
  2.3 0.6 shard_map.56
  2.9 18.7 %collective-permute-start = (f32[48,128]{1,0:T(8,128)S(1)}, f32[48,128]{1,0:T(8,128)S(1)}, u32[]{:S(2)}, u32[]{:S(2)}) collective-permute-start(f32[48,128]{1,0:T(8,128)S(1)} %slice.4), channel_id=1, source_target_pairs={{48,112},{0,448},{112,176},{64,0},{176,240},{128,64},{240,304},{19... | collective-permute-start | bytes 73736 | tf_op jit(solution)/shard_map/ppermute | solution.py:278
  21.7 0.9 collective-permute-done
  22.6 2.6 %collective-permute-start.1 = (f32[112,128]{1,0:T(8,128)S(1)}, f32[112,128]{1,0:T(8,128)S(1)}, u32[]{:S(2)}, u32[]{:S(2)}) collective-permute-start(f32[112,128]{1,0:T(8,128)S(1)} %pad_maximum_fusion.1), channel_id=1, source_target_pairs={{0,2},{2,4},{4,6},{6,8},{8,10},{10,12},{12,14},{1,3},{3,5},{5,7},{... | collective-permute-start | bytes 172040 | tf_op jit(solution)/shard_map/ppermute | solution.py:280
  25.2 1.3 collective-permute-start.2
  26.6 0.0 copy-start
  26.6 1.0 copy-done
  27.5 0.0 copy-start.2
  27.6 0.8 copy-done.2
  28.3 2.7 %shard_map.55 = f32[16,64,128]{2,1,0:T(8,128)} custom-call(f32[4,3,8,1024]{3,2,1,0:T(8,128)S(1)} %copy-done, s32[8,1024]{1,0:T(8,128)S(1)} %copy-done.2), custom_call_target="tpu_custom_call" | custom-call | tf_op jit(solution)/shard_map/pallas_call | solution.py:281
  31.0 0.0 collective-permute-done.1
  31.0 0.0 collective-permute-done.2
  31.1 16.5 %all-to-all-start = ((f32[16,64,128]{2,1,0:T(8,128)}), f32[16,64,128]{2,1,0:T(8,128)S(1)}, u32[]{:S(2)}, u32[]{:S(2)}) async-start(f32[16,64,128]{2,1,0:T(8,128)} %shard_map.55), calls=%async_computation | async-start | bytes 1048576 | tf_op jit(solution)/shard_map/all_to_all | solution.py:289
  47.6 1.9 %collective-permute-start.3 = (f32[336,128]{1,0:T(8,128)S(1)}, f32[336,128]{1,0:T(8,128)S(1)}, u32[]{:S(2)}, u32[]{:S(2)}) collective-permute-start(f32[336,128]{1,0:T(8,128)S(1)} %pad_maximum_fusion), channel_id=1, source_target_pairs={{0,16},{16,32},{32,48},{48,0},{1,17},{17,33},{33,49},{49,1},{2,18}... | collective-permute-start | bytes 516104 | tf_op jit(solution)/shard_map/ppermute | solution.py:292
  49.5 3.7 %collective-permute-start.4 = (f32[336,128]{1,0:T(8,128)S(1)}, f32[336,128]{1,0:T(8,128)S(1)}, u32[]{:S(2)}, u32[]{:S(2)}) collective-permute-start(f32[336,128]{1,0:T(8,128)S(1)} %pad_maximum_fusion), channel_id=1, source_target_pairs={{0,32},{16,48},{32,0},{48,16},{1,33},{17,49},{33,1},{49,17},{2,34}... | collective-permute-start | bytes 516104 | tf_op jit(solution)/shard_map/ppermute | solution.py:292
  53.2 2.8 %collective-permute-start.5 = (f32[336,128]{1,0:T(8,128)S(1)}, f32[336,128]{1,0:T(8,128)S(1)}, u32[]{:S(2)}, u32[]{:S(2)}) collective-permute-start(f32[336,128]{1,0:T(8,128)S(1)} %pad_maximum_fusion), channel_id=1, source_target_pairs={{0,48},{16,0},{32,16},{48,32},{1,49},{17,1},{33,17},{49,33},{2,50}... | collective-permute-start | bytes 516104 | tf_op jit(solution)/shard_map/ppermute | solution.py:292
  56.1 4.2 %collective-permute-done.3 = f32[336,128]{1,0:T(8,128)S(1)} collective-permute-done((f32[336,128]{1,0:T(8,128)S(1)}, f32[336,128]{1,0:T(8,128)S(1)}, u32[]{:S(2)}, u32[]{:S(2)}) %collective-permute-start.3) | collective-permute-done | bytes 172064 | tf_op jit(solution)/shard_map/ppermute | solution.py:292
  60.4 0.0 collective-permute-done.4
  60.4 2.1 %collective-permute-done.5 = f32[336,128]{1,0:T(8,128)S(1)} collective-permute-done((f32[336,128]{1,0:T(8,128)S(1)}, f32[336,128]{1,0:T(8,128)S(1)}, u32[]{:S(2)}, u32[]{:S(2)}) %collective-permute-start.5) | collective-permute-done | bytes 172064 | tf_op jit(solution)/shard_map/ppermute | solution.py:292
  62.5 3.1 %collective-permute-start.6 = (f32[1344,128]{1,0:T(8,128)S(1)}, f32[1344,128]{1,0:T(8,128)S(1)}, u32[]{:S(2)}, u32[]{:S(2)}) collective-permute-start(f32[1344,128]{1,0:T(8,128)S(1)} %constant_dynamic-update-slice_fusion.strip_ref), channel_id=1, source_target_pairs={{0,1},{1,0},{2,3},{3,2},{4,5},{5,4},{6,7},{7,6},{8,9},{9,8},{10,11... | collective-permute-start | bytes 2064392 | tf_op jit(solution)/shard_map/ppermute | solution.py:294
  65.6 1.7 %collective-permute-done.6.other_ref = f32[1344,128]{1,0:T(8,128)S(1)} collective-permute-done((f32[1344,128]{1,0:T(8,128)S(1)}, f32[1344,128]{1,0:T(8,128)S(1)}, u32[]{:S(2)}, u32[]{:S(2)}) %collective-permute-start.6) | collective-permute-done | bytes 688160 | tf_op jit(solution)/shard_map/ppermute | solution.py:294
  67.4 0.0 all-to-all-done
  67.4 19.6 %collective-permute-start.7 = (f32[16,64,128]{2,1,0:T(8,128)S(1)}, f32[16,64,128]{2,1,0:T(8,128)S(1)}, u32[]{:S(2)}, u32[]{:S(2)}) collective-permute-start(f32[16,64,128]{2,1,0:T(8,128)S(1)} %all-to-all-done), channel_id=1, source_target_pairs={{0,2},{2,4},{4,6},{6,8},{8,10},{10,12},{12,14},{1,3},{3,5},{5,7},{... | collective-permute-start | bytes 1572872 | tf_op jit(solution)/shard_map/ppermute | solution.py:308
  87.0 1.3 collective-permute-start.8
  88.3 0.1 pad_add_fusion.core_ref
  88.4 0.0 copy-start.4
  88.4 17.6 %shard_map.57.coef = f32[8,15,5,56,128]{4,3,2,1,0:T(8,128)S(1)} custom-call(s32[2]{0:T(128)S(1)} %pad_add_fusion.core_ref, f32[1344,128]{1,0:T(8,128)S(1)} %constant_dynamic-update-slice_fusion.strip_ref, f32[1344,128]{1,0:T(8,128)S(1)} %collective-permute-done.6.other_ref), custom_call_target="tpu_custom_call" | custom-call | flops 2000000000 | bytes 50000000 | tf_op jit(solution)/shard_map/pallas_call | solution.py:296
  106.0 0.0 collective-permute-done.7
  106.0 0.0 collective-permute-done.8
  106.0 13.8 %shard_map.58 = f32[8,96,128]{2,1,0:T(8,128)S(1)} custom-call(f32[1024,128]{1,0:T(8,128)S(1)} %bitcast.12, f32[1024,128]{1,0:T(8,128)S(1)} %bitcast.10, f32[1024,128]{1,0:T(8,128)S(1)} %bitcast.13, f32[8,15,5,56,128]{4,3,2,1,0:T(8,128)S(1)} %shard_map.57.coef), custom_call_target="tpu_custom_call" | custom-call | tf_op jit(solution)/shard_map/pallas_call | solution.py:310
  119.8 11.9 %all_to_all.10 = f32[8,96,128]{2,1,0:T(8,128)S(1)} all-to-all(f32[8,96,128]{2,1,0:T(8,128)S(1)} %shard_map.58), channel_id=1, replica_groups=mesh['y'=4,'zh'=2,'x'=4,'zl'=8,'c'=2] {'x','c'}, dimensions={0} | all-to-all | bytes 786432 | tf_op jit(solution)/shard_map/all_to_all | solution.py:322
  131.8 0.0 copy-done.4
  131.8 1.3 shard_map.59
  (10 shorter events, 0.1 us)
Async XLA Ops:
  0.0 0.8 copy-start.1
  0.8 0.9 copy-start.3
  1.7 0.7 copy-start.5
  2.9 19.7 %collective-permute-start = (f32[48,128]{1,0:T(8,128)S(1)}, f32[48,128]{1,0:T(8,128)S(1)}, u32[]{:S(2)}, u32[]{:S(2)}) collective-permute-start(f32[48,128]{1,0:T(8,128)S(1)} %slice.4), channel_id=1, source_target_pairs={{48,112},{0,448},{112,176},{64,0},{176,240},{128,64},{240,304},{19... | collective-permute-start | bytes 73736 | tf_op jit(solution)/shard_map/ppermute | solution.py:278
  22.6 8.4 %collective-permute-start.1 = (f32[112,128]{1,0:T(8,128)S(1)}, f32[112,128]{1,0:T(8,128)S(1)}, u32[]{:S(2)}, u32[]{:S(2)}) collective-permute-start(f32[112,128]{1,0:T(8,128)S(1)} %pad_maximum_fusion.1), channel_id=1, source_target_pairs={{0,2},{2,4},{4,6},{6,8},{8,10},{10,12},{12,14},{1,3},{3,5},{5,7},{... | collective-permute-start | bytes 172040 | tf_op jit(solution)/shard_map/ppermute | solution.py:280
  25.2 5.8 %collective-permute-start.2 = (f32[112,128]{1,0:T(8,128)S(1)}, f32[112,128]{1,0:T(8,128)S(1)}, u32[]{:S(2)}, u32[]{:S(2)}) collective-permute-start(f32[112,128]{1,0:T(8,128)S(1)} %pad_maximum_fusion.1), channel_id=1, source_target_pairs={{2,0},{4,2},{6,4},{8,6},{10,8},{12,10},{14,12},{3,1},{5,3},{7,5},{... | collective-permute-start | bytes 172040 | tf_op jit(solution)/shard_map/ppermute | solution.py:280
  26.6 1.0 copy-start
  27.5 0.8 copy-start.2
  31.1 36.3 %all-to-all-start = ((f32[16,64,128]{2,1,0:T(8,128)}), f32[16,64,128]{2,1,0:T(8,128)S(1)}, u32[]{:S(2)}, u32[]{:S(2)}) async-start(f32[16,64,128]{2,1,0:T(8,128)} %shard_map.55), calls=%async_computation | async-start | bytes 1048576 | tf_op jit(solution)/shard_map/all_to_all | solution.py:289
  47.6 12.7 %collective-permute-start.3 = (f32[336,128]{1,0:T(8,128)S(1)}, f32[336,128]{1,0:T(8,128)S(1)}, u32[]{:S(2)}, u32[]{:S(2)}) collective-permute-start(f32[336,128]{1,0:T(8,128)S(1)} %pad_maximum_fusion), channel_id=1, source_target_pairs={{0,16},{16,32},{32,48},{48,0},{1,17},{17,33},{33,49},{49,1},{2,18}... | collective-permute-start | bytes 516104 | tf_op jit(solution)/shard_map/ppermute | solution.py:292
  49.5 10.8 %collective-permute-start.4 = (f32[336,128]{1,0:T(8,128)S(1)}, f32[336,128]{1,0:T(8,128)S(1)}, u32[]{:S(2)}, u32[]{:S(2)}) collective-permute-start(f32[336,128]{1,0:T(8,128)S(1)} %pad_maximum_fusion), channel_id=1, source_target_pairs={{0,32},{16,48},{32,0},{48,16},{1,33},{17,49},{33,1},{49,17},{2,34}... | collective-permute-start | bytes 516104 | tf_op jit(solution)/shard_map/ppermute | solution.py:292
  53.2 9.3 %collective-permute-start.5 = (f32[336,128]{1,0:T(8,128)S(1)}, f32[336,128]{1,0:T(8,128)S(1)}, u32[]{:S(2)}, u32[]{:S(2)}) collective-permute-start(f32[336,128]{1,0:T(8,128)S(1)} %pad_maximum_fusion), channel_id=1, source_target_pairs={{0,48},{16,0},{32,16},{48,32},{1,49},{17,1},{33,17},{49,33},{2,50}... | collective-permute-start | bytes 516104 | tf_op jit(solution)/shard_map/ppermute | solution.py:292
  62.5 4.9 %collective-permute-start.6 = (f32[1344,128]{1,0:T(8,128)S(1)}, f32[1344,128]{1,0:T(8,128)S(1)}, u32[]{:S(2)}, u32[]{:S(2)}) collective-permute-start(f32[1344,128]{1,0:T(8,128)S(1)} %constant_dynamic-update-slice_fusion.strip_ref), channel_id=1, source_target_pairs={{0,1},{1,0},{2,3},{3,2},{4,5},{5,4},{6,7},{7,6},{8,9},{9,8},{10,11... | collective-permute-start | bytes 2064392 | tf_op jit(solution)/shard_map/ppermute | solution.py:294
  67.4 38.6 %collective-permute-start.7 = (f32[16,64,128]{2,1,0:T(8,128)S(1)}, f32[16,64,128]{2,1,0:T(8,128)S(1)}, u32[]{:S(2)}, u32[]{:S(2)}) collective-permute-start(f32[16,64,128]{2,1,0:T(8,128)S(1)} %all-to-all-done), channel_id=1, source_target_pairs={{0,2},{2,4},{4,6},{6,8},{8,10},{10,12},{12,14},{1,3},{3,5},{5,7},{... | collective-permute-start | bytes 1572872 | tf_op jit(solution)/shard_map/ppermute | solution.py:308
  87.0 19.0 %collective-permute-start.8 = (f32[16,64,128]{2,1,0:T(8,128)S(1)}, f32[16,64,128]{2,1,0:T(8,128)S(1)}, u32[]{:S(2)}, u32[]{:S(2)}) collective-permute-start(f32[16,64,128]{2,1,0:T(8,128)S(1)} %all-to-all-done), channel_id=1, source_target_pairs={{2,0},{4,2},{6,4},{8,6},{10,8},{12,10},{14,12},{3,1},{5,3},{7,5},{... | collective-permute-start | bytes 1572872 | tf_op jit(solution)/shard_map/ppermute | solution.py:308
  88.4 43.4 %copy-start.4 = (f32[128,128]{1,0:T(8,128)S(1)}, f32[128,128]{1,0:T(8,128)}, u32[]{:S(2)}) copy-start(f32[128,128]{1,0:T(8,128)} %coef_ref.1) | copy-start | bytes 196612

commit v9 on v8

--- a/solution.py
+++ b/solution.py
@@ -292,7 +292,6 @@
         [chips] + [lax.ppermute(chips, "x", [(i, (i + k) % 4) for i in range(4)]) for k in (1, 2, 3)], axis=0
     )
     other = lax.ppermute(strip, "c", [(0, 1), (1, 0)])
-    own, strip, other = lax.optimization_barrier((own, strip, other))
     coef = pl.pallas_call(
         coef_kernel,
         out_shape=jax.ShapeDtypeStruct((STEPS, COEFS, PARTS, TALL + 8, LANES), f32),
@@ -305,6 +304,7 @@
         compiler_params=pltpu.CompilerParams(vmem_limit_bytes=32 * 2**20),
         cost_estimate=pl.CostEstimate(flops=2 * 10**9, bytes_accessed=50 * 10**6, transcendentals=0),
     )(jnp.stack([core, lax.axis_index("x")]).astype(jnp.int32), strip, other)
+    own, coef = lax.optimization_barrier((own, coef))
     parts = [lax.ppermute(own, "zl", up), own, lax.ppermute(own, "zl", down)]
     parts = [x.reshape(PEERS * 64, LANES) for x in parts]
     out = pl.pallas_call(

time: 134 us -> 143 us (1.067)
  starting transfers between devices: 71.6 us -> 55.4 us
  waiting for transfers between devices: 9.03 us -> 21.9 us
  local copies, waits for them, and re-layouts: 4.12 us -> 15.9 us
    ppermute x2, starting transfers between devices: 20.9 us -> 5.3 us  [on_device(): parts = [lax.ppermute(own, 'zl', up), own, lax.ppermute(own, 'zl', down)]]
    unnamed x18 -> x22, local copies, waits for them, and re-layouts: 4.11 us -> 15.9 us
    ppermute x2, waiting for transfers between devices: 0.01 us -> 10.6 us  [on_device(): parts = [lax.ppermute(own, 'zl', up), own, lax.ppermute(own, 'zl', down)]]
    ppermute x3, waiting for transfers between devices: 6.35 us -> 8.74 us  [on_device(): lax.ppermute(chips, 'x', [(i, (i + k) % 4) for i in range(4)])]
  transfers between devices with their start and end apart: 10 -> 10, of which waited for: 4 -> 5; matrix products, arithmetic and copies ran while one was open for 0% -> 0% of each run, Pallas kernels for 15% -> 14%
where the time goes in v9:
time: 143 us; the launch traced here: 142 us
  starting transfers between devices  55.4 us (39%)
  Pallas kernels  36.1 us (25%)
  waiting for transfers between devices  21.9 us (15%)
  local copies, waits for them, and re-layouts  15.9 us (11%)
  blocking collectives  12 us (8%)
    ppermute x1, starting transfers between devices, on_device(): halo = lax.ppermute(raw[:48], ('y', 'zh', 'x'), ring)  18.7 us
    pallas_call x1, Pallas kernels, on_device(): pl.pallas_call(coef_kernel, out_shape=jax.ShapeDtypeStruct((STEPS, COEFS,...  17.6 us
    all_to_all x1, starting transfers between devices, on_device(): own = lax.all_to_all(send, ('y', 'zh', 'c'), 0, 0, tiled=True)  16.5 us
    unnamed x22, local copies, waits for them, and re-layouts  15.9 us
    pallas_call x1, Pallas kernels, on_device(): pl.pallas_call(march_kernel, out_shape=jax.ShapeDtypeStruct((8, 96, LANES...  13.8 us
    all_to_all x1, blocking collectives, on_device(): cells = lax.all_to_all(out, ('x', 'c'), 0, 0, tiled=True)  12 us
    ppermute x2, waiting for transfers between devices, on_device(): parts = [lax.ppermute(own, 'zl', up), own, lax.ppermute(own, 'zl', down)]  10.6 us
    ppermute x3, waiting for transfers between devices, on_device(): lax.ppermute(chips, 'x', [(i, (i + k) % 4) for i in range(4)])  8.74 us
  transfers between devices with their start and end apart: 10, of which 5 were waited for; matrix products, arithmetic and copies ran while one was open for 0% of the time, Pallas kernels for 14%

profile of v9, /device:TPU:1, one launch (start us, length us, event | category | flops | bytes accessed | tf_op | source)
XLA Modules:
  0.0 141.6 jit_solution(6997728557548279327)
XLA Ops:
  0.0 0.0 copy-start.3
  0.0 0.8 copy-done.3
  0.8 0.0 copy-start.5
  0.8 0.9 copy-done.5
  1.7 0.0 copy-start.7
  1.7 0.7 copy-done.7
  2.3 0.6 shard_map.56
  2.9 18.7 %collective-permute-start = (f32[48,128]{1,0:T(8,128)S(1)}, f32[48,128]{1,0:T(8,128)S(1)}, u32[]{:S(2)}, u32[]{:S(2)}) collective-permute-start(f32[48,128]{1,0:T(8,128)S(1)} %slice.4), channel_id=1, source_target_pairs={{48,112},{0,448},{112,176},{64,0},{176,240},{128,64},{240,304},{19... | collective-permute-start | bytes 73736 | tf_op jit(solution)/shard_map/ppermute | solution.py:278
  21.7 0.9 collective-permute-done
  22.6 1.3 collective-permute-start.2
  23.9 4.0 %collective-permute-start.1 = (f32[112,128]{1,0:T(8,128)S(1)}, f32[112,128]{1,0:T(8,128)S(1)}, u32[]{:S(2)}, u32[]{:S(2)}) collective-permute-start(f32[112,128]{1,0:T(8,128)S(1)} %pad_maximum_fusion.1), channel_id=1, source_target_pairs={{0,2},{2,4},{4,6},{6,8},{8,10},{10,12},{12,14},{1,3},{3,5},{5,7},{... | collective-permute-start | bytes 172040 | tf_op jit(solution)/shard_map/ppermute | solution.py:280
  27.9 0.0 copy-start.2
  27.9 1.0 copy-done.2
  28.9 0.0 copy-start.4
  28.9 0.8 copy-done.4
  29.7 2.7 %shard_map.55 = f32[16,64,128]{2,1,0:T(8,128)} custom-call(f32[4,3,8,1024]{3,2,1,0:T(8,128)S(1)} %copy-done.2, s32[8,1024]{1,0:T(8,128)S(1)} %copy-done.4), custom_call_target="tpu_custom_call" | custom-call | tf_op jit(solution)/shard_map/pallas_call | solution.py:281
  32.4 0.0 collective-permute-done.2
  32.4 0.0 collective-permute-done.1
  32.4 16.5 %all-to-all-start = ((f32[16,64,128]{2,1,0:T(8,128)}), f32[16,64,128]{2,1,0:T(8,128)S(1)}, u32[]{:S(2)}, u32[]{:S(2)}) async-start(f32[16,64,128]{2,1,0:T(8,128)} %shard_map.55), calls=%async_computation | async-start | bytes 1048576 | tf_op jit(solution)/shard_map/all_to_all | solution.py:289
  48.9 2.6 %collective-permute-start.5 = (f32[336,128]{1,0:T(8,128)S(1)}, f32[336,128]{1,0:T(8,128)S(1)}, u32[]{:S(2)}, u32[]{:S(2)}) collective-permute-start(f32[336,128]{1,0:T(8,128)S(1)} %pad_maximum_fusion), channel_id=1, source_target_pairs={{0,48},{16,0},{32,16},{48,32},{1,49},{17,1},{33,17},{49,33},{2,50}... | collective-permute-start | bytes 516104 | tf_op jit(solution)/shard_map/ppermute | solution.py:292
  51.6 1.9 %collective-permute-start.4 = (f32[336,128]{1,0:T(8,128)S(1)}, f32[336,128]{1,0:T(8,128)S(1)}, u32[]{:S(2)}, u32[]{:S(2)}) collective-permute-start(f32[336,128]{1,0:T(8,128)S(1)} %pad_maximum_fusion), channel_id=1, source_target_pairs={{0,32},{16,48},{32,0},{48,16},{1,33},{17,49},{33,1},{49,17},{2,34}... | collective-permute-start | bytes 516104 | tf_op jit(solution)/shard_map/ppermute | solution.py:292
  53.5 2.7 %collective-permute-start.3 = (f32[336,128]{1,0:T(8,128)S(1)}, f32[336,128]{1,0:T(8,128)S(1)}, u32[]{:S(2)}, u32[]{:S(2)}) collective-permute-start(f32[336,128]{1,0:T(8,128)S(1)} %pad_maximum_fusion), channel_id=1, source_target_pairs={{0,16},{16,32},{32,48},{48,0},{1,17},{17,33},{33,49},{49,1},{2,18}... | collective-permute-start | bytes 516104 | tf_op jit(solution)/shard_map/ppermute | solution.py:292
  56.2 8.7 %collective-permute-done.3 = f32[336,128]{1,0:T(8,128)S(1)} collective-permute-done((f32[336,128]{1,0:T(8,128)S(1)}, f32[336,128]{1,0:T(8,128)S(1)}, u32[]{:S(2)}, u32[]{:S(2)}) %collective-permute-start.3) | collective-permute-done | bytes 172064 | tf_op jit(solution)/shard_map/ppermute | solution.py:292
  65.0 0.0 collective-permute-done.4
  65.0 0.0 collective-permute-done.5
  65.0 2.4 %collective-permute-start.6 = (f32[1344,128]{1,0:T(8,128)S(1)}, f32[1344,128]{1,0:T(8,128)S(1)}, u32[]{:S(2)}, u32[]{:S(2)}) collective-permute-start(f32[1344,128]{1,0:T(8,128)S(1)} %constant_dynamic-update-slice_fusion.strip_ref), channel_id=1, source_target_pairs={{0,1},{1,0},{2,3},{3,2},{4,5},{5,4},{6,7},{7,6},{8,9},{9,8},{10,11... | collective-permute-start | bytes 2064392 | tf_op jit(solution)/shard_map/ppermute | solution.py:294
  67.4 0.1 pad_add_fusion.core_ref
  67.5 0.0 copy-start.6
  67.5 1.7 %collective-permute-done.6.other_ref = f32[1344,128]{1,0:T(8,128)S(1)} collective-permute-done((f32[1344,128]{1,0:T(8,128)S(1)}, f32[1344,128]{1,0:T(8,128)S(1)}, u32[]{:S(2)}, u32[]{:S(2)}) %collective-permute-start.6) | collective-permute-done | bytes 688160 | tf_op jit(solution)/shard_map/ppermute | solution.py:294
  69.2 17.6 %shard_map.57.coef = f32[8,15,5,56,128]{4,3,2,1,0:T(8,128)S(1)} custom-call(s32[2]{0:T(128)S(1)} %pad_add_fusion.core_ref, f32[1344,128]{1,0:T(8,128)S(1)} %constant_dynamic-update-slice_fusion.strip_ref, f32[1344,128]{1,0:T(8,128)S(1)} %collective-permute-done.6.other_ref), custom_call_target="tpu_custom_call" | custom-call | flops 2000000000 | bytes 50000000 | tf_op jit(solution)/shard_map/pallas_call | solution.py:295
  86.8 0.0 copy-start
  86.8 5.9 %copy-done = f32[8,15,5,56,128]{4,3,2,1,0:T(8,128)} copy-done((f32[8,15,5,56,128]{4,3,2,1,0:T(8,128)}, f32[8,15,5,56,128]{4,3,2,1,0:T(8,128)S(1)}, u32[]{:S(2)}) %copy-start) | copy-done | bytes 17203224
  92.7 0.0 all-to-all-done
  92.7 1.3 collective-permute-start.8
  94.0 4.0 %collective-permute-start.7 = (f32[16,64,128]{2,1,0:T(8,128)S(1)}, f32[16,64,128]{2,1,0:T(8,128)S(1)}, u32[]{:S(2)}, u32[]{:S(2)}) collective-permute-start(f32[16,64,128]{2,1,0:T(8,128)S(1)} %all-to-all-done), channel_id=1, source_target_pairs={{0,2},{2,4},{4,6},{6,8},{8,10},{10,12},{12,14},{1,3},{3,5},{5,7},{... | collective-permute-start | bytes 1572872 | tf_op jit(solution)/shard_map/ppermute | solution.py:308
  98.0 9.7 %collective-permute-done.8 = f32[16,64,128]{2,1,0:T(8,128)S(1)} collective-permute-done((f32[16,64,128]{2,1,0:T(8,128)S(1)}, f32[16,64,128]{2,1,0:T(8,128)S(1)}, u32[]{:S(2)}, u32[]{:S(2)}) %collective-permute-start.8) | collective-permute-done | bytes 524320 | tf_op jit(solution)/shard_map/ppermute | solution.py:308
  107.7 0.9 collective-permute-done.7
  108.6 0.0 copy-start.1
  108.6 5.9 %copy-done.1 = f32[8,15,5,56,128]{4,3,2,1,0:T(8,128)S(1)} copy-done((f32[8,15,5,56,128]{4,3,2,1,0:T(8,128)S(1)}, f32[8,15,5,56,128]{4,3,2,1,0:T(8,128)}, u32[]{:S(2)}) %copy-start.1) | copy-done | bytes 17203224
  114.5 13.8 %shard_map.58 = f32[8,96,128]{2,1,0:T(8,128)S(1)} custom-call(f32[1024,128]{1,0:T(8,128)S(1)} %bitcast.13, f32[1024,128]{1,0:T(8,128)S(1)} %bitcast.10, f32[1024,128]{1,0:T(8,128)S(1)} %bitcast.12, f32[8,15,5,56,128]{4,3,2,1,0:T(8,128)S(1)} %copy-done.1), custom_call_target="tpu_custom_call" | custom-call | tf_op jit(solution)/shard_map/pallas_call | solution.py:310
  128.3 12.0 %all_to_all.10 = f32[8,96,128]{2,1,0:T(8,128)S(1)} all-to-all(f32[8,96,128]{2,1,0:T(8,128)S(1)} %shard_map.58), channel_id=1, replica_groups=mesh['y'=4,'zh'=2,'x'=4,'zl'=8,'c'=2] {'x','c'}, dimensions={0} | all-to-all | bytes 786432 | tf_op jit(solution)/shard_map/all_to_all | solution.py:322
  140.3 0.0 copy-done.6
  140.3 1.3 shard_map.59
  (10 shorter events, 0.1 us)
Async XLA Ops:
  0.0 0.8 copy-start.3
  0.8 0.9 copy-start.5
  1.7 0.7 copy-start.7
  2.9 19.7 %collective-permute-start = (f32[48,128]{1,0:T(8,128)S(1)}, f32[48,128]{1,0:T(8,128)S(1)}, u32[]{:S(2)}, u32[]{:S(2)}) collective-permute-start(f32[48,128]{1,0:T(8,128)S(1)} %slice.4), channel_id=1, source_target_pairs={{48,112},{0,448},{112,176},{64,0},{176,240},{128,64},{240,304},{19... | collective-permute-start | bytes 73736 | tf_op jit(solution)/shard_map/ppermute | solution.py:278
  22.6 9.8 %collective-permute-start.2 = (f32[112,128]{1,0:T(8,128)S(1)}, f32[112,128]{1,0:T(8,128)S(1)}, u32[]{:S(2)}, u32[]{:S(2)}) collective-permute-start(f32[112,128]{1,0:T(8,128)S(1)} %pad_maximum_fusion.1), channel_id=1, source_target_pairs={{2,0},{4,2},{6,4},{8,6},{10,8},{12,10},{14,12},{3,1},{5,3},{7,5},{... | collective-permute-start | bytes 172040 | tf_op jit(solution)/shard_map/ppermute | solution.py:280
  23.9 8.5 %collective-permute-start.1 = (f32[112,128]{1,0:T(8,128)S(1)}, f32[112,128]{1,0:T(8,128)S(1)}, u32[]{:S(2)}, u32[]{:S(2)}) collective-permute-start(f32[112,128]{1,0:T(8,128)S(1)} %pad_maximum_fusion.1), channel_id=1, source_target_pairs={{0,2},{2,4},{4,6},{6,8},{8,10},{10,12},{12,14},{1,3},{3,5},{5,7},{... | collective-permute-start | bytes 172040 | tf_op jit(solution)/shard_map/ppermute | solution.py:280
  27.9 1.0 copy-start.2
  28.9 0.8 copy-start.4
  32.4 60.3 %all-to-all-start = ((f32[16,64,128]{2,1,0:T(8,128)}), f32[16,64,128]{2,1,0:T(8,128)S(1)}, u32[]{:S(2)}, u32[]{:S(2)}) async-start(f32[16,64,128]{2,1,0:T(8,128)} %shard_map.55), calls=%async_computation | async-start | bytes 1048576 | tf_op jit(solution)/shard_map/all_to_all | solution.py:289
  48.9 16.1 %collective-permute-start.5 = (f32[336,128]{1,0:T(8,128)S(1)}, f32[336,128]{1,0:T(8,128)S(1)}, u32[]{:S(2)}, u32[]{:S(2)}) collective-permute-start(f32[336,128]{1,0:T(8,128)S(1)} %pad_maximum_fusion), channel_id=1, source_target_pairs={{0,48},{16,0},{32,16},{48,32},{1,49},{17,1},{33,17},{49,33},{2,50}... | collective-permute-start | bytes 516104 | tf_op jit(solution)/shard_map/ppermute | solution.py:292
  51.6 13.4 %collective-permute-start.4 = (f32[336,128]{1,0:T(8,128)S(1)}, f32[336,128]{1,0:T(8,128)S(1)}, u32[]{:S(2)}, u32[]{:S(2)}) collective-permute-start(f32[336,128]{1,0:T(8,128)S(1)} %pad_maximum_fusion), channel_id=1, source_target_pairs={{0,32},{16,48},{32,0},{48,16},{1,33},{17,49},{33,1},{49,17},{2,34}... | collective-permute-start | bytes 516104 | tf_op jit(solution)/shard_map/ppermute | solution.py:292
  53.5 11.5 %collective-permute-start.3 = (f32[336,128]{1,0:T(8,128)S(1)}, f32[336,128]{1,0:T(8,128)S(1)}, u32[]{:S(2)}, u32[]{:S(2)}) collective-permute-start(f32[336,128]{1,0:T(8,128)S(1)} %pad_maximum_fusion), channel_id=1, source_target_pairs={{0,16},{16,32},{32,48},{48,0},{1,17},{17,33},{33,49},{49,1},{2,18}... | collective-permute-start | bytes 516104 | tf_op jit(solution)/shard_map/ppermute | solution.py:292
  65.0 4.1 %collective-permute-start.6 = (f32[1344,128]{1,0:T(8,128)S(1)}, f32[1344,128]{1,0:T(8,128)S(1)}, u32[]{:S(2)}, u32[]{:S(2)}) collective-permute-start(f32[1344,128]{1,0:T(8,128)S(1)} %constant_dynamic-update-slice_fusion.strip_ref), channel_id=1, source_target_pairs={{0,1},{1,0},{2,3},{3,2},{4,5},{5,4},{6,7},{7,6},{8,9},{9,8},{10,11... | collective-permute-start | bytes 2064392 | tf_op jit(solution)/shard_map/ppermute | solution.py:294
  67.5 72.8 %copy-start.6 = (f32[128,128]{1,0:T(8,128)S(1)}, f32[128,128]{1,0:T(8,128)}, u32[]{:S(2)}) copy-start(f32[128,128]{1,0:T(8,128)} %coef_ref.1) | copy-start | bytes 196612
  86.8 5.9 %copy-start = (f32[8,15,5,56,128]{4,3,2,1,0:T(8,128)}, f32[8,15,5,56,128]{4,3,2,1,0:T(8,128)S(1)}, u32[]{:S(2)}) copy-start(f32[8,15,5,56,128]{4,3,2,1,0:T(8,128)S(1)} %shard_map.57.coef) | copy-start | bytes 51609604
  92.7 15.0 %collective-permute-start.8 = (f32[16,64,128]{2,1,0:T(8,128)S(1)}, f32[16,64,128]{2,1,0:T(8,128)S(1)}, u32[]{:S(2)}, u32[]{:S(2)}) collective-permute-start(f32[16,64,128]{2,1,0:T(8,128)S(1)} %all-to-all-done), channel_id=1, source_target_pairs={{2,0},{4,2},{6,4},{8,6},{10,8},{12,10},{14,12},{3,1},{5,3},{7,5},{... | collective-permute-start | bytes 1572872 | tf_op jit(solution)/shard_map/ppermute | solution.py:308
  94.0 14.6 %collective-permute-start.7 = (f32[16,64,128]{2,1,0:T(8,128)S(1)}, f32[16,64,128]{2,1,0:T(8,128)S(1)}, u32[]{:S(2)}, u32[]{:S(2)}) collective-permute-start(f32[16,64,128]{2,1,0:T(8,128)S(1)} %all-to-all-done), channel_id=1, source_target_pairs={{0,2},{2,4},{4,6},{6,8},{8,10},{10,12},{12,14},{1,3},{3,5},{5,7},{... | collective-permute-start | bytes 1572872 | tf_op jit(solution)/shard_map/ppermute | solution.py:308
  108.6 5.9 %copy-start.1 = (f32[8,15,5,56,128]{4,3,2,1,0:T(8,128)S(1)}, f32[8,15,5,56,128]{4,3,2,1,0:T(8,128)}, u32[]{:S(2)}) copy-start(f32[8,15,5,56,128]{4,3,2,1,0:T(8,128)} %copy-done) | copy-start | bytes 51609604

commit v10 on v8

--- a/solution.py
+++ b/solution.py
@@ -93,7 +93,7 @@
     lax.fori_loop(0, 2, send, None)
 
 
-def coef_kernel(core_ref, strip_ref, other_ref, coef, base, wet):
+def coef_kernel(core_ref, strip_ref, other_ref, coef, base, lines, spread_matrix):
     lane = lax.broadcasted_iota(jnp.int32, (8, LANES), 1)
     core, me = core_ref[0], core_ref[1]
     blocks = [lax.rem(me - x + 4, 4) * 336 for x in range(4)]
@@ -104,8 +104,8 @@
             top = pl.multiple_of((1 - core if other else core) * 8 + z * 16, 8)
             strips.append((ref, z * 112, top))
             at = z * 112 + 48
-            for j in range(PARTS):
-                wet[j, pl.ds(top, 8), :] = spread(ref[at : at + 8, :], ref[at + 8 : at + 16, :], j, lane) * 0.25
+            lines[STEPS, pl.ds(top, 8), :LANES] = ref[at : at + 8, :]
+            lines[STEPS, pl.ds(top, 8), LANES:] = ref[at + 8 : at + 16, :]
 
     def unpack(part, _):
         high, f = part // 3, part % 3
@@ -119,14 +119,37 @@
                 left = pltpu.roll(quads[4], (96 - 32 * low) % 128, 1)
                 right = pltpu.roll(quads[5], (128 - 32 * low) % 128, 1)
                 halo = halo_columns(left, right, lane)
-                for j in range(PARTS):
-                    base[high * 4 + low, f, j, pl.ds(top + 8, 8), :] = spread(out, halo, j, lane)
+                rows = pl.ds(pl.multiple_of(f * TALL + top, 8), 8)
+                lines[high * 4 + low, rows, :LANES] = out
+                lines[high * 4 + low, rows, LANES:] = halo
 
     lax.fori_loop(0, 6, unpack, None)
+
+    place = lax.broadcasted_iota(jnp.int32, (2 * LANES, LANES), 0)
+    column = jnp.where(place < LANES, place, jnp.where(place < LANES + 16, place, place - 2 * LANES))
+    target = lax.broadcasted_iota(jnp.int32, (2 * LANES, LANES), 1) % 32 * PARTS - HALO
+    for j in range(PARTS):
+        spread_matrix[:, j * LANES : (j + 1) * LANES] = (column == target + j).astype(jnp.bfloat16)
+
+    def spread_lines(step, _):
+        cells = lines[step]
+        high = cells.astype(jnp.bfloat16)
+        rest = cells - high.astype(f32)
+        mid = rest.astype(jnp.bfloat16)
+        low = (rest - mid.astype(f32)).astype(jnp.bfloat16)
+        out = [jnp.dot(x, spread_matrix[...], preferred_element_type=f32) for x in (high, mid, low)]
+        out = (out[0] + out[1]) + out[2]
+        for j in range(PARTS):
+            for f in range(3):
+                part = out[f * TALL : (f + 1) * TALL, j * LANES : (j + 1) * LANES]
+                base[step, f, j, 8 : TALL + 8, :] = part
+        return _
+
+    lax.fori_loop(0, STEPS + 1, spread_lines, None)
 
     def prepare(step, tile):
         top = pl.multiple_of(tile * 8, 8)
-        w = [wet[v, pl.ds(top, 8), :] for v in range(PARTS)]
+        w = [base[STEPS, 0, v, pl.ds(top + 8, 8), :] * 0.25 for v in range(PARTS)]
 
         def rows(f, shift):
             return [base[step, f, v, pl.ds(top + 8 + shift, 8), :] for v in range(PARTS)]
@@ -299,8 +322,9 @@
         in_specs=[SMEM, VMEM, VMEM],
         out_specs=VMEM,
         scratch_shapes=[
-            pltpu.VMEM((STEPS, 3, PARTS, TALL + 16, LANES), f32),
-            pltpu.VMEM((PARTS, TALL, LANES), f32),
+            pltpu.VMEM((STEPS + 1, 3, PARTS, TALL + 16, LANES), f32),
+            pltpu.VMEM((STEPS + 1, 3 * TALL, 2 * LANES), f32),
+            pltpu.VMEM((2 * LANES, PARTS * LANES), jnp.bfloat16),
         ],
         compiler_params=pltpu.CompilerParams(vmem_limit_bytes=32 * 2**20),
         cost_estimate=pl.CostEstimate(flops=2 * 10**9, bytes_accessed=50 * 10**6, transcendentals=0),

time: 134 us -> 129 us (0.963)
  Pallas kernels: 36.1 us -> 27.2 us
  waiting for transfers between devices: 9.03 us -> 12.8 us
    pallas_call x1, Pallas kernels: 17.6 us -> 8.7 us  [on_device(): pl.pallas_call(coef_kernel, out_shape=jax.ShapeDtypeStruct((STEPS, COEFS,...]
    ppermute x2, waiting for transfers between devices: 0.01 us -> 3.77 us  [on_device(): parts = [lax.ppermute(own, 'zl', up), own, lax.ppermute(own, 'zl', down)]]
  transfers between devices with their start and end apart: 10 -> 10, of which waited for: 4 -> 5; matrix products, arithmetic and copies ran while one was open for 0% -> 0% of each run, Pallas kernels for 15% -> 9%
where the time goes in v10:
time: 129 us
  starting transfers between devices  71.6 us (56%)
  Pallas kernels  27.2 us (21%)
  waiting for transfers between devices  12.8 us (10%)
  blocking collectives  12.8 us (10%)
  local copies, waits for them, and re-layouts  4.12 us (3%)
    ppermute x2, starting transfers between devices, on_device(): parts = [lax.ppermute(own, 'zl', up), own, lax.ppermute(own, 'zl', down)]  20.9 us
    ppermute x1, starting transfers between devices, on_device(): halo = lax.ppermute(raw[:48], ('y', 'zh', 'x'), ring)  18.7 us
    all_to_all x1, starting transfers between devices, on_device(): own = lax.all_to_all(send, ('y', 'zh', 'c'), 0, 0, tiled=True)  16.5 us
    pallas_call x1, Pallas kernels, on_device(): pl.pallas_call(march_kernel, out_shape=jax.ShapeDtypeStruct((8, 96, LANES...  13.8 us
    all_to_all x1, blocking collectives, on_device(): cells = lax.all_to_all(out, ('x', 'c'), 0, 0, tiled=True)  12.8 us
    pallas_call x1, Pallas kernels, on_device(): pl.pallas_call(coef_kernel, out_shape=jax.ShapeDtypeStruct((STEPS, COEFS,...  8.7 us
    ppermute x3, starting transfers between devices, on_device(): lax.ppermute(chips, 'x', [(i, (i + k) % 4) for i in range(4)])  8.44 us
    ppermute x3, waiting for transfers between devices, on_device(): lax.ppermute(chips, 'x', [(i, (i + k) % 4) for i in range(4)])  6.35 us
  transfers between devices with their start and end apart: 10, of which 5 were waited for; matrix products, arithmetic and copies ran while one was open for 0% of the time, Pallas kernels for 9%

profile of v10, /device:TPU:1, one launch (start us, length us, event | category | flops | bytes accessed | tf_op | source)
XLA Modules:
  0.0 128.8 jit_solution(18173772515803527162)
XLA Ops:
  0.0 0.0 copy-start.1
  0.0 0.8 copy-done.1
  0.8 0.0 copy-start.3
  0.8 0.9 copy-done.3
  1.7 0.0 copy-start.5
  1.7 0.7 copy-done.5
  2.3 0.6 shard_map.56
  2.9 18.7 %collective-permute-start = (f32[48,128]{1,0:T(8,128)S(1)}, f32[48,128]{1,0:T(8,128)S(1)}, u32[]{:S(2)}, u32[]{:S(2)}) collective-permute-start(f32[48,128]{1,0:T(8,128)S(1)} %slice.4), channel_id=1, source_target_pairs={{48,112},{0,448},{112,176},{64,0},{176,240},{128,64},{240,304},{19... | collective-permute-start | bytes 73736 | tf_op jit(solution)/shard_map/ppermute | solution.py:301
  21.7 0.9 collective-permute-done
  22.6 2.6 %collective-permute-start.1 = (f32[112,128]{1,0:T(8,128)S(1)}, f32[112,128]{1,0:T(8,128)S(1)}, u32[]{:S(2)}, u32[]{:S(2)}) collective-permute-start(f32[112,128]{1,0:T(8,128)S(1)} %pad_maximum_fusion.1), channel_id=1, source_target_pairs={{0,2},{2,4},{4,6},{6,8},{8,10},{10,12},{12,14},{1,3},{3,5},{5,7},{... | collective-permute-start | bytes 172040 | tf_op jit(solution)/shard_map/ppermute | solution.py:303
  25.2 1.3 %collective-permute-start.2 = (f32[112,128]{1,0:T(8,128)S(1)}, f32[112,128]{1,0:T(8,128)S(1)}, u32[]{:S(2)}, u32[]{:S(2)}) collective-permute-start(f32[112,128]{1,0:T(8,128)S(1)} %pad_maximum_fusion.1), channel_id=1, source_target_pairs={{2,0},{4,2},{6,4},{8,6},{10,8},{12,10},{14,12},{3,1},{5,3},{7,5},{... | collective-permute-start | bytes 172040 | tf_op jit(solution)/shard_map/ppermute | solution.py:303
  26.5 0.0 copy-start
  26.6 1.0 copy-done
  27.5 0.0 copy-start.2
  27.6 0.8 copy-done.2
  28.3 2.7 %shard_map.55 = f32[16,64,128]{2,1,0:T(8,128)} custom-call(f32[4,3,8,1024]{3,2,1,0:T(8,128)S(1)} %copy-done, s32[8,1024]{1,0:T(8,128)S(1)} %copy-done.2), custom_call_target="tpu_custom_call" | custom-call | tf_op jit(solution)/shard_map/pallas_call | solution.py:304
  31.0 0.0 collective-permute-done.1
  31.0 0.0 collective-permute-done.2
  31.1 16.5 %all-to-all-start = ((f32[16,64,128]{2,1,0:T(8,128)}), f32[16,64,128]{2,1,0:T(8,128)S(1)}, u32[]{:S(2)}, u32[]{:S(2)}) async-start(f32[16,64,128]{2,1,0:T(8,128)} %shard_map.55), calls=%async_computation | async-start | bytes 1048576 | tf_op jit(solution)/shard_map/all_to_all | solution.py:312
  47.6 1.9 %collective-permute-start.3 = (f32[336,128]{1,0:T(8,128)S(1)}, f32[336,128]{1,0:T(8,128)S(1)}, u32[]{:S(2)}, u32[]{:S(2)}) collective-permute-start(f32[336,128]{1,0:T(8,128)S(1)} %pad_maximum_fusion), channel_id=1, source_target_pairs={{0,16},{16,32},{32,48},{48,0},{1,17},{17,33},{33,49},{49,1},{2,18}... | collective-permute-start | bytes 516104 | tf_op jit(solution)/shard_map/ppermute | solution.py:315
  49.5 3.7 %collective-permute-start.4 = (f32[336,128]{1,0:T(8,128)S(1)}, f32[336,128]{1,0:T(8,128)S(1)}, u32[]{:S(2)}, u32[]{:S(2)}) collective-permute-start(f32[336,128]{1,0:T(8,128)S(1)} %pad_maximum_fusion), channel_id=1, source_target_pairs={{0,32},{16,48},{32,0},{48,16},{1,33},{17,49},{33,1},{49,17},{2,34}... | collective-permute-start | bytes 516104 | tf_op jit(solution)/shard_map/ppermute | solution.py:315
  53.2 2.8 %collective-permute-start.5 = (f32[336,128]{1,0:T(8,128)S(1)}, f32[336,128]{1,0:T(8,128)S(1)}, u32[]{:S(2)}, u32[]{:S(2)}) collective-permute-start(f32[336,128]{1,0:T(8,128)S(1)} %pad_maximum_fusion), channel_id=1, source_target_pairs={{0,48},{16,0},{32,16},{48,32},{1,49},{17,1},{33,17},{49,33},{2,50}... | collective-permute-start | bytes 516104 | tf_op jit(solution)/shard_map/ppermute | solution.py:315
  56.1 4.2 %collective-permute-done.3 = f32[336,128]{1,0:T(8,128)S(1)} collective-permute-done((f32[336,128]{1,0:T(8,128)S(1)}, f32[336,128]{1,0:T(8,128)S(1)}, u32[]{:S(2)}, u32[]{:S(2)}) %collective-permute-start.3) | collective-permute-done | bytes 172064 | tf_op jit(solution)/shard_map/ppermute | solution.py:315
  60.4 0.0 collective-permute-done.4
  60.4 2.1 %collective-permute-done.5 = f32[336,128]{1,0:T(8,128)S(1)} collective-permute-done((f32[336,128]{1,0:T(8,128)S(1)}, f32[336,128]{1,0:T(8,128)S(1)}, u32[]{:S(2)}, u32[]{:S(2)}) %collective-permute-start.5) | collective-permute-done | bytes 172064 | tf_op jit(solution)/shard_map/ppermute | solution.py:315
  62.5 3.1 %collective-permute-start.6 = (f32[1344,128]{1,0:T(8,128)S(1)}, f32[1344,128]{1,0:T(8,128)S(1)}, u32[]{:S(2)}, u32[]{:S(2)}) collective-permute-start(f32[1344,128]{1,0:T(8,128)S(1)} %constant_dynamic-update-slice_fusion.strip_ref), channel_id=1, source_target_pairs={{0,1},{1,0},{2,3},{3,2},{4,5},{5,4},{6,7},{7,6},{8,9},{9,8},{10,11... | collective-permute-start | bytes 2064392 | tf_op jit(solution)/shard_map/ppermute | solution.py:317
  65.6 1.7 %collective-permute-done.6.other_ref = f32[1344,128]{1,0:T(8,128)S(1)} collective-permute-done((f32[1344,128]{1,0:T(8,128)S(1)}, f32[1344,128]{1,0:T(8,128)S(1)}, u32[]{:S(2)}, u32[]{:S(2)}) %collective-permute-start.6) | collective-permute-done | bytes 688160 | tf_op jit(solution)/shard_map/ppermute | solution.py:317
  67.4 0.0 all-to-all-done
  67.4 19.6 %collective-permute-start.7 = (f32[16,64,128]{2,1,0:T(8,128)S(1)}, f32[16,64,128]{2,1,0:T(8,128)S(1)}, u32[]{:S(2)}, u32[]{:S(2)}) collective-permute-start(f32[16,64,128]{2,1,0:T(8,128)S(1)} %all-to-all-done), channel_id=1, source_target_pairs={{0,2},{2,4},{4,6},{6,8},{8,10},{10,12},{12,14},{1,3},{3,5},{5,7},{... | collective-permute-start | bytes 1572872 | tf_op jit(solution)/shard_map/ppermute | solution.py:332
  87.0 1.3 %collective-permute-start.8 = (f32[16,64,128]{2,1,0:T(8,128)S(1)}, f32[16,64,128]{2,1,0:T(8,128)S(1)}, u32[]{:S(2)}, u32[]{:S(2)}) collective-permute-start(f32[16,64,128]{2,1,0:T(8,128)S(1)} %all-to-all-done), channel_id=1, source_target_pairs={{2,0},{4,2},{6,4},{8,6},{10,8},{12,10},{14,12},{3,1},{5,3},{7,5},{... | collective-permute-start | bytes 1572872 | tf_op jit(solution)/shard_map/ppermute | solution.py:332
  88.3 0.1 pad_add_fusion.core_ref
  88.4 0.0 copy-start.4
  88.4 8.7 %shard_map.57.coef = f32[8,15,5,56,128]{4,3,2,1,0:T(8,128)S(1)} custom-call(s32[2]{0:T(128)S(1)} %pad_add_fusion.core_ref, f32[1344,128]{1,0:T(8,128)S(1)} %constant_dynamic-update-slice_fusion.strip_ref, f32[1344,128]{1,0:T(8,128)S(1)} %collective-permute-done.6.other_ref), custom_call_target="tpu_custom_call" | custom-call | flops 2000000000 | bytes 50000000 | tf_op jit(solution)/shard_map/pallas_call | solution.py:319
  97.1 0.0 collective-permute-done.7
  97.1 3.8 %collective-permute-done.8 = f32[16,64,128]{2,1,0:T(8,128)S(1)} collective-permute-done((f32[16,64,128]{2,1,0:T(8,128)S(1)}, f32[16,64,128]{2,1,0:T(8,128)S(1)}, u32[]{:S(2)}, u32[]{:S(2)}) %collective-permute-start.8) | collective-permute-done | bytes 524320 | tf_op jit(solution)/shard_map/ppermute | solution.py:332
  100.8 13.8 %shard_map.58 = f32[8,96,128]{2,1,0:T(8,128)S(1)} custom-call(f32[1024,128]{1,0:T(8,128)S(1)} %bitcast.12, f32[1024,128]{1,0:T(8,128)S(1)} %bitcast.10, f32[1024,128]{1,0:T(8,128)S(1)} %bitcast.13, f32[8,15,5,56,128]{4,3,2,1,0:T(8,128)S(1)} %shard_map.57.coef), custom_call_target="tpu_custom_call" | custom-call | tf_op jit(solution)/shard_map/pallas_call | solution.py:334
  114.7 12.8 %all_to_all.10 = f32[8,96,128]{2,1,0:T(8,128)S(1)} all-to-all(f32[8,96,128]{2,1,0:T(8,128)S(1)} %shard_map.58), channel_id=1, replica_groups=mesh['y'=4,'zh'=2,'x'=4,'zl'=8,'c'=2] {'x','c'}, dimensions={0} | all-to-all | bytes 786432 | tf_op jit(solution)/shard_map/all_to_all | solution.py:346
  127.5 0.0 copy-done.4
  127.5 1.3 shard_map.59
  (10 shorter events, 0.1 us)
Async XLA Ops:
  0.0 0.8 copy-start.1
  0.8 0.9 copy-start.3
  1.7 0.7 copy-start.5
  2.9 19.7 %collective-permute-start = (f32[48,128]{1,0:T(8,128)S(1)}, f32[48,128]{1,0:T(8,128)S(1)}, u32[]{:S(2)}, u32[]{:S(2)}) collective-permute-start(f32[48,128]{1,0:T(8,128)S(1)} %slice.4), channel_id=1, source_target_pairs={{48,112},{0,448},{112,176},{64,0},{176,240},{128,64},{240,304},{19... | collective-permute-start | bytes 73736 | tf_op jit(solution)/shard_map/ppermute | solution.py:301
  22.6 8.4 %collective-permute-start.1 = (f32[112,128]{1,0:T(8,128)S(1)}, f32[112,128]{1,0:T(8,128)S(1)}, u32[]{:S(2)}, u32[]{:S(2)}) collective-permute-start(f32[112,128]{1,0:T(8,128)S(1)} %pad_maximum_fusion.1), channel_id=1, source_target_pairs={{0,2},{2,4},{4,6},{6,8},{8,10},{10,12},{12,14},{1,3},{3,5},{5,7},{... | collective-permute-start | bytes 172040 | tf_op jit(solution)/shard_map/ppermute | solution.py:303
  25.2 5.8 %collective-permute-start.2 = (f32[112,128]{1,0:T(8,128)S(1)}, f32[112,128]{1,0:T(8,128)S(1)}, u32[]{:S(2)}, u32[]{:S(2)}) collective-permute-start(f32[112,128]{1,0:T(8,128)S(1)} %pad_maximum_fusion.1), channel_id=1, source_target_pairs={{2,0},{4,2},{6,4},{8,6},{10,8},{12,10},{14,12},{3,1},{5,3},{7,5},{... | collective-permute-start | bytes 172040 | tf_op jit(solution)/shard_map/ppermute | solution.py:303
  26.5 1.0 copy-start
  27.5 0.8 copy-start.2
  31.1 36.3 %all-to-all-start = ((f32[16,64,128]{2,1,0:T(8,128)}), f32[16,64,128]{2,1,0:T(8,128)S(1)}, u32[]{:S(2)}, u32[]{:S(2)}) async-start(f32[16,64,128]{2,1,0:T(8,128)} %shard_map.55), calls=%async_computation | async-start | bytes 1048576 | tf_op jit(solution)/shard_map/all_to_all | solution.py:312
  47.6 12.7 %collective-permute-start.3 = (f32[336,128]{1,0:T(8,128)S(1)}, f32[336,128]{1,0:T(8,128)S(1)}, u32[]{:S(2)}, u32[]{:S(2)}) collective-permute-start(f32[336,128]{1,0:T(8,128)S(1)} %pad_maximum_fusion), channel_id=1, source_target_pairs={{0,16},{16,32},{32,48},{48,0},{1,17},{17,33},{33,49},{49,1},{2,18}... | collective-permute-start | bytes 516104 | tf_op jit(solution)/shard_map/ppermute | solution.py:315
  49.5 10.8 %collective-permute-start.4 = (f32[336,128]{1,0:T(8,128)S(1)}, f32[336,128]{1,0:T(8,128)S(1)}, u32[]{:S(2)}, u32[]{:S(2)}) collective-permute-start(f32[336,128]{1,0:T(8,128)S(1)} %pad_maximum_fusion), channel_id=1, source_target_pairs={{0,32},{16,48},{32,0},{48,16},{1,33},{17,49},{33,1},{49,17},{2,34}... | collective-permute-start | bytes 516104 | tf_op jit(solution)/shard_map/ppermute | solution.py:315
  53.2 9.3 %collective-permute-start.5 = (f32[336,128]{1,0:T(8,128)S(1)}, f32[336,128]{1,0:T(8,128)S(1)}, u32[]{:S(2)}, u32[]{:S(2)}) collective-permute-start(f32[336,128]{1,0:T(8,128)S(1)} %pad_maximum_fusion), channel_id=1, source_target_pairs={{0,48},{16,0},{32,16},{48,32},{1,49},{17,1},{33,17},{49,33},{2,50}... | collective-permute-start | bytes 516104 | tf_op jit(solution)/shard_map/ppermute | solution.py:315
  62.5 4.9 %collective-permute-start.6 = (f32[1344,128]{1,0:T(8,128)S(1)}, f32[1344,128]{1,0:T(8,128)S(1)}, u32[]{:S(2)}, u32[]{:S(2)}) collective-permute-start(f32[1344,128]{1,0:T(8,128)S(1)} %constant_dynamic-update-slice_fusion.strip_ref), channel_id=1, source_target_pairs={{0,1},{1,0},{2,3},{3,2},{4,5},{5,4},{6,7},{7,6},{8,9},{9,8},{10,11... | collective-permute-start | bytes 2064392 | tf_op jit(solution)/shard_map/ppermute | solution.py:317
  67.4 29.7 %collective-permute-start.7 = (f32[16,64,128]{2,1,0:T(8,128)S(1)}, f32[16,64,128]{2,1,0:T(8,128)S(1)}, u32[]{:S(2)}, u32[]{:S(2)}) collective-permute-start(f32[16,64,128]{2,1,0:T(8,128)S(1)} %all-to-all-done), channel_id=1, source_target_pairs={{0,2},{2,4},{4,6},{6,8},{8,10},{10,12},{12,14},{1,3},{3,5},{5,7},{... | collective-permute-start | bytes 1572872 | tf_op jit(solution)/shard_map/ppermute | solution.py:332
  87.0 13.9 %collective-permute-start.8 = (f32[16,64,128]{2,1,0:T(8,128)S(1)}, f32[16,64,128]{2,1,0:T(8,128)S(1)}, u32[]{:S(2)}, u32[]{:S(2)}) collective-permute-start(f32[16,64,128]{2,1,0:T(8,128)S(1)} %all-to-all-done), channel_id=1, source_target_pairs={{2,0},{4,2},{6,4},{8,6},{10,8},{12,10},{14,12},{3,1},{5,3},{7,5},{... | collective-permute-start | bytes 1572872 | tf_op jit(solution)/shard_map/ppermute | solution.py:332
  88.4 39.2 %copy-start.4 = (f32[128,128]{1,0:T(8,128)S(1)}, f32[128,128]{1,0:T(8,128)}, u32[]{:S(2)}) copy-start(f32[128,128]{1,0:T(8,128)} %coef_ref.1) | copy-start | bytes 196612

commit v11 on v10

--- a/solution.py
+++ b/solution.py
@@ -88,7 +88,7 @@
             for i in range(8):
                 a, b, c, d = lines[4 * i : 4 * i + 4]
                 out = jnp.where(lane < 32, a, jnp.where(lane < 64, b, jnp.where(lane < 96, c, d)))
-                send_ref[2 * k + core, i * 8 : i * 8 + 8, :] = out
+                send_ref[(k % 2 * 4 + k // 2) * 2 + core, i * 8 : i * 8 + 8, :] = out
 
     lax.fori_loop(0, 2, send, None)
 
@@ -189,7 +189,7 @@
                     for j in range(PARTS):
                         i, odd = divmod(f * PARTS + j, 2)
                         one, two = (
-                            ref[pl.ds(pl.multiple_of((4 * quad + 2 * p + c) * 64 + i * 8, 8), 8), :] for p in range(2)
+                            ref[pl.ds(pl.multiple_of(((p * 4 + quad) * 2 + c) * 64 + i * 8, 8), 8), :] for p in range(2)
                         )
                         one, two = (pltpu.roll(one, 64, 1), two) if odd else (one, pltpu.roll(two, 64, 1))
                         rows = slice(z * 16 + c * 8, z * 16 + c * 8 + 8)
@@ -309,7 +309,7 @@
         compiler_params=pltpu.CompilerParams(vmem_limit_bytes=16 * 2**20),
     )(tangents, land_mask)
     send, above, below = lax.optimization_barrier((send, above, below))
-    own = lax.all_to_all(send, ("y", "zh", "c"), 0, 0, tiled=True)
+    own = lax.all_to_all(send, ("zh", "y", "c"), 0, 0, tiled=True)
     chips = jnp.concatenate([above, wide, below], axis=0)
     strip = jnp.concatenate(
         [chips] + [lax.ppermute(chips, "x", [(i, (i + k) % 4) for i in range(4)]) for k in (1, 2, 3)], axis=0

time: 129 us -> 129 us (level)
  no operation moved by 1% of the time
where the time goes in v11:
time: 129 us
  starting transfers between devices  71.6 us (56%)
  Pallas kernels  27.2 us (21%)
  waiting for transfers between devices  12.8 us (10%)
  blocking collectives  12.8 us (10%)
  local copies, waits for them, and re-layouts  4.12 us (3%)
    ppermute x2, starting transfers between devices, on_device(): parts = [lax.ppermute(own, 'zl', up), own, lax.ppermute(own, 'zl', down)]  20.9 us
    ppermute x1, starting transfers between devices, on_device(): halo = lax.ppermute(raw[:48], ('y', 'zh', 'x'), ring)  18.7 us
    all_to_all x1, starting transfers between devices, on_device(): own = lax.all_to_all(send, ('zh', 'y', 'c'), 0, 0, tiled=True)  16.5 us
    pallas_call x1, Pallas kernels, on_device(): pl.pallas_call(march_kernel, out_shape=jax.ShapeDtypeStruct((8, 96, LANES...  13.8 us
    all_to_all x1, blocking collectives, on_device(): cells = lax.all_to_all(out, ('x', 'c'), 0, 0, tiled=True)  12.8 us
    pallas_call x1, Pallas kernels, on_device(): pl.pallas_call(coef_kernel, out_shape=jax.ShapeDtypeStruct((STEPS, COEFS,...  8.73 us
    ppermute x3, starting transfers between devices, on_device(): lax.ppermute(chips, 'x', [(i, (i + k) % 4) for i in range(4)])  8.44 us
    ppermute x3, waiting for transfers between devices, on_device(): lax.ppermute(chips, 'x', [(i, (i + k) % 4) for i in range(4)])  6.35 us
  transfers between devices with their start and end apart: 10, of which 5 were waited for; matrix products, arithmetic and copies ran while one was open for 0% of the time, Pallas kernels for 9%

profile of v11, /device:TPU:1, one launch (start us, length us, event | category | flops | bytes accessed | tf_op | source)
XLA Modules:
  0.0 128.8 jit_solution(2017078642675072456)
XLA Ops:
  0.0 0.0 copy-start.1
  0.0 0.8 copy-done.1
  0.8 0.0 copy-start.3
  0.8 0.9 copy-done.3
  1.7 0.0 copy-start.5
  1.7 0.7 copy-done.5
  2.3 0.6 shard_map.56
  2.9 18.7 %collective-permute-start = (f32[48,128]{1,0:T(8,128)S(1)}, f32[48,128]{1,0:T(8,128)S(1)}, u32[]{:S(2)}, u32[]{:S(2)}) collective-permute-start(f32[48,128]{1,0:T(8,128)S(1)} %slice.4), channel_id=1, source_target_pairs={{48,112},{0,448},{112,176},{64,0},{176,240},{128,64},{240,304},{19... | collective-permute-start | bytes 73736 | tf_op jit(solution)/shard_map/ppermute | solution.py:301
  21.7 0.9 collective-permute-done
  22.6 2.6 %collective-permute-start.1 = (f32[112,128]{1,0:T(8,128)S(1)}, f32[112,128]{1,0:T(8,128)S(1)}, u32[]{:S(2)}, u32[]{:S(2)}) collective-permute-start(f32[112,128]{1,0:T(8,128)S(1)} %pad_maximum_fusion.1), channel_id=1, source_target_pairs={{0,2},{2,4},{4,6},{6,8},{8,10},{10,12},{12,14},{1,3},{3,5},{5,7},{... | collective-permute-start | bytes 172040 | tf_op jit(solution)/shard_map/ppermute | solution.py:303
  25.2 1.3 %collective-permute-start.2 = (f32[112,128]{1,0:T(8,128)S(1)}, f32[112,128]{1,0:T(8,128)S(1)}, u32[]{:S(2)}, u32[]{:S(2)}) collective-permute-start(f32[112,128]{1,0:T(8,128)S(1)} %pad_maximum_fusion.1), channel_id=1, source_target_pairs={{2,0},{4,2},{6,4},{8,6},{10,8},{12,10},{14,12},{3,1},{5,3},{7,5},{... | collective-permute-start | bytes 172040 | tf_op jit(solution)/shard_map/ppermute | solution.py:303
  26.5 0.0 copy-start
  26.6 1.0 copy-done
  27.5 0.0 copy-start.2
  27.6 0.8 copy-done.2
  28.3 2.7 %shard_map.55 = f32[16,64,128]{2,1,0:T(8,128)} custom-call(f32[4,3,8,1024]{3,2,1,0:T(8,128)S(1)} %copy-done, s32[8,1024]{1,0:T(8,128)S(1)} %copy-done.2), custom_call_target="tpu_custom_call" | custom-call | tf_op jit(solution)/shard_map/pallas_call | solution.py:304
  31.0 0.0 collective-permute-done.1
  31.0 0.0 collective-permute-done.2
  31.1 16.5 %all-to-all-start = ((f32[16,64,128]{2,1,0:T(8,128)}), f32[16,64,128]{2,1,0:T(8,128)S(1)}, u32[]{:S(2)}, u32[]{:S(2)}) async-start(f32[16,64,128]{2,1,0:T(8,128)} %shard_map.55), calls=%async_computation | async-start | bytes 1048576 | tf_op jit(solution)/shard_map/all_to_all | solution.py:312
  47.6 1.9 %collective-permute-start.3 = (f32[336,128]{1,0:T(8,128)S(1)}, f32[336,128]{1,0:T(8,128)S(1)}, u32[]{:S(2)}, u32[]{:S(2)}) collective-permute-start(f32[336,128]{1,0:T(8,128)S(1)} %pad_maximum_fusion), channel_id=1, source_target_pairs={{0,16},{16,32},{32,48},{48,0},{1,17},{17,33},{33,49},{49,1},{2,18}... | collective-permute-start | bytes 516104 | tf_op jit(solution)/shard_map/ppermute | solution.py:315
  49.5 3.7 %collective-permute-start.4 = (f32[336,128]{1,0:T(8,128)S(1)}, f32[336,128]{1,0:T(8,128)S(1)}, u32[]{:S(2)}, u32[]{:S(2)}) collective-permute-start(f32[336,128]{1,0:T(8,128)S(1)} %pad_maximum_fusion), channel_id=1, source_target_pairs={{0,32},{16,48},{32,0},{48,16},{1,33},{17,49},{33,1},{49,17},{2,34}... | collective-permute-start | bytes 516104 | tf_op jit(solution)/shard_map/ppermute | solution.py:315
  53.2 2.8 %collective-permute-start.5 = (f32[336,128]{1,0:T(8,128)S(1)}, f32[336,128]{1,0:T(8,128)S(1)}, u32[]{:S(2)}, u32[]{:S(2)}) collective-permute-start(f32[336,128]{1,0:T(8,128)S(1)} %pad_maximum_fusion), channel_id=1, source_target_pairs={{0,48},{16,0},{32,16},{48,32},{1,49},{17,1},{33,17},{49,33},{2,50}... | collective-permute-start | bytes 516104 | tf_op jit(solution)/shard_map/ppermute | solution.py:315
  56.1 4.2 %collective-permute-done.3 = f32[336,128]{1,0:T(8,128)S(1)} collective-permute-done((f32[336,128]{1,0:T(8,128)S(1)}, f32[336,128]{1,0:T(8,128)S(1)}, u32[]{:S(2)}, u32[]{:S(2)}) %collective-permute-start.3) | collective-permute-done | bytes 172064 | tf_op jit(solution)/shard_map/ppermute | solution.py:315
  60.4 0.0 collective-permute-done.4
  60.4 2.1 %collective-permute-done.5 = f32[336,128]{1,0:T(8,128)S(1)} collective-permute-done((f32[336,128]{1,0:T(8,128)S(1)}, f32[336,128]{1,0:T(8,128)S(1)}, u32[]{:S(2)}, u32[]{:S(2)}) %collective-permute-start.5) | collective-permute-done | bytes 172064 | tf_op jit(solution)/shard_map/ppermute | solution.py:315
  62.5 3.1 %collective-permute-start.6 = (f32[1344,128]{1,0:T(8,128)S(1)}, f32[1344,128]{1,0:T(8,128)S(1)}, u32[]{:S(2)}, u32[]{:S(2)}) collective-permute-start(f32[1344,128]{1,0:T(8,128)S(1)} %constant_dynamic-update-slice_fusion.strip_ref), channel_id=1, source_target_pairs={{0,1},{1,0},{2,3},{3,2},{4,5},{5,4},{6,7},{7,6},{8,9},{9,8},{10,11... | collective-permute-start | bytes 2064392 | tf_op jit(solution)/shard_map/ppermute | solution.py:317
  65.6 1.7 %collective-permute-done.6.other_ref = f32[1344,128]{1,0:T(8,128)S(1)} collective-permute-done((f32[1344,128]{1,0:T(8,128)S(1)}, f32[1344,128]{1,0:T(8,128)S(1)}, u32[]{:S(2)}, u32[]{:S(2)}) %collective-permute-start.6) | collective-permute-done | bytes 688160 | tf_op jit(solution)/shard_map/ppermute | solution.py:317
  67.4 0.0 all-to-all-done
  67.4 19.6 %collective-permute-start.7 = (f32[16,64,128]{2,1,0:T(8,128)S(1)}, f32[16,64,128]{2,1,0:T(8,128)S(1)}, u32[]{:S(2)}, u32[]{:S(2)}) collective-permute-start(f32[16,64,128]{2,1,0:T(8,128)S(1)} %all-to-all-done), channel_id=1, source_target_pairs={{0,2},{2,4},{4,6},{6,8},{8,10},{10,12},{12,14},{1,3},{3,5},{5,7},{... | collective-permute-start | bytes 1572872 | tf_op jit(solution)/shard_map/ppermute | solution.py:332
  87.0 1.3 %collective-permute-start.8 = (f32[16,64,128]{2,1,0:T(8,128)S(1)}, f32[16,64,128]{2,1,0:T(8,128)S(1)}, u32[]{:S(2)}, u32[]{:S(2)}) collective-permute-start(f32[16,64,128]{2,1,0:T(8,128)S(1)} %all-to-all-done), channel_id=1, source_target_pairs={{2,0},{4,2},{6,4},{8,6},{10,8},{12,10},{14,12},{3,1},{5,3},{7,5},{... | collective-permute-start | bytes 1572872 | tf_op jit(solution)/shard_map/ppermute | solution.py:332
  88.3 0.1 pad_add_fusion.core_ref
  88.4 0.0 copy-start.4
  88.4 8.7 %shard_map.57.coef = f32[8,15,5,56,128]{4,3,2,1,0:T(8,128)S(1)} custom-call(s32[2]{0:T(128)S(1)} %pad_add_fusion.core_ref, f32[1344,128]{1,0:T(8,128)S(1)} %constant_dynamic-update-slice_fusion.strip_ref, f32[1344,128]{1,0:T(8,128)S(1)} %collective-permute-done.6.other_ref), custom_call_target="tpu_custom_call" | custom-call | flops 2000000000 | bytes 50000000 | tf_op jit(solution)/shard_map/pallas_call | solution.py:319
  97.1 0.0 collective-permute-done.7
  97.1 3.7 %collective-permute-done.8 = f32[16,64,128]{2,1,0:T(8,128)S(1)} collective-permute-done((f32[16,64,128]{2,1,0:T(8,128)S(1)}, f32[16,64,128]{2,1,0:T(8,128)S(1)}, u32[]{:S(2)}, u32[]{:S(2)}) %collective-permute-start.8) | collective-permute-done | bytes 524320 | tf_op jit(solution)/shard_map/ppermute | solution.py:332
  100.8 13.8 %shard_map.58 = f32[8,96,128]{2,1,0:T(8,128)S(1)} custom-call(f32[1024,128]{1,0:T(8,128)S(1)} %bitcast.12, f32[1024,128]{1,0:T(8,128)S(1)} %bitcast.10, f32[1024,128]{1,0:T(8,128)S(1)} %bitcast.13, f32[8,15,5,56,128]{4,3,2,1,0:T(8,128)S(1)} %shard_map.57.coef), custom_call_target="tpu_custom_call" | custom-call | tf_op jit(solution)/shard_map/pallas_call | solution.py:334
  114.7 12.8 %all_to_all.10 = f32[8,96,128]{2,1,0:T(8,128)S(1)} all-to-all(f32[8,96,128]{2,1,0:T(8,128)S(1)} %shard_map.58), channel_id=1, replica_groups=mesh['y'=4,'zh'=2,'x'=4,'zl'=8,'c'=2] {'x','c'}, dimensions={0} | all-to-all | bytes 786432 | tf_op jit(solution)/shard_map/all_to_all | solution.py:346
  127.5 0.0 copy-done.4
  127.5 1.3 shard_map.59
  (10 shorter events, 0.1 us)
Async XLA Ops:
  0.0 0.8 copy-start.1
  0.8 0.9 copy-start.3
  1.7 0.7 copy-start.5
  2.9 19.7 %collective-permute-start = (f32[48,128]{1,0:T(8,128)S(1)}, f32[48,128]{1,0:T(8,128)S(1)}, u32[]{:S(2)}, u32[]{:S(2)}) collective-permute-start(f32[48,128]{1,0:T(8,128)S(1)} %slice.4), channel_id=1, source_target_pairs={{48,112},{0,448},{112,176},{64,0},{176,240},{128,64},{240,304},{19... | collective-permute-start | bytes 73736 | tf_op jit(solution)/shard_map/ppermute | solution.py:301
  22.6 8.4 %collective-permute-start.1 = (f32[112,128]{1,0:T(8,128)S(1)}, f32[112,128]{1,0:T(8,128)S(1)}, u32[]{:S(2)}, u32[]{:S(2)}) collective-permute-start(f32[112,128]{1,0:T(8,128)S(1)} %pad_maximum_fusion.1), channel_id=1, source_target_pairs={{0,2},{2,4},{4,6},{6,8},{8,10},{10,12},{12,14},{1,3},{3,5},{5,7},{... | collective-permute-start | bytes 172040 | tf_op jit(solution)/shard_map/ppermute | solution.py:303
  25.2 5.8 %collective-permute-start.2 = (f32[112,128]{1,0:T(8,128)S(1)}, f32[112,128]{1,0:T(8,128)S(1)}, u32[]{:S(2)}, u32[]{:S(2)}) collective-permute-start(f32[112,128]{1,0:T(8,128)S(1)} %pad_maximum_fusion.1), channel_id=1, source_target_pairs={{2,0},{4,2},{6,4},{8,6},{10,8},{12,10},{14,12},{3,1},{5,3},{7,5},{... | collective-permute-start | bytes 172040 | tf_op jit(solution)/shard_map/ppermute | solution.py:303
  26.5 1.0 copy-start
  27.5 0.8 copy-start.2
  31.1 36.3 %all-to-all-start = ((f32[16,64,128]{2,1,0:T(8,128)}), f32[16,64,128]{2,1,0:T(8,128)S(1)}, u32[]{:S(2)}, u32[]{:S(2)}) async-start(f32[16,64,128]{2,1,0:T(8,128)} %shard_map.55), calls=%async_computation | async-start | bytes 1048576 | tf_op jit(solution)/shard_map/all_to_all | solution.py:312
  47.6 12.7 %collective-permute-start.3 = (f32[336,128]{1,0:T(8,128)S(1)}, f32[336,128]{1,0:T(8,128)S(1)}, u32[]{:S(2)}, u32[]{:S(2)}) collective-permute-start(f32[336,128]{1,0:T(8,128)S(1)} %pad_maximum_fusion), channel_id=1, source_target_pairs={{0,16},{16,32},{32,48},{48,0},{1,17},{17,33},{33,49},{49,1},{2,18}... | collective-permute-start | bytes 516104 | tf_op jit(solution)/shard_map/ppermute | solution.py:315
  49.5 10.8 %collective-permute-start.4 = (f32[336,128]{1,0:T(8,128)S(1)}, f32[336,128]{1,0:T(8,128)S(1)}, u32[]{:S(2)}, u32[]{:S(2)}) collective-permute-start(f32[336,128]{1,0:T(8,128)S(1)} %pad_maximum_fusion), channel_id=1, source_target_pairs={{0,32},{16,48},{32,0},{48,16},{1,33},{17,49},{33,1},{49,17},{2,34}... | collective-permute-start | bytes 516104 | tf_op jit(solution)/shard_map/ppermute | solution.py:315
  53.2 9.3 %collective-permute-start.5 = (f32[336,128]{1,0:T(8,128)S(1)}, f32[336,128]{1,0:T(8,128)S(1)}, u32[]{:S(2)}, u32[]{:S(2)}) collective-permute-start(f32[336,128]{1,0:T(8,128)S(1)} %pad_maximum_fusion), channel_id=1, source_target_pairs={{0,48},{16,0},{32,16},{48,32},{1,49},{17,1},{33,17},{49,33},{2,50}... | collective-permute-start | bytes 516104 | tf_op jit(solution)/shard_map/ppermute | solution.py:315
  62.5 4.9 %collective-permute-start.6 = (f32[1344,128]{1,0:T(8,128)S(1)}, f32[1344,128]{1,0:T(8,128)S(1)}, u32[]{:S(2)}, u32[]{:S(2)}) collective-permute-start(f32[1344,128]{1,0:T(8,128)S(1)} %constant_dynamic-update-slice_fusion.strip_ref), channel_id=1, source_target_pairs={{0,1},{1,0},{2,3},{3,2},{4,5},{5,4},{6,7},{7,6},{8,9},{9,8},{10,11... | collective-permute-start | bytes 2064392 | tf_op jit(solution)/shard_map/ppermute | solution.py:317
  67.4 29.7 %collective-permute-start.7 = (f32[16,64,128]{2,1,0:T(8,128)S(1)}, f32[16,64,128]{2,1,0:T(8,128)S(1)}, u32[]{:S(2)}, u32[]{:S(2)}) collective-permute-start(f32[16,64,128]{2,1,0:T(8,128)S(1)} %all-to-all-done), channel_id=1, source_target_pairs={{0,2},{2,4},{4,6},{6,8},{8,10},{10,12},{12,14},{1,3},{3,5},{5,7},{... | collective-permute-start | bytes 1572872 | tf_op jit(solution)/shard_map/ppermute | solution.py:332
  87.0 13.9 %collective-permute-start.8 = (f32[16,64,128]{2,1,0:T(8,128)S(1)}, f32[16,64,128]{2,1,0:T(8,128)S(1)}, u32[]{:S(2)}, u32[]{:S(2)}) collective-permute-start(f32[16,64,128]{2,1,0:T(8,128)S(1)} %all-to-all-done), channel_id=1, source_target_pairs={{2,0},{4,2},{6,4},{8,6},{10,8},{12,10},{14,12},{3,1},{5,3},{7,5},{... | collective-permute-start | bytes 1572872 | tf_op jit(solution)/shard_map/ppermute | solution.py:332
  88.4 39.2 %copy-start.4 = (f32[128,128]{1,0:T(8,128)S(1)}, f32[128,128]{1,0:T(8,128)}, u32[]{:S(2)}) copy-start(f32[128,128]{1,0:T(8,128)} %coef_ref.1) | copy-start | bytes 196612

commit v12 on v11

--- a/solution.py
+++ b/solution.py
@@ -52,12 +52,12 @@
     return [pltpu.roll(cells[-1], 1, 1), *cells[:-1]]
 
 
-def flow_kernel(block_ref, order_ref, base_ref, mask_ref, raw_ref):
+def flow_kernel(block_ref, base_ref, mask_ref, raw_ref):
     lane = lax.broadcasted_iota(jnp.int32, (8, LANES), 1)
     s = block_ref[0]
     for high in range(2):
         for f in range(3):
-            flow = jnp.concatenate([base_ref[order_ref[high * 4 + low], f] for low in range(4)], axis=1)
+            flow = jnp.concatenate([base_ref[high * 4 + low, f] for low in range(4)], axis=1)
             raw_ref[(high * 3 + f) * 8 : (high * 3 + f) * 8 + 8, :] = flow
 
     def column(k):
@@ -93,7 +93,7 @@
     lax.fori_loop(0, 2, send, None)
 
 
-def coef_kernel(core_ref, strip_ref, other_ref, coef, base, lines, spread_matrix):
+def coef_kernel(core_ref, order_ref, strip_ref, other_ref, coef, base, lines, spread_matrix):
     lane = lax.broadcasted_iota(jnp.int32, (8, LANES), 1)
     core, me = core_ref[0], core_ref[1]
     blocks = [lax.rem(me - x + 4, 4) * 336 for x in range(4)]
@@ -149,10 +149,11 @@
 
     def prepare(step, tile):
         top = pl.multiple_of(tile * 8, 8)
+        slot = order_ref[step]
         w = [base[STEPS, 0, v, pl.ds(top + 8, 8), :] * 0.25 for v in range(PARTS)]
 
         def rows(f, shift):
-            return [base[step, f, v, pl.ds(top + 8 + shift, 8), :] for v in range(PARTS)]
+            return [base[slot, f, v, pl.ds(top + 8 + shift, 8), :] for v in range(PARTS)]
 
         depth = [x + 1.0 for x in rows(0, 0)]
         b, c = rows(1, 0), rows(2, 0)
@@ -222,10 +223,15 @@
         return out
 
     def sweep(low, high, body):
-        def window(i, _):
-            lax.fori_loop(0, QUADS // GROUP, lambda g, _: body(low + 8 * i, [g * GROUP + k for k in range(GROUP)]), None)
-
-        lax.fori_loop(0, (high - low + 7) // 8, window, None)
+        count = (high - low + 7) // 8
+        quads = list(range(QUADS))
+
+        def two(i, _):
+            body(low + 16 * i, quads)
+            body(low + 16 * i + 8, quads)
+
+        lax.fori_loop(0, count // 2, two, None)
+        lax.fori_loop(count // 2 * 2, count, lambda i, _: body(low + 8 * i, quads), None)
 
     def first(step, top, pairs):
         for p, change in zip(pairs, changes(state, step, top, pairs)):
@@ -291,10 +297,10 @@
     raw = pl.pallas_call(
         flow_kernel,
         out_shape=jax.ShapeDtypeStruct((64, LANES), f32),
-        in_specs=[SMEM, SMEM, VMEM, VMEM],
+        in_specs=[SMEM, VMEM, VMEM],
         out_specs=VMEM,
         compiler_params=pltpu.CompilerParams(vmem_limit_bytes=16 * 2**20),
-    )(block.reshape(1).astype(jnp.int32), owner_order, checkpoints, land_mask)
+    )(block.reshape(1).astype(jnp.int32), checkpoints, land_mask)
     up = [(i, i + 1) for i in range(7)]
     down = [(i + 1, i) for i in range(7)]
     ring = [(s * 4 + x, (s + step) % 8 * 4 + x) for s in range(8) for x, step in ((3, 1), (0, -1))]
@@ -319,7 +325,7 @@
     coef = pl.pallas_call(
         coef_kernel,
         out_shape=jax.ShapeDtypeStruct((STEPS, COEFS, PARTS, TALL + 8, LANES), f32),
-        in_specs=[SMEM, VMEM, VMEM],
+        in_specs=[SMEM, SMEM, VMEM, VMEM],
         out_specs=VMEM,
         scratch_shapes=[
             pltpu.VMEM((STEPS + 1, 3, PARTS, TALL + 16, LANES), f32),
@@ -328,7 +334,7 @@
         ],
         compiler_params=pltpu.CompilerParams(vmem_limit_bytes=32 * 2**20),
         cost_estimate=pl.CostEstimate(flops=2 * 10**9, bytes_accessed=50 * 10**6, transcendentals=0),
-    )(jnp.stack([core, lax.axis_index("x")]).astype(jnp.int32), strip, other)
+    )(jnp.stack([core, lax.axis_index("x")]).astype(jnp.int32), owner_order, strip, other)
     parts = [lax.ppermute(own, "zl", up), own, lax.ppermute(own, "zl", down)]
     parts = [x.reshape(PEERS * 64, LANES) for x in parts]
     out = pl.pallas_call(

time: 129 us -> 128 us (level)
  no operation moved by 1% of the time
where the time goes in v12:
time: 128 us; the launch traced here: 127 us
  starting transfers between devices  71.6 us (56%)
  Pallas kernels  26.4 us (21%)
  blocking collectives  12.8 us (10%)
  waiting for transfers between devices  12.1 us (9%)
  local copies, waits for them, and re-layouts  4.12 us (3%)
    ppermute x2, starting transfers between devices, on_device(): parts = [lax.ppermute(own, 'zl', up), own, lax.ppermute(own, 'zl', down)]  20.9 us
    ppermute x1, starting transfers between devices, on_device(): halo = lax.ppermute(raw[:48], ('y', 'zh', 'x'), ring)  18.7 us
    all_to_all x1, starting transfers between devices, on_device(): own = lax.all_to_all(send, ('zh', 'y', 'c'), 0, 0, tiled=True)  16.5 us
    pallas_call x1, Pallas kernels, on_device(): pl.pallas_call(march_kernel, out_shape=jax.ShapeDtypeStruct((8, 96, LANES...  13.5 us
    all_to_all x1, blocking collectives, on_device(): cells = lax.all_to_all(out, ('x', 'c'), 0, 0, tiled=True)  12.8 us
    pallas_call x1, Pallas kernels, on_device(): pl.pallas_call(coef_kernel, out_shape=jax.ShapeDtypeStruct((STEPS, COEFS,...  8.77 us
    ppermute x3, starting transfers between devices, on_device(): lax.ppermute(chips, 'x', [(i, (i + k) % 4) for i in range(4)])  8.44 us
    ppermute x3, waiting for transfers between devices, on_device(): lax.ppermute(chips, 'x', [(i, (i + k) % 4) for i in range(4)])  6.35 us
  transfers between devices with their start and end apart: 10, of which 5 were waited for; matrix products, arithmetic and copies ran while one was open for 0% of the time, Pallas kernels for 9%

profile of v12, /device:TPU:1, one launch (start us, length us, event | category | flops | bytes accessed | tf_op | source)
XLA Modules:
  0.0 127.3 jit_solution(6855664741227530552)
XLA Ops:
  0.0 0.0 copy-start.1
  0.0 0.8 copy-done.1
  0.8 0.0 copy-start.3
  0.8 0.9 copy-done.3
  1.7 0.1 shard_map.56
  1.7 18.7 %collective-permute-start = (f32[48,128]{1,0:T(8,128)S(1)}, f32[48,128]{1,0:T(8,128)S(1)}, u32[]{:S(2)}, u32[]{:S(2)}) collective-permute-start(f32[48,128]{1,0:T(8,128)S(1)} %slice.4), channel_id=1, source_target_pairs={{48,112},{0,448},{112,176},{64,0},{176,240},{128,64},{240,304},{19... | collective-permute-start | bytes 73736 | tf_op jit(solution)/shard_map/ppermute | solution.py:307
  20.5 0.9 collective-permute-done
  21.4 2.6 %collective-permute-start.1 = (f32[112,128]{1,0:T(8,128)S(1)}, f32[112,128]{1,0:T(8,128)S(1)}, u32[]{:S(2)}, u32[]{:S(2)}) collective-permute-start(f32[112,128]{1,0:T(8,128)S(1)} %pad_maximum_fusion.1), channel_id=1, source_target_pairs={{0,2},{2,4},{4,6},{6,8},{8,10},{10,12},{12,14},{1,3},{3,5},{5,7},{... | collective-permute-start | bytes 172040 | tf_op jit(solution)/shard_map/ppermute | solution.py:309
  24.0 1.3 %collective-permute-start.2 = (f32[112,128]{1,0:T(8,128)S(1)}, f32[112,128]{1,0:T(8,128)S(1)}, u32[]{:S(2)}, u32[]{:S(2)}) collective-permute-start(f32[112,128]{1,0:T(8,128)S(1)} %pad_maximum_fusion.1), channel_id=1, source_target_pairs={{2,0},{4,2},{6,4},{8,6},{10,8},{12,10},{14,12},{3,1},{5,3},{7,5},{... | collective-permute-start | bytes 172040 | tf_op jit(solution)/shard_map/ppermute | solution.py:309
  25.3 0.0 copy-start
  25.4 1.0 copy-done
  26.3 0.0 copy-start.2
  26.4 0.8 copy-done.2
  27.1 2.7 %shard_map.55 = f32[16,64,128]{2,1,0:T(8,128)} custom-call(f32[4,3,8,1024]{3,2,1,0:T(8,128)S(1)} %copy-done, s32[8,1024]{1,0:T(8,128)S(1)} %copy-done.2), custom_call_target="tpu_custom_call" | custom-call | tf_op jit(solution)/shard_map/pallas_call | solution.py:310
  29.8 0.0 collective-permute-done.1
  29.8 0.0 collective-permute-done.2
  29.9 16.5 %all-to-all-start = ((f32[16,64,128]{2,1,0:T(8,128)}), f32[16,64,128]{2,1,0:T(8,128)S(1)}, u32[]{:S(2)}, u32[]{:S(2)}) async-start(f32[16,64,128]{2,1,0:T(8,128)} %shard_map.55), calls=%async_computation | async-start | bytes 1048576 | tf_op jit(solution)/shard_map/all_to_all | solution.py:318
  46.4 1.9 %collective-permute-start.3 = (f32[336,128]{1,0:T(8,128)S(1)}, f32[336,128]{1,0:T(8,128)S(1)}, u32[]{:S(2)}, u32[]{:S(2)}) collective-permute-start(f32[336,128]{1,0:T(8,128)S(1)} %pad_maximum_fusion), channel_id=1, source_target_pairs={{0,16},{16,32},{32,48},{48,0},{1,17},{17,33},{33,49},{49,1},{2,18}... | collective-permute-start | bytes 516104 | tf_op jit(solution)/shard_map/ppermute | solution.py:321
  48.3 3.7 %collective-permute-start.4 = (f32[336,128]{1,0:T(8,128)S(1)}, f32[336,128]{1,0:T(8,128)S(1)}, u32[]{:S(2)}, u32[]{:S(2)}) collective-permute-start(f32[336,128]{1,0:T(8,128)S(1)} %pad_maximum_fusion), channel_id=1, source_target_pairs={{0,32},{16,48},{32,0},{48,16},{1,33},{17,49},{33,1},{49,17},{2,34}... | collective-permute-start | bytes 516104 | tf_op jit(solution)/shard_map/ppermute | solution.py:321
  52.0 2.8 %collective-permute-start.5 = (f32[336,128]{1,0:T(8,128)S(1)}, f32[336,128]{1,0:T(8,128)S(1)}, u32[]{:S(2)}, u32[]{:S(2)}) collective-permute-start(f32[336,128]{1,0:T(8,128)S(1)} %pad_maximum_fusion), channel_id=1, source_target_pairs={{0,48},{16,0},{32,16},{48,32},{1,49},{17,1},{33,17},{49,33},{2,50}... | collective-permute-start | bytes 516104 | tf_op jit(solution)/shard_map/ppermute | solution.py:321
  54.9 4.2 %collective-permute-done.3 = f32[336,128]{1,0:T(8,128)S(1)} collective-permute-done((f32[336,128]{1,0:T(8,128)S(1)}, f32[336,128]{1,0:T(8,128)S(1)}, u32[]{:S(2)}, u32[]{:S(2)}) %collective-permute-start.3) | collective-permute-done | bytes 172064 | tf_op jit(solution)/shard_map/ppermute | solution.py:321
  59.2 0.0 collective-permute-done.4
  59.2 2.1 %collective-permute-done.5 = f32[336,128]{1,0:T(8,128)S(1)} collective-permute-done((f32[336,128]{1,0:T(8,128)S(1)}, f32[336,128]{1,0:T(8,128)S(1)}, u32[]{:S(2)}, u32[]{:S(2)}) %collective-permute-start.5) | collective-permute-done | bytes 172064 | tf_op jit(solution)/shard_map/ppermute | solution.py:321
  61.3 3.1 %collective-permute-start.6 = (f32[1344,128]{1,0:T(8,128)S(1)}, f32[1344,128]{1,0:T(8,128)S(1)}, u32[]{:S(2)}, u32[]{:S(2)}) collective-permute-start(f32[1344,128]{1,0:T(8,128)S(1)} %constant_dynamic-update-slice_fusion.strip_ref), channel_id=1, source_target_pairs={{0,1},{1,0},{2,3},{3,2},{4,5},{5,4},{6,7},{7,6},{8,9},{9,8},{10,11... | collective-permute-start | bytes 2064392 | tf_op jit(solution)/shard_map/ppermute | solution.py:323
  64.4 1.7 %collective-permute-done.6.other_ref = f32[1344,128]{1,0:T(8,128)S(1)} collective-permute-done((f32[1344,128]{1,0:T(8,128)S(1)}, f32[1344,128]{1,0:T(8,128)S(1)}, u32[]{:S(2)}, u32[]{:S(2)}) %collective-permute-start.6) | collective-permute-done | bytes 688160 | tf_op jit(solution)/shard_map/ppermute | solution.py:323
  66.2 0.0 all-to-all-done
  66.2 19.6 %collective-permute-start.7 = (f32[16,64,128]{2,1,0:T(8,128)S(1)}, f32[16,64,128]{2,1,0:T(8,128)S(1)}, u32[]{:S(2)}, u32[]{:S(2)}) collective-permute-start(f32[16,64,128]{2,1,0:T(8,128)S(1)} %all-to-all-done), channel_id=1, source_target_pairs={{0,2},{2,4},{4,6},{6,8},{8,10},{10,12},{12,14},{1,3},{3,5},{5,7},{... | collective-permute-start | bytes 1572872 | tf_op jit(solution)/shard_map/ppermute | solution.py:338
  85.8 1.3 %collective-permute-start.8 = (f32[16,64,128]{2,1,0:T(8,128)S(1)}, f32[16,64,128]{2,1,0:T(8,128)S(1)}, u32[]{:S(2)}, u32[]{:S(2)}) collective-permute-start(f32[16,64,128]{2,1,0:T(8,128)S(1)} %all-to-all-done), channel_id=1, source_target_pairs={{2,0},{4,2},{6,4},{8,6},{10,8},{12,10},{14,12},{3,1},{5,3},{7,5},{... | collective-permute-start | bytes 1572872 | tf_op jit(solution)/shard_map/ppermute | solution.py:338
  87.1 0.1 pad_add_fusion.core_ref
  87.2 0.0 copy-start.5
  87.2 0.7 copy-done.5
  87.8 0.0 copy-start.4
  87.8 8.8 %shard_map.57.coef = f32[8,15,5,56,128]{4,3,2,1,0:T(8,128)S(1)} custom-call(s32[2]{0:T(128)S(1)} %pad_add_fusion.core_ref, s32[8]{0:T(128)S(1)} %copy-done.5, f32[1344,128]{1,0:T(8,128)S(1)} %constant_dynamic-update-slice_fusion.strip_ref, f32[1344,128]{1,0:T(8,128)S(1)} %collective-permute-done.6.other_ref), custom_call_target="tpu_custom_call" | custom-call | flops 2000000000 | bytes 50000000 | tf_op jit(solution)/shard_map/pallas_call | solution.py:325
  96.6 0.0 collective-permute-done.7
  96.6 3.0 %collective-permute-done.8 = f32[16,64,128]{2,1,0:T(8,128)S(1)} collective-permute-done((f32[16,64,128]{2,1,0:T(8,128)S(1)}, f32[16,64,128]{2,1,0:T(8,128)S(1)}, u32[]{:S(2)}, u32[]{:S(2)}) %collective-permute-start.8) | collective-permute-done | bytes 524320 | tf_op jit(solution)/shard_map/ppermute | solution.py:338
  99.6 13.5 %shard_map.58 = f32[8,96,128]{2,1,0:T(8,128)S(1)} custom-call(f32[1024,128]{1,0:T(8,128)S(1)} %bitcast.12, f32[1024,128]{1,0:T(8,128)S(1)} %bitcast.10, f32[1024,128]{1,0:T(8,128)S(1)} %bitcast.13, f32[8,15,5,56,128]{4,3,2,1,0:T(8,128)S(1)} %shard_map.57.coef), custom_call_target="tpu_custom_call" | custom-call | tf_op jit(solution)/shard_map/pallas_call | solution.py:340
  113.1 12.8 %all_to_all.10 = f32[8,96,128]{2,1,0:T(8,128)S(1)} all-to-all(f32[8,96,128]{2,1,0:T(8,128)S(1)} %shard_map.58), channel_id=1, replica_groups=mesh['y'=4,'zh'=2,'x'=4,'zl'=8,'c'=2] {'x','c'}, dimensions={0} | all-to-all | bytes 786432 | tf_op jit(solution)/shard_map/all_to_all | solution.py:352
  126.0 0.0 copy-done.4
  126.0 1.3 %shard_map.59 = f32[768,128]{1,0:T(8,128)} custom-call(f32[128,128]{1,0:T(8,128)S(1)} %copy-done.4, f32[768,128]{1,0:T(8,128)S(1)} %bitcast.11), custom_call_target="tpu_custom_call" | custom-call | tf_op jit(solution)/shard_map/pallas_call | solution.py:353
  (10 shorter events, 0.1 us)
Async XLA Ops:
  0.0 0.8 copy-start.1
  0.8 0.9 copy-start.3
  1.7 19.7 %collective-permute-start = (f32[48,128]{1,0:T(8,128)S(1)}, f32[48,128]{1,0:T(8,128)S(1)}, u32[]{:S(2)}, u32[]{:S(2)}) collective-permute-start(f32[48,128]{1,0:T(8,128)S(1)} %slice.4), channel_id=1, source_target_pairs={{48,112},{0,448},{112,176},{64,0},{176,240},{128,64},{240,304},{19... | collective-permute-start | bytes 73736 | tf_op jit(solution)/shard_map/ppermute | solution.py:307
  21.4 8.4 %collective-permute-start.1 = (f32[112,128]{1,0:T(8,128)S(1)}, f32[112,128]{1,0:T(8,128)S(1)}, u32[]{:S(2)}, u32[]{:S(2)}) collective-permute-start(f32[112,128]{1,0:T(8,128)S(1)} %pad_maximum_fusion.1), channel_id=1, source_target_pairs={{0,2},{2,4},{4,6},{6,8},{8,10},{10,12},{12,14},{1,3},{3,5},{5,7},{... | collective-permute-start | bytes 172040 | tf_op jit(solution)/shard_map/ppermute | solution.py:309
  24.0 5.8 %collective-permute-start.2 = (f32[112,128]{1,0:T(8,128)S(1)}, f32[112,128]{1,0:T(8,128)S(1)}, u32[]{:S(2)}, u32[]{:S(2)}) collective-permute-start(f32[112,128]{1,0:T(8,128)S(1)} %pad_maximum_fusion.1), channel_id=1, source_target_pairs={{2,0},{4,2},{6,4},{8,6},{10,8},{12,10},{14,12},{3,1},{5,3},{7,5},{... | collective-permute-start | bytes 172040 | tf_op jit(solution)/shard_map/ppermute | solution.py:309
  25.3 1.0 copy-start
  26.3 0.8 copy-start.2
  29.9 36.3 %all-to-all-start = ((f32[16,64,128]{2,1,0:T(8,128)}), f32[16,64,128]{2,1,0:T(8,128)S(1)}, u32[]{:S(2)}, u32[]{:S(2)}) async-start(f32[16,64,128]{2,1,0:T(8,128)} %shard_map.55), calls=%async_computation | async-start | bytes 1048576 | tf_op jit(solution)/shard_map/all_to_all | solution.py:318
  46.4 12.7 %collective-permute-start.3 = (f32[336,128]{1,0:T(8,128)S(1)}, f32[336,128]{1,0:T(8,128)S(1)}, u32[]{:S(2)}, u32[]{:S(2)}) collective-permute-start(f32[336,128]{1,0:T(8,128)S(1)} %pad_maximum_fusion), channel_id=1, source_target_pairs={{0,16},{16,32},{32,48},{48,0},{1,17},{17,33},{33,49},{49,1},{2,18}... | collective-permute-start | bytes 516104 | tf_op jit(solution)/shard_map/ppermute | solution.py:321
  48.3 10.8 %collective-permute-start.4 = (f32[336,128]{1,0:T(8,128)S(1)}, f32[336,128]{1,0:T(8,128)S(1)}, u32[]{:S(2)}, u32[]{:S(2)}) collective-permute-start(f32[336,128]{1,0:T(8,128)S(1)} %pad_maximum_fusion), channel_id=1, source_target_pairs={{0,32},{16,48},{32,0},{48,16},{1,33},{17,49},{33,1},{49,17},{2,34}... | collective-permute-start | bytes 516104 | tf_op jit(solution)/shard_map/ppermute | solution.py:321
  52.0 9.3 %collective-permute-start.5 = (f32[336,128]{1,0:T(8,128)S(1)}, f32[336,128]{1,0:T(8,128)S(1)}, u32[]{:S(2)}, u32[]{:S(2)}) collective-permute-start(f32[336,128]{1,0:T(8,128)S(1)} %pad_maximum_fusion), channel_id=1, source_target_pairs={{0,48},{16,0},{32,16},{48,32},{1,49},{17,1},{33,17},{49,33},{2,50}... | collective-permute-start | bytes 516104 | tf_op jit(solution)/shard_map/ppermute | solution.py:321
  61.3 4.9 %collective-permute-start.6 = (f32[1344,128]{1,0:T(8,128)S(1)}, f32[1344,128]{1,0:T(8,128)S(1)}, u32[]{:S(2)}, u32[]{:S(2)}) collective-permute-start(f32[1344,128]{1,0:T(8,128)S(1)} %constant_dynamic-update-slice_fusion.strip_ref), channel_id=1, source_target_pairs={{0,1},{1,0},{2,3},{3,2},{4,5},{5,4},{6,7},{7,6},{8,9},{9,8},{10,11... | collective-permute-start | bytes 2064392 | tf_op jit(solution)/shard_map/ppermute | solution.py:323
  66.2 30.4 %collective-permute-start.7 = (f32[16,64,128]{2,1,0:T(8,128)S(1)}, f32[16,64,128]{2,1,0:T(8,128)S(1)}, u32[]{:S(2)}, u32[]{:S(2)}) collective-permute-start(f32[16,64,128]{2,1,0:T(8,128)S(1)} %all-to-all-done), channel_id=1, source_target_pairs={{0,2},{2,4},{4,6},{6,8},{8,10},{10,12},{12,14},{1,3},{3,5},{5,7},{... | collective-permute-start | bytes 1572872 | tf_op jit(solution)/shard_map/ppermute | solution.py:338
  85.8 13.9 %collective-permute-start.8 = (f32[16,64,128]{2,1,0:T(8,128)S(1)}, f32[16,64,128]{2,1,0:T(8,128)S(1)}, u32[]{:S(2)}, u32[]{:S(2)}) collective-permute-start(f32[16,64,128]{2,1,0:T(8,128)S(1)} %all-to-all-done), channel_id=1, source_target_pairs={{2,0},{4,2},{6,4},{8,6},{10,8},{12,10},{14,12},{3,1},{5,3},{7,5},{... | collective-permute-start | bytes 1572872 | tf_op jit(solution)/shard_map/ppermute | solution.py:338
  87.2 0.7 copy-start.5
  87.8 38.2 %copy-start.4 = (f32[128,128]{1,0:T(8,128)S(1)}, f32[128,128]{1,0:T(8,128)}, u32[]{:S(2)}) copy-start(f32[128,128]{1,0:T(8,128)} %coef_ref.1) | copy-start | bytes 196612

commit v13 on v12

--- a/solution.py
+++ b/solution.py
@@ -52,8 +52,9 @@
     return [pltpu.roll(cells[-1], 1, 1), *cells[:-1]]
 
 
-def flow_kernel(block_ref, base_ref, mask_ref, raw_ref):
+def flow_kernel(block_ref, base_ref, mask_ref, raw_ref, wet_ref):
     lane = lax.broadcasted_iota(jnp.int32, (8, LANES), 1)
+    wet_ref[...] = mask_ref[...].astype(f32)
     s = block_ref[0]
     for high in range(2):
         for f in range(3):
@@ -67,9 +68,9 @@
     raw_ref[56:64, :] = halo_columns(column(lax.rem(s + 7, 8)), column(lax.rem(s + 1, 8)), lane)
 
 
-def pack_kernel(tan_ref, mask_ref, send_ref):
+def pack_kernel(tan_ref, wet_ref, send_ref):
     lane = lax.broadcasted_iota(jnp.int32, (8, LANES), 1)
-    wet = [mask_ref[:, k * LANES : (k + 1) * LANES].astype(f32) for k in range(8)]
+    wet = [wet_ref[:, k * LANES : (k + 1) * LANES] for k in range(8)]
 
     def send(core, _):
         cells = [
@@ -294,11 +295,11 @@
 def on_device(tangents, checkpoints, owner_order, land_mask, coefficients):
     block = lax.axis_index("y") * 2 + lax.axis_index("zh")
     core = lax.axis_index("c")
-    raw = pl.pallas_call(
+    raw, mask = pl.pallas_call(
         flow_kernel,
-        out_shape=jax.ShapeDtypeStruct((64, LANES), f32),
+        out_shape=(jax.ShapeDtypeStruct((64, LANES), f32), jax.ShapeDtypeStruct(land_mask.shape, f32)),
         in_specs=[SMEM, VMEM, VMEM],
-        out_specs=VMEM,
+        out_specs=(VMEM, VMEM),
         compiler_params=pltpu.CompilerParams(vmem_limit_bytes=16 * 2**20),
     )(block.reshape(1).astype(jnp.int32), checkpoints, land_mask)
     up = [(i, i + 1) for i in range(7)]
@@ -313,7 +314,7 @@
         in_specs=[VMEM, VMEM],
         out_specs=VMEM,
         compiler_params=pltpu.CompilerParams(vmem_limit_bytes=16 * 2**20),
-    )(tangents, land_mask)
+    )(tangents, mask)
     send, above, below = lax.optimization_barrier((send, above, below))
     own = lax.all_to_all(send, ("zh", "y", "c"), 0, 0, tiled=True)
     chips = jnp.concatenate([above, wide, below], axis=0)

time: 128 us -> 127 us (level)
    unnamed x18 -> x16, local copies, waits for them, and re-layouts: 4.11 us -> 3.35 us
where the time goes in v13:
time: 127 us; the launch traced here: 126 us
  starting transfers between devices  71.5 us (56%)
  Pallas kernels  26.4 us (21%)
  blocking collectives  12.8 us (10%)
  waiting for transfers between devices  12.1 us (10%)
  local copies, waits for them, and re-layouts  3.38 us (3%)
    ppermute x2, starting transfers between devices, on_device(): parts = [lax.ppermute(own, 'zl', up), own, lax.ppermute(own, 'zl', down)]  20.1 us
    ppermute x1, starting transfers between devices, on_device(): halo = lax.ppermute(raw[:48], ('y', 'zh', 'x'), ring)  18.7 us
    all_to_all x1, starting transfers between devices, on_device(): own = lax.all_to_all(send, ('zh', 'y', 'c'), 0, 0, tiled=True)  17.3 us
    pallas_call x1, Pallas kernels, on_device(): pl.pallas_call(march_kernel, out_shape=jax.ShapeDtypeStruct((8, 96, LANES...  13.5 us
    all_to_all x1, blocking collectives, on_device(): cells = lax.all_to_all(out, ('x', 'c'), 0, 0, tiled=True)  12.8 us
    pallas_call x1, Pallas kernels, on_device(): pl.pallas_call(coef_kernel, out_shape=jax.ShapeDtypeStruct((STEPS, COEFS,...  8.8 us
    ppermute x3, starting transfers between devices, on_device(): lax.ppermute(chips, 'x', [(i, (i + k) % 4) for i in range(4)])  8.44 us
    ppermute x3, waiting for transfers between devices, on_device(): lax.ppermute(chips, 'x', [(i, (i + k) % 4) for i in range(4)])  6.4 us
  transfers between devices with their start and end apart: 10, of which 5 were waited for; matrix products, arithmetic and copies ran while one was open for 0% of the time, Pallas kernels for 9%

profile of v13, /device:TPU:1, one launch (start us, length us, event | category | flops | bytes accessed | tf_op | source)
XLA Modules:
  0.0 126.5 jit_solution(12001679567566570693)
XLA Ops:
  0.0 0.0 copy-start.1
  0.0 0.9 copy-done.1
  0.9 0.0 copy-start.3
  0.9 0.8 copy-done.3
  1.7 0.1 shard_map.55
  1.7 18.7 %collective-permute-start = (f32[48,128]{1,0:T(8,128)S(1)}, f32[48,128]{1,0:T(8,128)S(1)}, u32[]{:S(2)}, u32[]{:S(2)}) collective-permute-start(f32[48,128]{1,0:T(8,128)S(1)} %slice.3), channel_id=1, source_target_pairs={{48,112},{0,448},{112,176},{64,0},{176,240},{128,64},{240,304},{19... | collective-permute-start | bytes 73736 | tf_op jit(solution)/shard_map/ppermute | solution.py:308
  20.5 0.9 collective-permute-done
  21.4 2.6 %collective-permute-start.1 = (f32[112,128]{1,0:T(8,128)S(1)}, f32[112,128]{1,0:T(8,128)S(1)}, u32[]{:S(2)}, u32[]{:S(2)}) collective-permute-start(f32[112,128]{1,0:T(8,128)S(1)} %constant_dynamic-update-slice_fusion), channel_id=1, source_target_pairs={{0,2},{2,4},{4,6},{6,8},{8,10},{10,12},{12,14},{1,3},{3,5},{5,7},{... | collective-permute-start | bytes 172040 | tf_op jit(solution)/shard_map/ppermute | solution.py:310
  24.0 1.3 %collective-permute-start.2 = (f32[112,128]{1,0:T(8,128)S(1)}, f32[112,128]{1,0:T(8,128)S(1)}, u32[]{:S(2)}, u32[]{:S(2)}) collective-permute-start(f32[112,128]{1,0:T(8,128)S(1)} %constant_dynamic-update-slice_fusion), channel_id=1, source_target_pairs={{2,0},{4,2},{6,4},{8,6},{10,8},{12,10},{14,12},{3,1},{5,3},{7,5},{... | collective-permute-start | bytes 172040 | tf_op jit(solution)/shard_map/ppermute | solution.py:310
  25.3 0.0 copy-start
  25.4 1.0 copy-done
  26.3 2.7 %shard_map.56 = f32[16,64,128]{2,1,0:T(8,128)} custom-call(f32[4,3,8,1024]{3,2,1,0:T(8,128)S(1)} %copy-done, f32[8,1024]{1,0:T(8,128)S(1)} %get-tuple-element.13.wet_ref), custom_call_target="tpu_custom_call" | custom-call | tf_op jit(solution)/shard_map/pallas_call | solution.py:311
  29.1 0.0 collective-permute-done.1
  29.1 0.0 collective-permute-done.2
  29.1 17.3 %all-to-all-start = ((f32[16,64,128]{2,1,0:T(8,128)}), f32[16,64,128]{2,1,0:T(8,128)S(1)}, u32[]{:S(2)}, u32[]{:S(2)}) async-start(f32[16,64,128]{2,1,0:T(8,128)} %shard_map.56), calls=%async_computation | async-start | bytes 1048576 | tf_op jit(solution)/shard_map/all_to_all | solution.py:319
  46.4 1.9 %collective-permute-start.3 = (f32[336,128]{1,0:T(8,128)S(1)}, f32[336,128]{1,0:T(8,128)S(1)}, u32[]{:S(2)}, u32[]{:S(2)}) collective-permute-start(f32[336,128]{1,0:T(8,128)S(1)} %get-tuple-element.21), channel_id=1, source_target_pairs={{0,16},{16,32},{32,48},{48,0},{1,17},{17,33},{33,49},{49,1},{2,18}... | collective-permute-start | bytes 516104 | tf_op jit(solution)/shard_map/ppermute | solution.py:322
  48.4 3.7 %collective-permute-start.4 = (f32[336,128]{1,0:T(8,128)S(1)}, f32[336,128]{1,0:T(8,128)S(1)}, u32[]{:S(2)}, u32[]{:S(2)}) collective-permute-start(f32[336,128]{1,0:T(8,128)S(1)} %get-tuple-element.21), channel_id=1, source_target_pairs={{0,32},{16,48},{32,0},{48,16},{1,33},{17,49},{33,1},{49,17},{2,34}... | collective-permute-start | bytes 516104 | tf_op jit(solution)/shard_map/ppermute | solution.py:322
  52.1 2.8 %collective-permute-start.5 = (f32[336,128]{1,0:T(8,128)S(1)}, f32[336,128]{1,0:T(8,128)S(1)}, u32[]{:S(2)}, u32[]{:S(2)}) collective-permute-start(f32[336,128]{1,0:T(8,128)S(1)} %get-tuple-element.21), channel_id=1, source_target_pairs={{0,48},{16,0},{32,16},{48,32},{1,49},{17,1},{33,17},{49,33},{2,50}... | collective-permute-start | bytes 516104 | tf_op jit(solution)/shard_map/ppermute | solution.py:322
  54.9 4.3 %collective-permute-done.3 = f32[336,128]{1,0:T(8,128)S(1)} collective-permute-done((f32[336,128]{1,0:T(8,128)S(1)}, f32[336,128]{1,0:T(8,128)S(1)}, u32[]{:S(2)}, u32[]{:S(2)}) %collective-permute-start.3) | collective-permute-done | bytes 172064 | tf_op jit(solution)/shard_map/ppermute | solution.py:322
  59.2 0.0 collective-permute-done.4
  59.2 2.1 %collective-permute-done.5 = f32[336,128]{1,0:T(8,128)S(1)} collective-permute-done((f32[336,128]{1,0:T(8,128)S(1)}, f32[336,128]{1,0:T(8,128)S(1)}, u32[]{:S(2)}, u32[]{:S(2)}) %collective-permute-start.5) | collective-permute-done | bytes 172064 | tf_op jit(solution)/shard_map/ppermute | solution.py:322
  61.4 3.1 %collective-permute-start.6 = (f32[1344,128]{1,0:T(8,128)S(1)}, f32[1344,128]{1,0:T(8,128)S(1)}, u32[]{:S(2)}, u32[]{:S(2)}) collective-permute-start(f32[1344,128]{1,0:T(8,128)S(1)} %constant_dynamic-update-slice_fusion.6.strip_ref), channel_id=1, source_target_pairs={{0,1},{1,0},{2,3},{3,2},{4,5},{5,4},{6,7},{7,6},{8,9},{9,8},{10,11... | collective-permute-start | bytes 2064392 | tf_op jit(solution)/shard_map/ppermute | solution.py:324
  64.5 1.7 %collective-permute-done.6.other_ref = f32[1344,128]{1,0:T(8,128)S(1)} collective-permute-done((f32[1344,128]{1,0:T(8,128)S(1)}, f32[1344,128]{1,0:T(8,128)S(1)}, u32[]{:S(2)}, u32[]{:S(2)}) %collective-permute-start.6) | collective-permute-done | bytes 688160 | tf_op jit(solution)/shard_map/ppermute | solution.py:324
  66.2 0.0 all-to-all-done
  66.2 18.8 %collective-permute-start.7 = (f32[16,64,128]{2,1,0:T(8,128)S(1)}, f32[16,64,128]{2,1,0:T(8,128)S(1)}, u32[]{:S(2)}, u32[]{:S(2)}) collective-permute-start(f32[16,64,128]{2,1,0:T(8,128)S(1)} %all-to-all-done), channel_id=1, source_target_pairs={{0,2},{2,4},{4,6},{6,8},{8,10},{10,12},{12,14},{1,3},{3,5},{5,7},{... | collective-permute-start | bytes 1572872 | tf_op jit(solution)/shard_map/ppermute | solution.py:339
  85.0 1.3 %collective-permute-start.8 = (f32[16,64,128]{2,1,0:T(8,128)S(1)}, f32[16,64,128]{2,1,0:T(8,128)S(1)}, u32[]{:S(2)}, u32[]{:S(2)}) collective-permute-start(f32[16,64,128]{2,1,0:T(8,128)S(1)} %all-to-all-done), channel_id=1, source_target_pairs={{2,0},{4,2},{6,4},{8,6},{10,8},{12,10},{14,12},{3,1},{5,3},{7,5},{... | collective-permute-start | bytes 1572872 | tf_op jit(solution)/shard_map/ppermute | solution.py:339
  86.3 0.1 pad_add_fusion.core_ref
  86.4 0.0 copy-start.4
  86.4 0.7 copy-done.4
  87.0 0.0 copy-start.2
  87.0 8.8 %shard_map.57.coef = f32[8,15,5,56,128]{4,3,2,1,0:T(8,128)S(1)} custom-call(s32[2]{0:T(128)S(1)} %pad_add_fusion.core_ref, s32[8]{0:T(128)S(1)} %copy-done.4, f32[1344,128]{1,0:T(8,128)S(1)} %constant_dynamic-update-slice_fusion.6.strip_ref, f32[1344,128]{1,0:T(8,128)S(1)} %collective-permute-done.6.other_ref), custom_call_target="tpu_custom_call" | custom-call | flops 2000000000 | bytes 50000000 | tf_op jit(solution)/shard_map/pallas_call | solution.py:326
  95.9 0.0 collective-permute-done.7
  95.9 3.0 %collective-permute-done.8 = f32[16,64,128]{2,1,0:T(8,128)S(1)} collective-permute-done((f32[16,64,128]{2,1,0:T(8,128)S(1)}, f32[16,64,128]{2,1,0:T(8,128)S(1)}, u32[]{:S(2)}, u32[]{:S(2)}) %collective-permute-start.8) | collective-permute-done | bytes 524320 | tf_op jit(solution)/shard_map/ppermute | solution.py:339
  98.9 13.5 %shard_map.58 = f32[8,96,128]{2,1,0:T(8,128)S(1)} custom-call(f32[1024,128]{1,0:T(8,128)S(1)} %bitcast.12, f32[1024,128]{1,0:T(8,128)S(1)} %bitcast.10, f32[1024,128]{1,0:T(8,128)S(1)} %bitcast.13, f32[8,15,5,56,128]{4,3,2,1,0:T(8,128)S(1)} %shard_map.57.coef), custom_call_target="tpu_custom_call" | custom-call | tf_op jit(solution)/shard_map/pallas_call | solution.py:341
  112.4 12.8 %all_to_all.10 = f32[8,96,128]{2,1,0:T(8,128)S(1)} all-to-all(f32[8,96,128]{2,1,0:T(8,128)S(1)} %shard_map.58), channel_id=1, replica_groups=mesh['y'=4,'zh'=2,'x'=4,'zl'=8,'c'=2] {'x','c'}, dimensions={0} | all-to-all | bytes 786432 | tf_op jit(solution)/shard_map/all_to_all | solution.py:353
  125.2 0.0 copy-done.2
  125.2 1.3 %shard_map.59 = f32[768,128]{1,0:T(8,128)} custom-call(f32[128,128]{1,0:T(8,128)S(1)} %copy-done.2, f32[768,128]{1,0:T(8,128)S(1)} %bitcast.11), custom_call_target="tpu_custom_call" | custom-call | tf_op jit(solution)/shard_map/pallas_call | solution.py:354
  (10 shorter events, 0.1 us)
Async XLA Ops:
  0.0 0.9 copy-start.1
  0.9 0.8 copy-start.3
  1.7 19.7 %collective-permute-start = (f32[48,128]{1,0:T(8,128)S(1)}, f32[48,128]{1,0:T(8,128)S(1)}, u32[]{:S(2)}, u32[]{:S(2)}) collective-permute-start(f32[48,128]{1,0:T(8,128)S(1)} %slice.3), channel_id=1, source_target_pairs={{48,112},{0,448},{112,176},{64,0},{176,240},{128,64},{240,304},{19... | collective-permute-start | bytes 73736 | tf_op jit(solution)/shard_map/ppermute | solution.py:308
  21.4 7.7 %collective-permute-start.1 = (f32[112,128]{1,0:T(8,128)S(1)}, f32[112,128]{1,0:T(8,128)S(1)}, u32[]{:S(2)}, u32[]{:S(2)}) collective-permute-start(f32[112,128]{1,0:T(8,128)S(1)} %constant_dynamic-update-slice_fusion), channel_id=1, source_target_pairs={{0,2},{2,4},{4,6},{6,8},{8,10},{10,12},{12,14},{1,3},{3,5},{5,7},{... | collective-permute-start | bytes 172040 | tf_op jit(solution)/shard_map/ppermute | solution.py:310
  24.0 5.0 %collective-permute-start.2 = (f32[112,128]{1,0:T(8,128)S(1)}, f32[112,128]{1,0:T(8,128)S(1)}, u32[]{:S(2)}, u32[]{:S(2)}) collective-permute-start(f32[112,128]{1,0:T(8,128)S(1)} %constant_dynamic-update-slice_fusion), channel_id=1, source_target_pairs={{2,0},{4,2},{6,4},{8,6},{10,8},{12,10},{14,12},{3,1},{5,3},{7,5},{... | collective-permute-start | bytes 172040 | tf_op jit(solution)/shard_map/ppermute | solution.py:310
  25.3 1.0 copy-start
  29.1 37.1 %all-to-all-start = ((f32[16,64,128]{2,1,0:T(8,128)}), f32[16,64,128]{2,1,0:T(8,128)S(1)}, u32[]{:S(2)}, u32[]{:S(2)}) async-start(f32[16,64,128]{2,1,0:T(8,128)} %shard_map.56), calls=%async_computation | async-start | bytes 1048576 | tf_op jit(solution)/shard_map/all_to_all | solution.py:319
  46.4 12.7 %collective-permute-start.3 = (f32[336,128]{1,0:T(8,128)S(1)}, f32[336,128]{1,0:T(8,128)S(1)}, u32[]{:S(2)}, u32[]{:S(2)}) collective-permute-start(f32[336,128]{1,0:T(8,128)S(1)} %get-tuple-element.21), channel_id=1, source_target_pairs={{0,16},{16,32},{32,48},{48,0},{1,17},{17,33},{33,49},{49,1},{2,18}... | collective-permute-start | bytes 516104 | tf_op jit(solution)/shard_map/ppermute | solution.py:322
  48.4 10.8 %collective-permute-start.4 = (f32[336,128]{1,0:T(8,128)S(1)}, f32[336,128]{1,0:T(8,128)S(1)}, u32[]{:S(2)}, u32[]{:S(2)}) collective-permute-start(f32[336,128]{1,0:T(8,128)S(1)} %get-tuple-element.21), channel_id=1, source_target_pairs={{0,32},{16,48},{32,0},{48,16},{1,33},{17,49},{33,1},{49,17},{2,34}... | collective-permute-start | bytes 516104 | tf_op jit(solution)/shard_map/ppermute | solution.py:322
  52.1 9.3 %collective-permute-start.5 = (f32[336,128]{1,0:T(8,128)S(1)}, f32[336,128]{1,0:T(8,128)S(1)}, u32[]{:S(2)}, u32[]{:S(2)}) collective-permute-start(f32[336,128]{1,0:T(8,128)S(1)} %get-tuple-element.21), channel_id=1, source_target_pairs={{0,48},{16,0},{32,16},{48,32},{1,49},{17,1},{33,17},{49,33},{2,50}... | collective-permute-start | bytes 516104 | tf_op jit(solution)/shard_map/ppermute | solution.py:322
  61.4 4.9 %collective-permute-start.6 = (f32[1344,128]{1,0:T(8,128)S(1)}, f32[1344,128]{1,0:T(8,128)S(1)}, u32[]{:S(2)}, u32[]{:S(2)}) collective-permute-start(f32[1344,128]{1,0:T(8,128)S(1)} %constant_dynamic-update-slice_fusion.6.strip_ref), channel_id=1, source_target_pairs={{0,1},{1,0},{2,3},{3,2},{4,5},{5,4},{6,7},{7,6},{8,9},{9,8},{10,11... | collective-permute-start | bytes 2064392 | tf_op jit(solution)/shard_map/ppermute | solution.py:324
  66.2 29.6 %collective-permute-start.7 = (f32[16,64,128]{2,1,0:T(8,128)S(1)}, f32[16,64,128]{2,1,0:T(8,128)S(1)}, u32[]{:S(2)}, u32[]{:S(2)}) collective-permute-start(f32[16,64,128]{2,1,0:T(8,128)S(1)} %all-to-all-done), channel_id=1, source_target_pairs={{0,2},{2,4},{4,6},{6,8},{8,10},{10,12},{12,14},{1,3},{3,5},{5,7},{... | collective-permute-start | bytes 1572872 | tf_op jit(solution)/shard_map/ppermute | solution.py:339
  85.0 13.9 %collective-permute-start.8 = (f32[16,64,128]{2,1,0:T(8,128)S(1)}, f32[16,64,128]{2,1,0:T(8,128)S(1)}, u32[]{:S(2)}, u32[]{:S(2)}) collective-permute-start(f32[16,64,128]{2,1,0:T(8,128)S(1)} %all-to-all-done), channel_id=1, source_target_pairs={{2,0},{4,2},{6,4},{8,6},{10,8},{12,10},{14,12},{3,1},{5,3},{7,5},{... | collective-permute-start | bytes 1572872 | tf_op jit(solution)/shard_map/ppermute | solution.py:339
  86.4 0.7 copy-start.4
  87.0 38.2 %copy-start.2 = (f32[128,128]{1,0:T(8,128)S(1)}, f32[128,128]{1,0:T(8,128)}, u32[]{:S(2)}) copy-start(f32[128,128]{1,0:T(8,128)} %coef_ref.1) | copy-start | bytes 196612
